TPU v7x, 32 devices: a whole 2x2x4 slice. The times are simulated.
32 devices in a mesh: seq: 4 (over y, x), group: 8 (over z, core).
Axes of the slice: x: 2, y: 2, z: 4, core: 2. Of those that a mesh axis runs over, the one named last changes fastest.
Arguments:
- block_input: bfloat16 [4, 2048, 2048], P('seq', 'group'), may hold values from -6 to 6
- out_cotangent: bfloat16 [4, 2048, 2048], P('seq', 'group'), may hold values from -6 to 6
- norm_gain: float32 [2048], replicated, may hold values from 0.1 to 1.9
- in_weight: bfloat16 [2048, 5120], P('group'), may hold values from -0.125 to 0.125
- conv_weight: float32 [4, 2560], replicated, may hold values from -3 to 3
- conv_bias: float32 [2560], replicated, may hold values from -3 to 3
- gate_weight: bfloat16 [2, 10, 256, 256], replicated, may hold values from -0.375 to 0.375
- gate_bias: float32 [2, 2560], replicated, may hold values from -3 to 3
- decay_param: float32 [2560], replicated, as said below
- out_weight: bfloat16 [2560, 2048], P('group'), may hold values from -0.125 to 0.125
- mlp_gain: float32 [2048], replicated, may hold values from 0.1 to 1.9
- mlp_weight: bfloat16 [2048, 12288], P('group'), may hold values from -0.125 to 0.125
- down_weight: bfloat16 [6144, 2048], P('group'), may hold values from -0.078125 to 0.078125
Outputs:
- block_out: bfloat16 [4, 2048, 2048], P('seq', 'group')
- input_grad: float32 [4, 2048, 2048], P('seq', 'group')
- norm_gain_grad: float32 [2048], replicated
- in_weight_grad: float32 [2048, 5120], P('group')
- conv_weight_grad: float32 [4, 2560], replicated
- conv_bias_grad: float32 [2560], replicated
- gate_weight_grad: float32 [2, 10, 256, 256], replicated
- gate_bias_grad: float32 [2, 2560], replicated
- decay_grad: float32 [2560], replicated
- out_weight_grad: float32 [2560, 2048], P('group')
- mlp_gain_grad: float32 [2048], replicated
- mlp_weight_grad: float32 [2048, 12288], P('group')
- down_weight_grad: float32 [6144, 2048], P('group')
Inputs may be any that keep to these rules, and one draw needn't show every extreme that they name: `decay_param`: softplus of every entry lies between 0.01 / 2048 and 0.03.
All inputs are finite; a program needn't handle non-finite values.
Results may differ from a plain program's by a relative error of at most 0.013.
Values may be sent and summed in bfloat16 or wider, within the bound.
No kernel may reach another device: no remote copies, remote signals or barrier semaphores. Data moves between devices by JAX's collectives and lax.ppermute only.
A program may use at most 576 MiB of HBM per device.

v0:
```python
import jax
import jax.numpy as jnp
from jax import lax
from jax.sharding import PartitionSpec as P

epsilon = 1e-06


def entering(value, axis, join, neutral, backward):
    count, mine = (lax.axis_size(axis), lax.axis_index(axis))
    pieces = jax.tree.map(lambda part: lax.all_gather(part, axis), value)
    if backward:
        pieces = jax.tree.map(lambda part: part[::-1], pieces)
        mine = count - 1 - mine
    running = jax.tree.map(
        lambda part, zero: jnp.full_like(part, 0) + jnp.asarray(zero, part.dtype), value, neutral
    )

    def step(position, running):
        longer = join(running, jax.tree.map(lambda part: part[position], pieces))
        return jax.tree.map(lambda new, old: jnp.where(position < mine, new, old), longer, running)

    return lax.fori_loop(0, count - 1, step, running)


def from_behind(block, axis, distance):
    devices = range(lax.axis_size(axis))
    route = [(i - distance, i) for i in devices if i - distance in devices]
    return lax.ppermute(block, axis, route)


def rms_piece(value, gain):
    return value * lax.rsqrt(jnp.mean(value * value, axis=-1, keepdims=True) + epsilon) * gain


def gate_piece(conv_out, gate_pre, gate_bias, decay_param):
    recur_gate = jax.nn.sigmoid(gate_pre[0] + gate_bias[0])
    input_gate = jax.nn.sigmoid(gate_pre[1] + gate_bias[1])
    log_decay = -8.0 * recur_gate * jax.nn.softplus(decay_param)
    decay = jnp.exp(log_decay)
    return (decay, conv_out * input_gate * jnp.sqrt(-jnp.expm1(2.0 * log_decay)))


def link(earlier, later):
    return (earlier[0] * later[0], later[1] + later[0] * earlier[1])


def contract(active, weight):
    full_weight = lax.all_gather(weight, "group", axis=0, tiled=True)
    return jnp.dot(active, full_weight, preferred_element_type=jnp.float32)


def pull_back(grad_low, weight):
    full_weight = lax.all_gather(weight, "group", axis=0, tiled=True)
    return lax.dot_general(
        grad_low, full_weight, (((1,), (1,)), ((), ())), preferred_element_type=jnp.float32
    )


def weight_grad(active_low, grad_low):
    return lax.psum_scatter(
        lax.dot_general(
            active_low, grad_low, (((0,), (0,)), ((), ())), preferred_element_type=jnp.float32
        ),
        "group",
        scatter_dimension=0,
        tiled=True,
    )


def carry_forward(decay_last, state_last):
    return entering(
        (decay_last, state_last),
        "group",
        link,
        (jnp.ones_like(decay_last), jnp.zeros_like(state_last)),
        False,
    )


def carry_backward(decay_first, adjoint_first):
    return entering(
        (decay_first, adjoint_first),
        "group",
        link,
        (jnp.ones_like(decay_first), jnp.zeros_like(adjoint_first)),
        True,
    )


def shards(
    block_input,
    out_cotangent,
    norm_gain,
    in_weight,
    conv_weight,
    conv_bias,
    gate_weight,
    gate_bias,
    decay_param,
    out_weight,
    mlp_gain,
    mlp_weight,
    down_weight,
):
    seq_count, tok_count, model_width = block_input.shape
    row_count = seq_count * tok_count
    conv_span, rec_width = conv_weight.shape
    head_count = gate_weight.shape[1]
    hidden_width = mlp_weight.shape[1] // 2
    lead = conv_span - 1
    inputs = block_input.reshape(row_count, model_width).astype(jnp.float32)
    normed_low = rms_piece(inputs, norm_gain).astype(jnp.bfloat16)
    projected = contract(normed_low, in_weight)
    branch_x = projected[:, :rec_width].reshape(seq_count, tok_count, rec_width)
    branch_pre = projected[:, rec_width:]
    rim = from_behind(branch_x[:, tok_count - lead :], "group", 1)
    padded = jnp.concatenate([rim, branch_x], 1)
    conv_out = conv_bias + conv_weight[0] * padded[:, lead : lead + tok_count]
    for offset in range(1, conv_span):
        conv_out = (
            conv_out + conv_weight[offset] * padded[:, lead - offset : lead - offset + tok_count]
        )
    conv_flat = conv_out.reshape(row_count, rec_width)
    conv_low = conv_flat.astype(jnp.bfloat16).reshape(
        row_count, head_count, rec_width // head_count
    )
    gate_pre = jnp.einsum(
        "thk,ghkj->gthj", conv_low, gate_weight, preferred_element_type=jnp.float32
    ).reshape(2, row_count, rec_width)
    decay, driven = gate_piece(conv_flat, gate_pre, gate_bias, decay_param)
    decay_seq = decay.reshape(seq_count, tok_count, rec_width)
    driven_seq = driven.reshape(seq_count, tok_count, rec_width)
    decay_cum, state_local = lax.associative_scan(link, (decay_seq, driven_seq), axis=1)
    _, carried = carry_forward(decay_cum[:, -1], state_local[:, -1])
    states = state_local + decay_cum * carried[:, None]
    states_flat = states.reshape(row_count, rec_width)
    gelu_y = jax.nn.gelu(branch_pre)
    merged_low = (states_flat * gelu_y).astype(jnp.bfloat16)
    resid = inputs + contract(merged_low, out_weight)
    normed2_low = rms_piece(resid, mlp_gain).astype(jnp.bfloat16)
    gate_up = contract(normed2_low, mlp_weight)

    def mlp_act(values):
        return jax.nn.gelu(values[:, :hidden_width]) * values[:, hidden_width:]

    hidden_low = mlp_act(gate_up).astype(jnp.bfloat16)
    final = resid + contract(hidden_low, down_weight)
    block_out = final.astype(jnp.bfloat16).reshape(seq_count, tok_count, model_width)
    grad_out = out_cotangent.reshape(row_count, model_width).astype(jnp.float32)
    grad_out_low = grad_out.astype(jnp.bfloat16)
    grad_hidden = pull_back(grad_out_low, down_weight)
    down_grad = weight_grad(hidden_low, grad_out_low)
    _, act_pull = jax.vjp(mlp_act, gate_up)
    grad_gu_low = act_pull(grad_hidden)[0].astype(jnp.bfloat16)
    grad_normed2 = pull_back(grad_gu_low, mlp_weight)
    mlp_grad = weight_grad(normed2_low, grad_gu_low)
    _, second_pull = jax.vjp(rms_piece, resid, mlp_gain)
    grad_resid_norm, mlp_gain_grad = second_pull(grad_normed2)
    grad_resid = grad_out + grad_resid_norm
    grad_resid_low = grad_resid.astype(jnp.bfloat16)
    grad_merged = pull_back(grad_resid_low, out_weight)
    out_grad = weight_grad(merged_low, grad_resid_low)
    grad_states = (grad_merged * gelu_y).reshape(seq_count, tok_count, rec_width)
    _, gelu_pull = jax.vjp(jax.nn.gelu, branch_pre)
    grad_pre = gelu_pull(grad_merged * states_flat)[0]
    coeff = jnp.concatenate([decay_seq[:, 1:], jnp.ones_like(decay_seq[:, :1])], 1)
    coeff_cum, adjoint_local = lax.associative_scan(
        link, (coeff, grad_states), reverse=True, axis=1
    )
    first_decay = decay_seq[:, 0]
    _, incoming = carry_backward(first_decay * coeff_cum[:, 0], first_decay * adjoint_local[:, 0])
    adjoint = adjoint_local + coeff_cum * incoming[:, None]
    prev_states = jnp.concatenate([carried[:, None], states[:, :-1]], 1)
    grad_decay = (adjoint * prev_states).reshape(row_count, rec_width)
    grad_driven = adjoint.reshape(row_count, rec_width)
    _, gate_pull = jax.vjp(gate_piece, conv_flat, gate_pre, gate_bias, decay_param)
    grad_conv_direct, grad_gate_pre, gate_bias_grad, decay_grad = gate_pull(
        (grad_decay, grad_driven)
    )
    grad_gate_low = grad_gate_pre.astype(jnp.bfloat16).reshape(
        2, row_count, head_count, rec_width // head_count
    )
    grad_conv_gates = jnp.einsum(
        "gthj,ghkj->thk", grad_gate_low, gate_weight, preferred_element_type=jnp.float32
    )
    grad_conv = grad_conv_direct + grad_conv_gates.reshape(row_count, rec_width)
    gate_weight_grad = jnp.einsum(
        "thk,gthj->ghkj", conv_low, grad_gate_low, preferred_element_type=jnp.float32
    )
    grad_conv_seq = grad_conv.reshape(seq_count, tok_count, rec_width)
    conv_weight_grad = jnp.stack(
        [
            jnp.sum(
                padded[:, lead - offset : lead - offset + tok_count] * grad_conv_seq, axis=(0, 1)
            )
            for offset in range(conv_span)
        ],
        0,
    )
    conv_bias_grad = jnp.sum(grad_conv_seq, axis=(0, 1))
    grad_padded = conv_weight[0] * jnp.pad(grad_conv_seq, ((0, 0), (lead, 0), (0, 0)))
    for offset in range(1, conv_span):
        grad_padded = grad_padded + conv_weight[offset] * jnp.pad(
            grad_conv_seq, ((0, 0), (lead - offset, offset), (0, 0))
        )
    back_rim = from_behind(grad_padded[:, :lead], "group", -1)
    grad_branch_x = grad_padded[:, lead:] + jnp.pad(
        back_rim, ((0, 0), (tok_count - lead, 0), (0, 0))
    )
    grad_proj_low = jnp.concatenate(
        [grad_branch_x.reshape(row_count, rec_width), grad_pre], 1
    ).astype(jnp.bfloat16)
    grad_normed = pull_back(grad_proj_low, in_weight)
    in_grad = weight_grad(normed_low, grad_proj_low)
    _, first_pull = jax.vjp(rms_piece, inputs, norm_gain)
    grad_input_norm, norm_gain_grad = first_pull(grad_normed)
    input_grad = (grad_resid + grad_input_norm).reshape(seq_count, tok_count, model_width)
    in_grad, out_grad, mlp_grad, down_grad = (
        lax.psum(in_grad.astype(jnp.bfloat16), "seq").astype(jnp.float32),
        lax.psum(out_grad.astype(jnp.bfloat16), "seq").astype(jnp.float32),
        lax.psum(mlp_grad.astype(jnp.bfloat16), "seq").astype(jnp.float32),
        lax.psum(down_grad.astype(jnp.bfloat16), "seq").astype(jnp.float32),
    )
    summed = lax.psum(
        (
            norm_gain_grad,
            conv_weight_grad,
            conv_bias_grad,
            gate_weight_grad,
            gate_bias_grad,
            decay_grad,
            mlp_gain_grad,
        ),
        ("seq", "group"),
    )
    return (
        block_out,
        input_grad,
        summed[0],
        in_grad,
        summed[1],
        summed[2],
        summed[3],
        summed[4],
        summed[5],
        out_grad,
        summed[6],
        mlp_grad,
        down_grad,
    )


def solution(mesh):
    in_specs = (
        P("seq", "group", None),
        P("seq", "group", None),
        P(),
        P("group", None),
        P(),
        P(),
        P(),
        P(),
        P(),
        P("group", None),
        P(),
        P("group", None),
        P("group", None),
    )
    out_specs = (
        P("seq", "group", None),
        P("seq", "group", None),
        P(),
        P("group", None),
        P(),
        P(),
        P(),
        P(),
        P(),
        P("group", None),
        P(),
        P("group", None),
        P("group", None),
    )
    return jax.shard_map(shards, mesh=mesh, in_specs=in_specs, out_specs=out_specs, check_vma=False)
```

profile of v0, /device:TPU:0, one launch (start us, length us, event | category | flops | bytes accessed | tf_op | source)
XLA Modules:
  0.0 3848.5 jit_solution(6371597326703259333)
XLA Ops:
  12.5 185.4 %all-gather.5.cloned.1.call-done = bf16[2048,5120]{1,0:T(8,128)(2,1)} async-done(((bf16[256,5120]{1,0:T(8,128)(2,1)}), bf16[2048,5120]{1,0:T(8,128)(2,1)}) %all-gather.5.cloned.1.call-update) | async-done | bytes 20971536 | tf_op jit(solution)/shard_map/all_gather | solution.py:49
  197.9 10.5 fusion.81
  454.6 9.3 pad.267
  466.4 9.2 pad.266
  476.5 44.8 %all_gather.31 = f32[8,1,2560]{2,1,0:T(1,128)S(1)} all-gather(f32[1,1,2560]{2,1,0:T(1,128)S(1)} %slice_add_fusion.4), channel_id=1, replica_groups=mesh['seq'=4,'group'=8] {'group'}, dimensions={0}, use_global_device_ids=true | all-gather | bytes 92160 | tf_op jit(solution)/shard_map/all_gather | solution.py:11
  522.2 33.6 all_gather.32
  573.6 152.5 %all-gather.9.cloned.1.call-done = bf16[2048,12288]{1,0:T(8,128)(2,1)} async-done(((bf16[256,12288]{1,0:T(8,128)(2,1)}), bf16[2048,12288]{1,0:T(8,128)(2,1)}) %all-gather.9.cloned.1.call-update) | async-done | bytes 50331664 | tf_op jit(solution)/shard_map/all_gather | solution.py:49
  726.1 27.8 fusion.106
  753.9 191.9 %all-gather.11.cloned.1.call-done = bf16[6144,2048]{1,0:T(8,128)(2,1)} async-done(((bf16[768,2048]{1,0:T(8,128)(2,1)}), bf16[6144,2048]{1,0:T(8,128)(2,1)}) %all-gather.11.cloned.1.call-update) | async-done | bytes 25165840 | tf_op jit(solution)/shard_map/all_gather | solution.py:49
  945.8 23.8 fusion.50
  969.5 26.6 multiply_reduce_fusion.5
  1029.9 10.8 slice.654
  1040.8 10.7 slice.662
  1051.5 10.7 slice.657
  1062.2 12.6 fusion.69
  1074.8 20.8 reverse.9
  1279.5 9.2 pad.285
  1293.1 20.8 rev.17
  1338.9 20.9 rev.18
  1360.9 14.0 all_gather.36
  1374.8 14.0 all_gather.37
  1429.6 16.6 fusion.60
  1447.4 21.9 fusion.65
  1470.8 38.3 fusion.70
  1518.6 332.4 %reduce-scatter.7.cloned.1.call-done = f32[256,5120]{1,0:T(8,128)} async-done(((f32[2048,5120]{1,0:T(8,128)}), f32[256,5120]{1,0:T(8,128)}) %reduce-scatter.7.cloned.1.call-update) | async-done | bytes 5242896 | tf_op jit(solution)/shard_map/reduce_scatter | solution.py:61
  1855.3 479.7 %reduce-scatter.11.cloned.1.call-done = f32[768,2048]{1,0:T(8,128)} async-done(((f32[6144,2048]{1,0:T(8,128)}), f32[768,2048]{1,0:T(8,128)}) %reduce-scatter.11.cloned.1.call-update) | async-done | bytes 6291472 | tf_op jit(solution)/shard_map/reduce_scatter | solution.py:61
  2339.9 950.9 %reduce-scatter.13.cloned.1.call-done = f32[256,12288]{1,0:T(8,128)} async-done(((f32[2048,12288]{1,0:T(8,128)}), f32[256,12288]{1,0:T(8,128)}) %reduce-scatter.13.cloned.1.call-update) | async-done | bytes 12582928
  3336.2 13.8 fusion.43
  3350.0 12.5 fusion.52
  3366.3 77.5 %all-reduce.84.cloned.1.call-done = f32[2,10,256,256]{2,3,0,1:T(8,128)} async-done(((f32[2,10,256,256]{2,3,0,1:T(8,128)}), f32[2,10,256,256]{2,3,0,1:T(8,128)}) %all-reduce.84.cloned.1.call-update) | async-done | bytes 5242896 | tf_op jit(solution)/shard_map/psum | solution.py:225
  3449.7 252.1 %all-reduce.88.cloned.1.call-done = (bf16[256,5120]{1,0:T(8,128)(2,1)}, bf16[320,2048]{1,0:T(8,128)(2,1)}, bf16[256,12288]{1,0:T(8,128)(2,1)}, bf16[768,2048]{1,0:T(8,128)(2,1)}) async-done(((bf16[256,5120]{1,0:T(8,128)(2,1)}, bf16[320,2048]{1,0:T(8,128)(2,1)}, bf16[256,12288]{1,0:T(8,128)(2,1)}, bf16[768,2048]{1,0:T(8,128)(2,1)}), (bf16[256,5120]{1,0:T(8,128)(2,1)}, bf16[320,2048]{1,0:T(8,128)(2,1)}, ...) | async-done | bytes 13369360 | tf_op jit(solution)/shard_map/psum | solution.py:220
  3718.3 115.4 %all-reduce.86.cloned.1.call-done = (f32[2048]{0:T(1024)}, f32[4,2560]{1,0:T(4,128)}, f32[2560]{0:T(1024)}, f32[2,2560]{1,0:T(2,128)}, f32[2560]{0:T(1024)}, /*index=5*/f32[2048]{0:T(1024)}) async-done(((f32[2048]{0:T(1024)}, f32[4,2560]{1,0:T(4,128)}, f32[2560]{0:T(1024)}, f32[2,2560]{1,0:T(2,128)}, f32[2560]{0:T(1024)}, /*index=5*/f32[2048]{0:T(1024)}), (f32[2048]{0:T(1024)}, f32[4,2560]{1,0:T(4,128)}, ...) | async-done | bytes 98320 | tf_op jit(solution)/shard_map/psum | solution.py:225
  (601 shorter events, 662.3 us)
Async XLA Ops:
  7.2 217.2 %copy-start = (bf16[2,10,256,256]{3,2,1,0:T(8,128)(2,1)S(1)}, bf16[2,10,256,256]{3,2,1,0:T(8,128)(2,1)}, u32[]{:S(2)}) copy-start(bf16[2,10,256,256]{3,2,1,0:T(8,128)(2,1)} %param.23) | copy-start | bytes 7864324
  7.2 190.7 %all-gather.5.cloned.1.call-start = ((), (), s32[]{:S(2)}) async-start(), calls=%async_computation.4 | async-start | bytes 23592960 | tf_op jit(solution)/shard_map/all_gather | solution.py:49
  7.9 556.8 %all-gather.7.cloned.1.call-start = ((), (), s32[]{:S(2)}) async-start(), calls=%async_computation.5 | async-start | bytes 11796480 | tf_op jit(solution)/shard_map/all_gather | solution.py:49
  8.7 717.5 %all-gather.9.cloned.1.call-start = ((), (), s32[]{:S(2)}) async-start(), calls=%async_computation.6 | async-start | bytes 56623104 | tf_op jit(solution)/shard_map/all_gather | solution.py:49
  9.4 188.5 %copy-start.69 = (f32[2048]{0:T(1024)S(1)}, f32[2048]{0:T(1024)}, u32[]{:S(2)}) copy-start(f32[2048]{0:T(1024)} %param.19) | copy-start | bytes 24580
  9.4 936.3 %all-gather.11.cloned.1.call-start = ((), (), s32[]{:S(2)}) async-start(), calls=%async_computation.7 | async-start | bytes 28311552 | tf_op jit(solution)/shard_map/all_gather | solution.py:49
  10.0 1505.5 %reduce-scatter.9.cloned.1.call-start = ((), (), s32[]{:S(2)}) async-start(), calls=%async_computation.10 | async-start | bytes 23592960 | tf_op jit(solution)/shard_map/reduce_scatter | solution.py:61
  10.3 205.0 %copy-start.78 = (f32[2560]{0:T(1024)}, f32[2560]{0:T(1024)S(1)}, u32[]{:S(2)}) copy-start(f32[2560]{0:T(1024)S(1)} %get-tuple-element.289) | copy-start | bytes 30724
  10.3 205.0 %copy-start.80 = (f32[2560]{0:T(1024)}, f32[2560]{0:T(1024)S(1)}, u32[]{:S(2)}) copy-start(f32[2560]{0:T(1024)S(1)} %get-tuple-element.290) | copy-start | bytes 30724
  10.3 205.0 %copy-start.82 = (f32[2560]{0:T(1024)}, f32[2560]{0:T(1024)S(1)}, u32[]{:S(2)}) copy-start(f32[2560]{0:T(1024)S(1)} %get-tuple-element.291) | copy-start | bytes 30724
  10.3 205.0 %copy-start.84 = (f32[2560]{0:T(1024)}, f32[2560]{0:T(1024)S(1)}, u32[]{:S(2)}) copy-start(f32[2560]{0:T(1024)S(1)} %get-tuple-element.292) | copy-start | bytes 30724
  11.9 196.6 %copy-start.113 = (f32[256]{0:T(256)}, f32[256]{0:T(256)S(1)}, u32[]{:S(2)}) copy-start(f32[256]{0:T(256)S(1)} %fusion.56) | copy-start | bytes 3076
  11.9 196.6 %copy-start.108 = (f32[256]{0:T(256)}, f32[256]{0:T(256)S(1)}, u32[]{:S(2)}) copy-start(f32[256]{0:T(256)S(1)} %fusion.100) | copy-start | bytes 3076
  12.5 224.7 %copy-start.51 = (f32[2560]{0:T(1024)}, f32[2560]{0:T(1024)S(1)}, u32[]{:S(2)}) copy-start(f32[2560]{0:T(1024)S(1)} %get-tuple-element.414) | copy-start | bytes 30724
  212.3 3.0 collective-permute-start
  214.7 22.4 copy-start.53
  214.8 22.4 copy-start.55
  564.8 161.4 %copy-start.47 = (f32[2048]{0:T(1024)S(1)}, f32[2048]{0:T(1024)}, u32[]{:S(2)}) copy-start(f32[2048]{0:T(1024)} %param.27) | copy-start | bytes 24580
  573.6 422.5 %copy-start.59 = (f32[256]{0:T(256)}, f32[256]{0:T(256)S(1)}, u32[]{:S(2)}) copy-start(f32[256]{0:T(256)S(1)} %fusion.101) | copy-start | bytes 3076
  1009.4 841.6 %reduce-scatter.7.cloned.1.call-start = ((), (), s32[]{:S(2)}) async-start(), calls=%async_computation.8 | async-start | bytes 47185920 | tf_op jit(solution)/shard_map/reduce_scatter | solution.py:61
  1179.3 18.6 copy-start.67
  1179.3 18.6 copy-start.68
  1338.9 50.3 %copy-start.52 = (f32[2560]{0:T(1024)S(1)}, f32[2560]{0:T(1024)}, u32[]{:S(2)}) copy-start(f32[2560]{0:T(1024)} %copy-done.51) | copy-start | bytes 30724
  1338.9 50.3 %copy-start.54 = (f32[2560]{0:T(1024)S(1)}, f32[2560]{0:T(1024)}, u32[]{:S(2)}) copy-start(f32[2560]{0:T(1024)} %copy-done.53) | copy-start | bytes 30724
  1338.9 50.3 %copy-start.56 = (f32[2560]{0:T(1024)S(1)}, f32[2560]{0:T(1024)}, u32[]{:S(2)}) copy-start(f32[2560]{0:T(1024)} %copy-done.55) | copy-start | bytes 30724
  1426.0 3.2 collective-permute-start.1
  1446.2 888.9 %reduce-scatter.11.cloned.1.call-start = ((), (), s32[]{:S(2)}) async-start(), calls=%async_computation.11 | async-start | bytes 56623104 | tf_op jit(solution)/shard_map/reduce_scatter | solution.py:61
  1469.2 1821.5 %reduce-scatter.13.cloned.1.call-start = ((), (), s32[]{:S(2)}) async-start(), calls=%async_computation.12 | async-start | bytes 113246208
  1509.1 1934.7 %all-reduce.84.cloned.1.call-start = ((), (), s32[]{:S(2)}) async-start(), calls=%async_computation.9 | async-start | bytes 10485760 | tf_op jit(solution)/shard_map/psum | solution.py:225
  1515.5 2186.3 %all-reduce.88.cloned.1.call-start = ((), (), s32[]{:S(2)}) async-start(), calls=%async_computation.14 | async-start | bytes 26738688 | tf_op jit(solution)/shard_map/psum | solution.py:220
  3298.9 534.8 %all-reduce.86.cloned.1.call-start = ((), (), s32[]{:S(2)}) async-start(), calls=%async_computation.13 | async-start | bytes 204800 | tf_op jit(solution)/shard_map/psum | solution.py:225
  3714.8 126.9 %copy-start.1 = (bf16[2,10,256,256]{3,2,1,0:T(8,128)(2,1)S(1)}, bf16[2,10,256,256]{3,2,1,0:T(8,128)(2,1)}, u32[]{:S(2)}) copy-start(bf16[2,10,256,256]{3,2,1,0:T(8,128)(2,1)} %param.23) | copy-start | bytes 7864324
  (98 other events, 723.5 us)
Sparse Core Ops, SparseCore 0:
  9.7 188.1 all-gather.4
  199.5 97.5 all-gather.6
  298.8 427.2 all-gather.8
  727.6 218.0 all-gather.10
  1009.5 205.8 reduce-scatter.8
  1446.3 404.6 reduce-scatter.6
  1853.5 481.4 reduce-scatter.10
  2337.4 953.3 reduce-scatter.12
  3297.9 145.8 all-reduce.83
  3448.8 252.8 all-reduce.87
  3710.5 123.1 all-reduce.85
where the time goes:
time: 3870 us; the launch traced here: 3850 us
  waiting for transfers between devices  2740 us (71%)
  local copies, waits for them, and re-layouts  526 us (14%)
  matrix products  233 us (6%)
  other arithmetic  220 us (6%)
  blocking collectives  106 us (3%)
    unnamed x12, waiting for transfers between devices  954 us
    reduce_scatter x3, waiting for transfers between devices, weight_grad(): lax.psum_scatter(lax.dot_general(active_low, grad_low, (((0,), (0,)), (()...  812 us
    all_gather x4, waiting for transfers between devices, contract(): full_weight = lax.all_gather(weight, 'group', axis=0, tiled=True)  530 us
    psum x1, waiting for transfers between devices, shards(): lax.psum(in_grad.astype(jnp.bfloat16), 'seq').astype(jnp.float32)  252 us
    psum x2, waiting for transfers between devices, shards(): lax.psum((norm_gain_grad, conv_weight_grad, conv_bias_grad, gate_weight_g...  193 us
    slice x54, local copies, waits for them, and re-layouts, shards(): lax.associative_scan(link, (coeff, grad_states), reverse=True, axis=1)  136 us
    all_gather x4, blocking collectives, entering(): pieces = jax.tree.map(lambda part: lax.all_gather(part, axis), value)  106 us
    slice x52, local copies, waits for them, and re-layouts, shards(): lax.associative_scan(link, (decay_seq, driven_seq), axis=1)  106 us
  transfers between devices with their start and end apart: 13, of which 11 were waited for; matrix products, arithmetic and copies ran while one was open for 23% of the time, Pallas kernels for 0%

commit v1 on v0

v1 whole, which is shorter than its diff:
```python
import functools

import jax
import jax.numpy as jnp
from jax import lax
from jax.experimental import pallas as pl
from jax.experimental.pallas import tpu as pltpu
from jax.sharding import PartitionSpec as P

epsilon = 1e-06
f32 = jnp.float32
bf16 = jnp.bfloat16
VMEM_LIMIT = 58 * 1024 * 1024


def swap(block, k):
    return lax.ppermute(block, "seq", [(i, i ^ k) for i in range(lax.axis_size("seq"))])


def shift(block, distance):
    devices = range(lax.axis_size("group"))
    return lax.ppermute(
        block, "group", [(i - distance, i) for i in devices if i - distance in devices]
    )


def gather_seq(block):
    half = block.shape[0] // 2
    first = swap(block, 1)
    second = swap(block, 2)
    third = jnp.concatenate([swap(first[:half], 2), swap(second[half:], 1)], 0)
    return [block, first, second, third]


def scatter_seq(parts):
    half = parts[0].shape[0] // 2
    own, first, second, third = parts
    top = swap(third[:half], 1)
    bottom = swap(third[half:], 2)
    first_top = swap(first[:half], 1)
    second_bottom = swap(second[half:], 2)
    second_top = swap((second[:half].astype(f32) + top.astype(f32)).astype(bf16), 2)
    first_bottom = swap((first[half:].astype(f32) + bottom.astype(f32)).astype(bf16), 1)
    return jnp.concatenate(
        [
            own[:half].astype(f32) + first_top.astype(f32) + second_top.astype(f32),
            own[half:].astype(f32) + first_bottom.astype(f32) + second_bottom.astype(f32),
        ],
        0,
    )


def gather_group(block):
    return lax.all_gather(block, "group", axis=0, tiled=True)


def scatter_group(block):
    return lax.psum_scatter(block, "group", scatter_dimension=0, tiled=True)


def total(value):
    for axis in ("group", "seq"):
        count = lax.axis_size(axis)
        step = 1
        while step < count:
            value = value + lax.ppermute(value, axis, [(i, i ^ step) for i in range(count)])
            step *= 2
    return value


def link(earlier, later):
    return (earlier[0] * later[0], later[1] + later[0] * earlier[1])


def entering(decay, state, sign):
    count = lax.axis_size("group")
    pair = jnp.stack([decay, state])
    pair = shift(pair, sign)
    step = 1
    while step < count:
        before = shift(pair, sign * step)
        pair = jnp.stack(link((before[0], before[1]), (pair[0], pair[1])))
        step *= 2
    return pair[1]


def rms_low(value, gain):
    scale = lax.rsqrt(jnp.mean(value * value, axis=-1, keepdims=True) + epsilon)
    return (value * scale * gain).astype(bf16)


def rms_back(value, gain, grad):
    width = value.shape[-1]
    scale = lax.rsqrt(jnp.mean(value * value, axis=-1, keepdims=True) + epsilon)
    scaled = grad * gain
    along = jnp.sum(scaled * value, axis=-1, keepdims=True) / width
    grad_value = scale * scaled - value * (scale * scale * scale * along)
    grad_gain = jnp.sum(grad * value * scale, axis=0)
    return grad_value, grad_gain


ROOT = 0.7978845608028654
CUBE = 0.044715


def gelu(v):
    return 0.5 * v * (1.0 + jnp.tanh(ROOT * (v + CUBE * v * v * v)))


def gelu_both(v):
    square = v * v
    t = jnp.tanh(ROOT * v * (1.0 + CUBE * square))
    half = 0.5 * (1.0 + t)
    slope = half + 0.5 * v * (1.0 - t * t) * (ROOT * (1.0 + 3.0 * CUBE * square))
    return v * half, slope


def one_less_square(double):
    series = jnp.full_like(double, 1.0 / 362880.0)
    for term in (40320.0, 5040.0, 720.0, 120.0, 24.0, 6.0, 2.0, 1.0):
        series = series * double + 1.0 / term
    return -double * series


def rows_of(shape):
    return lax.broadcasted_iota(jnp.int32, shape, 0)


def pick(odd, value, width):
    lanes = value.shape[-1]
    return jnp.where(odd, value[:, lanes - width :], value[:, lanes - 2 * width : lanes - width])


def forward_kernel(
    head, odd_ref, u_ref, rim_ref, cw_ref, cb_ref, gw_ref, gs_ref, gb_ref, sp_ref,
    conv_ref, recur_ref, input_ref, decay_ref, state_ref, cum_ref,
    padded, low, pre,
):
    tokens, wide = u_ref.shape[1:]
    own = recur_ref.shape[2]
    odd = odd_ref[0] == 1
    padded[0:8] = rim_ref[0]
    padded[8:] = u_ref[0]
    taps = cw_ref.shape[0]

    def convolve(index, carry):
        start = pl.multiple_of(index * 32, 32)
        window = padded[pl.ds(start, 40), :]
        out = cb_ref[...] + cw_ref[0:1] * window[8:]
        for k in range(1, taps):
            out = out + cw_ref[k : k + 1] * pltpu.roll(window, k, 0)[8:]
        conv_ref[0, pl.ds(start, 32), :] = out
        low[pl.ds(start, 32), :] = out.astype(bf16)
        return carry

    lax.fori_loop(0, tokens // 32, convolve, 0)
    for g in range(2):
        for h in range(2):
            cols = slice(h * head, (h + 1) * head)
            pre[g, :, cols] = jnp.dot(low[:, cols], gw_ref[g, h], preferred_element_type=f32)
        pre[g, :, 2 * head :] = jnp.dot(low[:, 2 * head :], gs_ref[g], preferred_element_type=f32)
    row = rows_of((8, own))

    def scan(index, carry):
        cum, state = carry
        start = pl.multiple_of(index * 16, 16)
        span = pl.ds(start, 16)
        recur = jax.nn.sigmoid(pre[0, span, :] + gb_ref[0:1])
        gate = jax.nn.sigmoid(pre[1, span, :] + gb_ref[1:2])
        log_decay = recur * sp_ref[...]
        decay = jnp.exp(log_decay)
        conv = conv_ref[0, span, :]
        conv = jnp.concatenate([conv[:, : 2 * head], pick(odd, conv, head // 2)], 1)
        driven = conv * gate * jnp.sqrt(one_less_square(2.0 * log_decay))
        recur_ref[0, span, :] = recur
        input_ref[0, span, :] = gate
        decay_ref[0, span, :] = decay
        for tile in range(2):
            a = decay[tile * 8 : tile * 8 + 8]
            b = driven[tile * 8 : tile * 8 + 8]
            for d in (1, 2, 4):
                there = row >= d
                before_a = jnp.where(there, pltpu.roll(a, d, 0), 1.0)
                before_b = jnp.where(there, pltpu.roll(b, d, 0), 0.0)
                b = b + a * before_b
                a = a * before_a
            b = b + a * state
            a = a * cum
            place = pl.ds(start + tile * 8, 8)
            state_ref[0, place, :] = b
            cum_ref[0, place, :] = a
            cum, state = a[7:8], b[7:8]
        return cum, state

    lax.fori_loop(
        0, tokens // 16, scan, (jnp.ones((1, own), f32), jnp.zeros((1, own), f32))
    )


def merge_kernel(state_ref, cum_ref, carry_ref, pre_ref, h_ref, merged_ref):
    def step(index, none):
        span = pl.ds(pl.multiple_of(index * 32, 32), 32)
        state = state_ref[0, span, :] + cum_ref[0, span, :] * carry_ref[0, 0:1]
        h_ref[0, span, :] = state
        merged_ref[0, span, :] = (state * gelu(pre_ref[0, span, :])).astype(bf16)
        return none

    lax.fori_loop(0, state_ref.shape[1] // 32, step, 0)


def adjoint_kernel(gm_ref, h_ref, pre_ref, decay_ref, gh_ref, gpre_ref, back_ref, cum_ref):
    tokens, own = gm_ref.shape[1:]
    row = rows_of((8, own))
    count = tokens // 16

    def step(index, carry):
        cum, back = carry
        start = pl.multiple_of((count - 1 - index) * 16, 16)
        span = pl.ds(start, 16)
        grad = gm_ref[0, span, :]
        act, slope = gelu_both(pre_ref[0, span, :])
        gpre_ref[0, span, :] = (grad * h_ref[0, span, :] * slope).astype(bf16)
        grad_h = grad * act
        gh_ref[0, span, :] = grad_h
        decay = decay_ref[0, span, :]
        driven = decay * grad_h
        for tile in (1, 0):
            a = decay[tile * 8 : tile * 8 + 8]
            b = driven[tile * 8 : tile * 8 + 8]
            for d in (1, 2, 4):
                there = row < 8 - d
                after_a = jnp.where(there, pltpu.roll(a, 8 - d, 0), 1.0)
                after_b = jnp.where(there, pltpu.roll(b, 8 - d, 0), 0.0)
                b = b + a * after_b
                a = a * after_a
            b = b + a * back
            a = a * cum
            place = pl.ds(start + tile * 8, 8)
            back_ref[0, place, :] = b
            cum_ref[0, place, :] = a
            cum, back = a[0:1], b[0:1]
        return cum, back

    lax.fori_loop(0, count, step, (jnp.ones((1, own), f32), jnp.zeros((1, own), f32)))


def backward_kernel(
    head, odd_ref, back_ref, cum_ref, gh_ref, h_ref, carry_ref, enter_ref, recur_ref, input_ref,
    decay_ref, conv_ref, u_ref, rim_ref, cw_ref, gw_ref, gs_ref, sp_ref,
    gu_ref, tail_ref, lead_ref, small_ref, taps_ref, gwg_ref, gsg_ref,
    padded, ahead, behind, low, gg, direct,
):
    tokens, wide = u_ref.shape[1:]
    own = recur_ref.shape[2]
    half = head // 2
    odd = odd_ref[0] == 1
    taps = cw_ref.shape[0]

    @pl.when(pl.program_id(0) == 0)
    def _():
        small_ref[...] = jnp.zeros_like(small_ref)
        taps_ref[...] = jnp.zeros_like(taps_ref)
        gwg_ref[...] = jnp.zeros_like(gwg_ref)
        gsg_ref[...] = jnp.zeros_like(gsg_ref)

    padded[0:8] = rim_ref[0]
    padded[8:] = u_ref[0]
    behind[0:8] = carry_ref[0]
    ahead[tokens:] = enter_ref[0]
    direct[tokens:] = jnp.zeros((8, wide), f32)
    enter = enter_ref[0, 0:1]

    def prepare(index, none):
        start = pl.multiple_of(index * 32, 32)
        span = pl.ds(start, 32)
        ahead[span, :] = back_ref[0, span, :] + cum_ref[0, span, :] * enter
        behind[pl.ds(start + 8, 32), :] = h_ref[0, span, :]
        return none

    lax.fori_loop(0, tokens // 32, prepare, 0)

    def gates(index, sums):
        sum_recur, sum_input, sum_decay = sums
        start = pl.multiple_of(index * 16, 16)
        span = pl.ds(start, 16)
        after = pltpu.roll(ahead[pl.ds(start, 24), :], 23, 0)[:16]
        before = pltpu.roll(behind[pl.ds(start, 24), :], 1, 0)[8:]
        adj = gh_ref[0, span, :] + after
        recur = recur_ref[0, span, :]
        gate = input_ref[0, span, :]
        decay = decay_ref[0, span, :]
        whole = conv_ref[0, span, :]
        low[span, :] = whole.astype(bf16)
        conv = jnp.concatenate([whole[:, : 2 * head], pick(odd, whole, half)], 1)
        square = one_less_square(2.0 * (recur * sp_ref[...]))
        inverse = lax.rsqrt(square)
        root = square * inverse
        grad_a = adj * before
        part = adj * gate
        grad_direct = part * root
        grad_gate = adj * conv * root
        grad_root = part * conv
        grad_log = decay * (grad_a - grad_root * decay * inverse)
        scaled = grad_log * recur
        grad_recur = scaled * sp_ref[...] * (1.0 - recur)
        grad_input = grad_gate * gate * (1.0 - gate)
        gg[0, span, :] = grad_recur.astype(bf16)
        gg[1, span, :] = grad_input.astype(bf16)
        shared = grad_direct[:, 2 * head :]
        none = jnp.zeros_like(shared)
        direct[span, :] = jnp.concatenate(
            [grad_direct[:, : 2 * head], jnp.where(odd, none, shared), jnp.where(odd, shared, none)],
            1,
        )
        fold = lambda old, new: old + new[:8] + new[8:]
        return fold(sum_recur, grad_recur), fold(sum_input, grad_input), fold(sum_decay, scaled)

    zero = jnp.zeros((8, own), f32)
    sums = lax.fori_loop(0, tokens // 16, gates, (zero, zero, zero))
    for position, value in enumerate(sums):
        small_ref[position : position + 1] += jnp.sum(value, axis=0, keepdims=True)
    across = (((1,), (1,)), ((), ()))
    down = (((0,), (0,)), ((), ()))
    for h in range(2):
        cols = slice(h * head, (h + 1) * head)
        direct[0:tokens, cols] += lax.dot_general(
            gg[0, :, cols], gw_ref[0, h], across, preferred_element_type=f32
        ) + lax.dot_general(gg[1, :, cols], gw_ref[1, h], across, preferred_element_type=f32)
        for g in range(2):
            gwg_ref[g, h] += lax.dot_general(
                low[:, cols], gg[g, :, cols], down, preferred_element_type=f32
            )
    direct[0:tokens, 2 * head :] += lax.dot_general(
        gg[0, :, 2 * head :], gs_ref[0], across, preferred_element_type=f32
    ) + lax.dot_general(gg[1, :, 2 * head :], gs_ref[1], across, preferred_element_type=f32)
    for g in range(2):
        gsg_ref[g] += lax.dot_general(
            low[:, 2 * head :], gg[g, :, 2 * head :], down, preferred_element_type=f32
        )

    def deconvolve(index, sums):
        start = pl.multiple_of(index * 16, 16)
        window = direct[pl.ds(start, 24), :]
        inputs = padded[pl.ds(start, 24), :]
        grad = window[:16]
        out = cw_ref[0:1] * grad
        fold = lambda old, new: old + new[:8] + new[8:]
        new = [fold(sums[0], grad), fold(sums[1], grad * inputs[8:])]
        for k in range(1, taps):
            out = out + cw_ref[k : k + 1] * pltpu.roll(window, 24 - k, 0)[:16]
            new.append(fold(sums[k + 1], grad * pltpu.roll(inputs, k, 0)[8:]))
        gu_ref[0, pl.ds(start, 16), :] = out.astype(bf16)

        @pl.when(index == tokens // 16 - 1)
        def _():
            tail_ref[0] = out[8:]

        return tuple(new)

    zero = jnp.zeros((8, wide), f32)
    sums = lax.fori_loop(0, tokens // 16, deconvolve, (zero,) * (taps + 1))
    for position, value in enumerate(sums):
        taps_ref[position : position + 1] += jnp.sum(value, axis=0, keepdims=True)
    first = direct[0:8, :]
    row = rows_of((8, wide))
    owed = jnp.zeros((8, wide), f32)
    for k in range(1, taps):
        moved = pltpu.roll(first, 8 - k, 0)
        owed = owed + cw_ref[k : k + 1] * jnp.where(row >= 8 - k, moved, 0.0)
    lead_ref[0] = owed


def mlp_kernel(normed_ref, weight_ref, grad_ref, hidden_ref, out_ref):
    part = hidden_ref.shape[1]
    rows = 256

    def step(index, none):
        span = pl.ds(pl.multiple_of(index * rows, rows), rows)
        both = jnp.dot(normed_ref[span, :], weight_ref[...], preferred_element_type=f32)
        act, slope = gelu_both(both[:, :part])
        up = both[:, part:]
        grad = grad_ref[span, :].astype(f32)
        hidden_ref[span, :] = (act * up).astype(bf16)
        out_ref[span, :part] = (grad * up * slope).astype(bf16)
        out_ref[span, part:] = (grad * act).astype(bf16)
        return none

    lax.fori_loop(0, normed_ref.shape[0] // rows, step, 0)


def params(*semantics):
    return pltpu.CompilerParams(dimension_semantics=semantics, vmem_limit_bytes=VMEM_LIMIT)


def per_seq(*shape):
    return pl.BlockSpec((1, *shape), lambda i: (i,) + (0,) * len(shape))


def whole(*shape):
    return pl.BlockSpec(shape, lambda i: (0,) * len(shape))


SCALAR = pl.BlockSpec(memory_space=pltpu.SMEM)


def cost(elements, operations, moved):
    return pl.CostEstimate(
        flops=elements * operations, bytes_accessed=moved, transcendentals=elements * 6
    )


def shards(
    block_input,
    out_cotangent,
    norm_gain,
    in_weight,
    conv_weight,
    conv_bias,
    gate_weight,
    gate_bias,
    decay_param,
    out_weight,
    mlp_gain,
    mlp_weight,
    down_weight,
):
    _, tokens, model = block_input.shape
    taps, rec = conv_weight.shape
    heads, head = gate_weight.shape[1:3]
    members = lax.axis_size("seq")
    devices = lax.axis_size("group")
    hidden = mlp_weight.shape[1] // 2
    assert members == 4 and heads == 10
    half = head // 2
    own = 2 * head + half
    wide = 3 * head
    mine = lax.axis_index("seq")
    odd = mine % 2

    def first_of(member):
        return 5 * (member // 2) + 3 * (member % 2), 5 * (member // 2) + 2

    first, shared = first_of(mine)

    def widen(value, offset=0):
        return jnp.concatenate(
            [
                lax.dynamic_slice_in_dim(value, offset + first * head, 2 * head, value.ndim - 1),
                lax.dynamic_slice_in_dim(value, offset + shared * head, head, value.ndim - 1),
            ],
            -1,
        )

    def owned(value, offset=0):
        return jnp.concatenate(
            [
                lax.dynamic_slice_in_dim(value, offset + first * head, 2 * head, value.ndim - 1),
                lax.dynamic_slice_in_dim(
                    value, offset + shared * head + odd * half, half, value.ndim - 1
                ),
            ],
            -1,
        )

    in_u = gather_group(widen(in_weight))
    in_y = gather_group(owned(in_weight, rec))
    out_piece = model // members
    out_cols = gather_group(
        lax.dynamic_slice_in_dim(out_weight, mine * out_piece, out_piece, 1)
    )
    fine = hidden // devices // members
    down_rows = gather_group(lax.dynamic_slice_in_dim(down_weight, mine * fine, fine, 0))
    part = min(384, hidden // members)
    per_part = part // fine
    parts = hidden // members // part
    cut = mlp_weight.reshape(-1, 2, parts, per_part, members, fine)
    cut = lax.dynamic_index_in_dim(cut, mine, 4, keepdims=False)
    mlp_cols = gather_group(cut.transpose(0, 2, 1, 3, 4).reshape(mlp_weight.shape[0], -1))

    x_own = block_input[0]
    c_own = out_cotangent[0]
    x_all = jnp.concatenate(gather_seq(x_own), 0)
    c_all = jnp.concatenate(gather_seq(c_own), 0)
    normed = rms_low(x_all.astype(f32), norm_gain)

    def rows_for(value, k):
        start, common = first_of(mine ^ k)
        return jnp.concatenate(
            [
                lax.dynamic_slice_in_dim(value, start * head, 2 * head, 0),
                lax.dynamic_slice_in_dim(
                    value, common * head + ((mine ^ k) % 2) * half, half, 0
                ),
            ],
            0,
        )

    out_rows = jnp.zeros((own, model), bf16)
    for k in range(members):
        piece = rows_for(out_cols, k)
        if k:
            piece = swap(piece, k)
        out_rows = lax.dynamic_update_slice_in_dim(out_rows, piece, (mine ^ k) * out_piece, 1)

    u = jnp.dot(normed, in_u, preferred_element_type=f32).reshape(members, tokens, wide)
    y = jnp.dot(normed, in_y, preferred_element_type=f32).reshape(members, tokens, own)
    lead = taps - 1
    rim = jnp.pad(shift(u[:, tokens - lead :], 1), ((0, 0), (8 - lead, 0), (0, 0)))
    odd_flag = odd.astype(jnp.int32).reshape(1)
    cw = widen(conv_weight)
    cb = widen(conv_bias)[None]
    gb = owned(gate_bias)
    soft = -8.0 * owned(jax.nn.softplus(decay_param))[None]
    gw = lax.dynamic_slice_in_dim(gate_weight, first, 2, 1)
    gs = lax.dynamic_slice(
        gate_weight, (0, shared, 0, odd * half), (2, 1, head, half)
    )[:, 0]
    rows = members * tokens
    full = jax.ShapeDtypeStruct((members, tokens, own), f32)
    conv, recur, gate, decay, state_local, decay_cum = pl.pallas_call(
        functools.partial(forward_kernel, head),
        grid=(members,),
        in_specs=[
            SCALAR,
            per_seq(tokens, wide),
            per_seq(8, wide),
            whole(taps, wide),
            whole(1, wide),
            whole(2, 2, head, head),
            whole(2, head, half),
            whole(2, own),
            whole(1, own),
        ],
        out_specs=[per_seq(tokens, wide)] + [per_seq(tokens, own)] * 5,
        out_shape=[jax.ShapeDtypeStruct((members, tokens, wide), f32)] + [full] * 5,
        scratch_shapes=[
            pltpu.VMEM((tokens + 8, wide), f32),
            pltpu.VMEM((tokens, wide), bf16),
            pltpu.VMEM((2, tokens, own), f32),
        ],
        compiler_params=params("arbitrary"),
        cost_estimate=cost(rows * own, 1100, rows * own * 28),
        name="recurrence_forward",
    )(odd_flag, u, rim, cw, cb, gw, gs, gb, soft)
    carried = entering(decay_cum[:, -1], state_local[:, -1], 1)
    carried8 = jnp.broadcast_to(carried[:, None], (members, 8, own))
    h, merged = pl.pallas_call(
        merge_kernel,
        grid=(members,),
        in_specs=[per_seq(tokens, own)] * 2 + [per_seq(8, own), per_seq(tokens, own)],
        out_specs=[per_seq(tokens, own)] * 2,
        out_shape=[full, jax.ShapeDtypeStruct((members, tokens, own), bf16)],
        compiler_params=params("arbitrary"),
        cost_estimate=cost(rows * own, 20, rows * own * 18),
        name="recurrence_merge",
    )(state_local, decay_cum, carried8, y)
    partial = [None] * members
    for k in (3, 1, 2, 0):
        partial[k] = jnp.dot(merged[k], out_rows, preferred_element_type=f32).astype(bf16)
    x32 = x_own.astype(f32)
    resid = x32 + scatter_seq(partial)
    normed2 = jnp.concatenate(gather_seq(rms_low(resid, mlp_gain)), 0)

    grad_hidden = lax.dot_general(
        c_all, down_rows, (((1,), (1,)), ((), ())), preferred_element_type=f32
    )
    width = parts * part
    hidden_low, grad_gu = pl.pallas_call(
        mlp_kernel,
        grid=(parts,),
        in_specs=[
            whole(rows, model),
            pl.BlockSpec((model, 2 * part), lambda i: (0, i)),
            pl.BlockSpec((rows, part), lambda i: (0, i)),
        ],
        out_specs=[
            pl.BlockSpec((rows, part), lambda i: (0, i)),
            pl.BlockSpec((rows, 2 * part), lambda i: (0, i)),
        ],
        out_shape=[
            jax.ShapeDtypeStruct((rows, width), bf16),
            jax.ShapeDtypeStruct((rows, 2 * width), bf16),
        ],
        compiler_params=params("arbitrary"),
        cost_estimate=pl.CostEstimate(
            flops=4 * rows * model * width,
            bytes_accessed=rows * model * 2 + model * width * 4 + rows * width * 10,
            transcendentals=rows * width,
        ),
        name="mlp",
    )(normed2, mlp_cols, grad_hidden)
    partial = [None] * members
    for k in (3, 1, 2, 0):
        partial[k] = lax.dot_general(
            grad_gu[k * tokens : (k + 1) * tokens],
            mlp_cols,
            (((1,), (1,)), ((), ())),
            preferred_element_type=f32,
        ).astype(bf16)
    grad_normed2 = scatter_seq(partial)
    grad_resid_norm, mlp_gain_grad = rms_back(resid, mlp_gain, grad_normed2)
    grad_resid = c_own.astype(f32) + grad_resid_norm
    grad_resid_all = jnp.concatenate(gather_seq(grad_resid.astype(bf16)), 0)

    down = (((0,), (0,)), ((), ()))
    down_sum = scatter_group(
        lax.dot_general(hidden_low, c_all, down, preferred_element_type=f32).astype(bf16)
    )
    mlp_sum = scatter_group(
        lax.dot_general(normed2, grad_gu, down, preferred_element_type=f32).astype(bf16)
    )
    partial = [None] * members
    for k in (3, 1, 2, 0):
        partial[k] = jnp.dot(
            hidden_low[k * tokens : (k + 1) * tokens], down_rows, preferred_element_type=f32
        ).astype(bf16)
    block_out = (resid + scatter_seq(partial)).astype(bf16)[None]

    grad_merged = lax.dot_general(
        grad_resid_all, out_rows, (((1,), (1,)), ((), ())), preferred_element_type=f32
    ).reshape(members, tokens, own)
    grad_h, grad_y, back_local, back_cum = pl.pallas_call(
        adjoint_kernel,
        grid=(members,),
        in_specs=[per_seq(tokens, own)] * 4,
        out_specs=[per_seq(tokens, own)] * 4,
        out_shape=[full, jax.ShapeDtypeStruct((members, tokens, own), bf16), full, full],
        compiler_params=params("arbitrary"),
        cost_estimate=cost(rows * own, 50, rows * own * 30),
        name="recurrence_adjoint",
    )(grad_merged, h, y, decay)
    incoming = entering(back_cum[:, 0], back_local[:, 0], -1)
    incoming8 = jnp.broadcast_to(incoming[:, None], (members, 8, own))
    grad_u, tail, owed, small, tap_sums, gw_grad, gs_grad = pl.pallas_call(
        functools.partial(backward_kernel, head),
        grid=(members,),
        in_specs=[
            SCALAR,
            *[per_seq(tokens, own)] * 4,
            per_seq(8, own),
            per_seq(8, own),
            *[per_seq(tokens, own)] * 3,
            *[per_seq(tokens, wide)] * 2,
            per_seq(8, wide),
            whole(taps, wide),
            whole(2, 2, head, head),
            whole(2, head, half),
            whole(1, own),
        ],
        out_specs=[
            per_seq(tokens, wide),
            per_seq(8, wide),
            per_seq(8, wide),
            whole(8, own),
            whole(8, wide),
            whole(2, 2, head, head),
            whole(2, head, half),
        ],
        out_shape=[
            jax.ShapeDtypeStruct((members, tokens, wide), bf16),
            jax.ShapeDtypeStruct((members, 8, wide), f32),
            jax.ShapeDtypeStruct((members, 8, wide), f32),
            jax.ShapeDtypeStruct((8, own), f32),
            jax.ShapeDtypeStruct((8, wide), f32),
            jax.ShapeDtypeStruct((2, 2, head, head), f32),
            jax.ShapeDtypeStruct((2, head, half), f32),
        ],
        scratch_shapes=[
            pltpu.VMEM((tokens + 8, wide), f32),
            pltpu.VMEM((tokens + 8, own), f32),
            pltpu.VMEM((tokens + 8, own), f32),
            pltpu.VMEM((tokens, wide), bf16),
            pltpu.VMEM((2, tokens, own), bf16),
            pltpu.VMEM((tokens + 8, wide), f32),
        ],
        compiler_params=params("arbitrary"),
        cost_estimate=cost(rows * own, 2200, rows * own * 36),
        name="recurrence_backward",
    )(
        odd_flag, back_local, back_cum, grad_h, h, carried8, incoming8, recur, gate,
        decay, conv, u, rim, cw, gw, gs, soft,
    )
    tail = (tail + shift(owed, -1)).astype(bf16)
    grad_u = lax.dynamic_update_slice(grad_u, tail, (0, tokens - 8, 0))
    flat_u = grad_u.reshape(rows, wide)
    flat_y = grad_y.reshape(rows, own)
    partial = [None] * members
    across = (((1,), (1,)), ((), ()))
    for k in (3, 1, 2, 0):
        partial[k] = (
            lax.dot_general(grad_u[k], in_u, across, preferred_element_type=f32)
            + lax.dot_general(grad_y[k], in_y, across, preferred_element_type=f32)
        ).astype(bf16)
    grad_normed = scatter_seq(partial)
    grad_input_norm, norm_gain_grad = rms_back(x32, norm_gain, grad_normed)
    input_grad = (grad_resid + grad_input_norm)[None]

    y_sum = scatter_group(
        lax.dot_general(normed, flat_y, down, preferred_element_type=f32).astype(bf16)
    )
    u_sum = scatter_group(
        lax.dot_general(normed, flat_u, down, preferred_element_type=f32).astype(bf16)
    )
    out_part = lax.dot_general(
        merged.reshape(rows, own), grad_resid_all, down, preferred_element_type=f32
    ).astype(bf16)
    out_terms = jnp.zeros((rec, out_piece), bf16)
    for k in range(members):
        piece = lax.dynamic_slice_in_dim(out_part, (mine ^ k) * out_piece, out_piece, 1)
        if k:
            piece = swap(piece, k)
        start, common = first_of(mine ^ k)
        out_terms = lax.dynamic_update_slice_in_dim(
            out_terms, piece[: 2 * head], start * head, 0
        )
        out_terms = lax.dynamic_update_slice_in_dim(
            out_terms, piece[2 * head :], common * head + ((mine ^ k) % 2) * half, 0
        )
    out_sum = scatter_group(out_terms)

    down_parts = jnp.stack(gather_seq(down_sum))
    down_grad = jnp.concatenate(
        [lax.dynamic_index_in_dim(down_parts, mine ^ a, 0, keepdims=False) for a in range(members)],
        0,
    ).astype(f32)
    mlp_parts = jnp.stack(gather_seq(mlp_sum))
    mlp_grad = jnp.stack(
        [
            lax.dynamic_index_in_dim(mlp_parts, mine ^ a, 0, keepdims=False).reshape(
                -1, parts, 2, per_part, fine
            )
            for a in range(members)
        ],
        4,
    )
    mlp_grad = mlp_grad.transpose(0, 2, 1, 3, 4, 5).reshape(-1, 2 * hidden).astype(f32)
    out_parts = jnp.stack(gather_seq(out_sum))
    out_grad = jnp.concatenate(
        [lax.dynamic_index_in_dim(out_parts, mine ^ a, 0, keepdims=False) for a in range(members)],
        1,
    ).astype(f32)
    u_parts = gather_seq(u_sum)
    y_parts = gather_seq(y_sum)
    in_grad = jnp.zeros((u_sum.shape[0], 2 * rec), f32)
    for k in range(members):
        start, common = first_of(mine ^ k)
        in_grad = lax.dynamic_update_slice_in_dim(
            in_grad, u_parts[k][:, : 2 * head].astype(f32), start * head, 1
        )
        in_grad = lax.dynamic_update_slice_in_dim(
            in_grad, y_parts[k][:, : 2 * head].astype(f32), rec + start * head, 1
        )
        in_grad = lax.dynamic_update_slice_in_dim(
            in_grad,
            y_parts[k][:, 2 * head :].astype(f32),
            rec + common * head + ((mine ^ k) % 2) * half,
            1,
        )
        if k % 2 == 0:
            both = u_parts[k][:, 2 * head :].astype(f32) + u_parts[k + 1][:, 2 * head :].astype(f32)
            in_grad = lax.dynamic_update_slice_in_dim(in_grad, both, common * head, 1)

    gate_terms = jnp.concatenate([gw_grad[:, 0], gw_grad[:, 1], gs_grad], -1).astype(bf16)
    gate_sum = lax.psum(gate_terms, "group")
    gate_parts = gather_seq(gate_sum.reshape(2 * head, own))
    gate_grad = jnp.zeros((2, heads, head, head), f32)
    for k in range(members):
        start, common = first_of(mine ^ k)
        block = gate_parts[k].reshape(2, head, own).astype(f32)
        pair = block[:, :, : 2 * head].reshape(2, head, 2, head).transpose(0, 2, 1, 3)
        gate_grad = lax.dynamic_update_slice_in_dim(gate_grad, pair, start, 1)
        if k % 2 == 0:
            other = gate_parts[k + 1].reshape(2, head, own).astype(f32)
            halves = jnp.where(
                odd == 1,
                jnp.concatenate([other[..., 2 * head :], block[..., 2 * head :]], -1),
                jnp.concatenate([block[..., 2 * head :], other[..., 2 * head :]], -1),
            )
            gate_grad = lax.dynamic_update_slice_in_dim(gate_grad, halves[:, None], common, 1)

    def place(value, wide_shared):
        out = jnp.zeros((value.shape[0], rec), f32)
        out = lax.dynamic_update_slice_in_dim(out, value[:, : 2 * head], first * head, 1)
        at = shared * head if wide_shared else shared * head + odd * half
        return lax.dynamic_update_slice_in_dim(out, value[:, 2 * head :], at, 1)

    decay_terms = small[2:3] * (-8.0) * owned(jax.nn.sigmoid(decay_param))[None]
    channel = jnp.concatenate(
        [place(tap_sums[: taps + 1], True), place(jnp.concatenate([small[:2], decay_terms], 0), False)],
        0,
    )
    packed = jnp.concatenate([channel.reshape(-1, 128), mlp_gain_grad.reshape(-1, 128)], 0)
    packed = total(packed)
    channel = packed[: (taps + 4) * rec // 128].reshape(taps + 4, rec)
    mlp_gain_grad = packed[(taps + 4) * rec // 128 :].reshape(-1)
    norm_gain_grad = total(norm_gain_grad.reshape(-1, 128)).reshape(-1)
    return (
        block_out,
        input_grad,
        norm_gain_grad,
        in_grad,
        channel[1 : taps + 1],
        channel[0],
        gate_grad,
        channel[taps + 1 : taps + 3],
        channel[taps + 3],
        out_grad,
        mlp_gain_grad,
        mlp_grad,
        down_grad,
    )


def solution(mesh):
    tokens = P("seq", "group", None)
    rows = P("group", None)
    in_specs = (tokens, tokens, P(), rows, P(), P(), P(), P(), P(), rows, P(), rows, rows)
    out_specs = (tokens, tokens, P(), rows, P(), P(), P(), P(), P(), rows, P(), rows, rows)
    return jax.shard_map(shards, mesh=mesh, in_specs=in_specs, out_specs=out_specs, check_vma=False)
```

time: 3870 us -> 987 us (0.26)
  waiting for transfers between devices: 2740 us -> 434 us
  local copies, waits for them, and re-layouts: 526 us -> 121 us
  other arithmetic: 220 us -> 64 us
  starting transfers between devices: 4.19 us -> 120 us
  blocking collectives: 106 us -> 0 us
  matrix products: 233 us -> 147 us
  Pallas kernels: 0 us -> 72.6 us
    unnamed x12 -> x11, waiting for transfers between devices: 954 us -> 0.18 us
    reduce_scatter x3 -> x5, waiting for transfers between devices: 812 us -> 88.4 us  [scatter_group(): return lax.psum_scatter(block, 'group', scatter_dimension=0, tiled=True)]
    all_gather x4 -> x5, waiting for transfers between devices: 530 us -> 22.2 us  [gather_group(): return lax.all_gather(block, 'group', axis=0, tiled=True)]
    psum x3 -> x1, waiting for transfers between devices: 445 us -> 0.01 us  [shards(): gate_sum = lax.psum(gate_terms, 'group')]
    ppermute x2 -> x90, waiting for transfers between devices: 2.38 us -> 323 us  [the longest x70 285 us: swap(): lax.ppermute(block, 'seq', [(i, i ^ k) for i in range(lax.axis_size('seq'...]
    slice x112 -> x42, local copies, waits for them, and re-layouts: 247 us -> 12.8 us  [the longest x20 5.8 us: gather_seq(): third = jnp.concatenate([swap(first[:half], 2), swap(second[half:], 1)], 0)]
    pad x56 -> x1, local copies, waits for them, and re-layouts: 146 us -> 0.66 us  [shards(): jnp.pad(shift(u[:, tokens - lead:], 1), ((0, 0), (8 - lead, 0), (0, 0)))]
    ppermute x2 -> x90, starting transfers between devices: 3.75 us -> 119 us  [the longest x70 81.3 us: swap(): lax.ppermute(block, 'seq', [(i, i ^ k) for i in range(lax.axis_size('seq'...]
  transfers between devices with their start and end apart: 13 -> 101, of which waited for: 11 -> 54; matrix products, arithmetic and copies ran while one was open for 23% -> 27% of each run, Pallas kernels for 0% -> 2%
where the time goes in v1:
time: 987 us; the launch traced here: 975 us
  waiting for transfers between devices  434 us (44%)
  matrix products  147 us (15%)
  local copies, waits for them, and re-layouts  121 us (12%)
  starting transfers between devices  120 us (12%)
  Pallas kernels  72.6 us (7%)
  other arithmetic  64 us (6%)
  between operations  16.3 us (2%)
    ppermute x70, waiting for transfers between devices, swap(): lax.ppermute(block, 'seq', [(i, i ^ k) for i in range(lax.axis_size('seq'...  285 us
    reduce_scatter x5, waiting for transfers between devices, scatter_group(): return lax.psum_scatter(block, 'group', scatter_dimension=0, tiled=True)  88.4 us
    ppermute x70, starting transfers between devices, swap(): lax.ppermute(block, 'seq', [(i, i ^ k) for i in range(lax.axis_size('seq'...  81.3 us
    unnamed x130, local copies, waits for them, and re-layouts  36.4 us
    dot_general x4, matrix products, shards(): lax.dot_general(grad_gu[k * tokens:(k + 1) * tokens], mlp_cols, (((1,), (...  34.2 us
    ppermute x10, starting transfers between devices, shift(): lax.ppermute(block, 'group', [(i - distance, i) for i in devices if i - d...  28.7 us
    pallas_call x1, Pallas kernels, shards(): pl.pallas_call(mlp_kernel, grid=(parts,), in_specs=[whole(rows, model), p...  23.1 us
    all_gather x5, waiting for transfers between devices, gather_group(): return lax.all_gather(block, 'group', axis=0, tiled=True)  22.2 us
  transfers between devices with their start and end apart: 101, of which 54 were waited for; matrix products, arithmetic and copies ran while one was open for 27% of the time, Pallas kernels for 2%

profile of v1, /device:TPU:0, one launch (start us, length us, event | category | flops | bytes accessed | tf_op | source)
XLA Modules:
  0.0 974.9 jit_solution(6440412985264364291)
XLA Ops:
  14.9 8.6 copy.49
  42.8 11.2 %collective-permute-done = bf16[256,2048]{1,0:T(8,128)(2,1)S(1)} collective-permute-done((bf16[256,2048]{1,0:T(8,128)(2,1)S(1)}, bf16[256,2048]{1,0:T(8,128)(2,1)S(1)}, u32[]{:S(2)}, u32[]{:S(2)}) %collective-permute-start) | collective-permute-done | bytes 1048608 | tf_op jit(solution)/shard_map/ppermute | solution.py:17
  69.3 17.6 %collective-permute-done.3 = bf16[128,2048]{1,0:T(8,128)(2,1)S(1)} collective-permute-done((bf16[128,2048]{1,0:T(8,128)(2,1)S(1)}, bf16[128,2048]{1,0:T(8,128)(2,1)S(1)}, u32[]{:S(2)}, u32[]{:S(2)}) %collective-permute-start.3) | collective-permute-done | bytes 524320 | tf_op jit(solution)/shard_map/ppermute | solution.py:17
  108.4 12.4 %all-gather.8.cloned.1.call-done = bf16[2048,640]{1,0:T(8,128)(2,1)} async-done(((bf16[256,640]{1,0:T(8,128)(2,1)}), bf16[2048,640]{1,0:T(8,128)(2,1)}) %all-gather.8.cloned.1.call-update) | async-done | bytes 2621456 | tf_op jit(solution)/shard_map/all_gather | solution.py:54
  129.4 14.5 %recurrence_forward.1 = (f32[4,256,768]{2,1,0:T(8,128)}, f32[4,256,640]{2,1,0:T(8,128)}, f32[4,256,640]{2,1,0:T(8,128)}, f32[4,256,640]{2,1,0:T(8,128)}, f32[4,256,640]{2,1,0:T(8,128)}, /*index=5*/f32[4,256,640]{2,1,0:T(8,128)}) custom-call(s32[1]{0:T(128)} %bitcast.odd_ref, f32[4,256,768]{2,1,0:T(8,128)} %bitcast.282, f32[4,8,768]{2,1,0:T(8,128)} %pad.4.rim_ref, ...), custom_call_target="tpu_custom_call" | custom-call | flops 720896000 | bytes 18350080 | tf_op jit(solution)/shard_map/recurrence_forward/pallas_call | solution.py:520
  160.6 9.3 collective-permute-start.8
  186.9 8.6 collective-permute-done.13
  207.9 11.2 %collective-permute-done.14 = bf16[128,2048]{1,0:T(8,128)(2,1)S(1)} collective-permute-done((bf16[128,2048]{1,0:T(8,128)(2,1)S(1)}, bf16[128,2048]{1,0:T(8,128)(2,1)S(1)}, u32[]{:S(2)}, u32[]{:S(2)}) %collective-permute-start.14) | collective-permute-done | bytes 524320 | tf_op jit(solution)/shard_map/ppermute | solution.py:17
  225.1 16.5 %collective-permute-done.23 = bf16[256,2048]{1,0:T(8,128)(2,1)S(1)} collective-permute-done((bf16[256,2048]{1,0:T(8,128)(2,1)}, bf16[256,2048]{1,0:T(8,128)(2,1)S(1)}, u32[]{:S(2)}, u32[]{:S(2)}) %collective-permute-start.23) | collective-permute-done | bytes 1048608 | tf_op jit(solution)/shard_map/ppermute | solution.py:17
  243.9 9.0 collective-permute-done.24
  254.6 20.0 %collective-permute-done.19 = bf16[256,2048]{1,0:T(8,128)(2,1)S(1)} collective-permute-done((bf16[256,2048]{1,0:T(8,128)(2,1)S(1)}, bf16[256,2048]{1,0:T(8,128)(2,1)S(1)}, u32[]{:S(2)}, u32[]{:S(2)}) %collective-permute-start.19) | collective-permute-done | bytes 1048608 | tf_op jit(solution)/shard_map/ppermute | solution.py:17
  284.7 11.7 %fusion.75.grad_ref = f32[1024,1536]{1,0:T(8,128)} fusion(bf16[1024,2048]{1,0:T(8,128)(2,1)} %copy-done.43, bf16[1536,2048]{1,0:T(8,128)(2,1)} %all-gather.14.cloned.1.call-done), kind=kOutput, calls=%fused_computation.295 | convolution fusion | flops 6442450944 | bytes 16777216 | tf_op jit(solution)/shard_map/dot_general | solution.py:564
  296.4 9.8 %all-gather.12.cloned.1.call-done.weight_ref = bf16[2048,3072]{1,0:T(8,128)(2,1)} async-done(((bf16[256,3072]{1,0:T(8,128)(2,1)}), bf16[2048,3072]{1,0:T(8,128)(2,1)}) %all-gather.12.cloned.1.call-update) | async-done | bytes 12582928 | tf_op jit(solution)/shard_map/all_gather | solution.py:54
  306.2 23.1 %mlp.1 = (bf16[1024,1536]{1,0:T(8,128)(2,1)}, bf16[1024,3072]{1,0:T(8,128)(2,1)}) custom-call(bf16[1024,2048]{1,0:T(8,128)(2,1)} %constant_dynamic-update-slice_fusion.5.normed_ref, bf16[2048,3072]{1,0:T(8,128)(2,1)} %all-gather.12.cloned.1.call-done.weight_ref, f32[1024,1536]{1,0:T(8,128)} %fusion.75.grad_ref), custom_call_target="tpu_custom_call" | custom-call | flops 12884901888 | bytes 32505856 | tf_op jit(solution)/shard_map/mlp/pallas_call | solution.py:568
  365.1 8.7 convolution_convert_fusion.16
  374.7 9.9 %collective-permute-done.34 = bf16[128,2048]{1,0:T(8,128)(2,1)S(1)} collective-permute-done((bf16[128,2048]{1,0:T(8,128)(2,1)S(1)}, bf16[128,2048]{1,0:T(8,128)(2,1)S(1)}, u32[]{:S(2)}, u32[]{:S(2)}) %collective-permute-start.34) | collective-permute-done | bytes 524320 | tf_op jit(solution)/shard_map/ppermute | solution.py:17
  391.4 20.9 %collective-permute-done.38 = bf16[256,2048]{1,0:T(8,128)(2,1)S(1)} collective-permute-done((bf16[256,2048]{1,0:T(8,128)(2,1)S(1)}, bf16[256,2048]{1,0:T(8,128)(2,1)S(1)}, u32[]{:S(2)}, u32[]{:S(2)}) %collective-permute-start.38) | collective-permute-done | bytes 1048608 | tf_op jit(solution)/shard_map/ppermute | solution.py:17
  415.7 9.1 collective-permute-done.40
  430.5 10.0 %recurrence_adjoint.1 = (f32[4,256,640]{2,1,0:T(8,128)}, bf16[4,256,640]{2,1,0:T(8,128)(2,1)}, f32[4,256,640]{2,1,0:T(8,128)}, f32[4,256,640]{2,1,0:T(8,128)}) custom-call(f32[4,256,640]{2,1,0:T(8,128)} %bitcast.284, f32[4,256,640]{2,1,0:T(8,128)} %get-tuple-element.39.h_ref, f32[4,256,640]{2,1,0:T(8,128)} %bitcast.258, ...), custom_call_target="tpu_custom_call" | custom-call | flops 32768000 | bytes 19660800 | tf_op jit(solution)/shard_map/recurrence_adjoint/pallas_call | solution.py:622
  461.8 18.9 %recurrence_backward.1 = (bf16[4,256,768]{2,1,0:T(8,128)(2,1)}, f32[4,8,768]{2,1,0:T(8,128)}, f32[4,8,768]{2,1,0:T(8,128)}, f32[8,640]{1,0:T(8,128)}, f32[8,768]...) custom-call(s32[1]{0:T(128)} %bitcast.odd_ref, f32[4,256,640]{2,1,0:T(8,128)} %get-tuple-element.41.back_ref, ...), custom_call_target="tpu_custom_call" | custom-call | flops 1441792000 | bytes 23592960 | tf_op jit(solution)/shard_map/recurrence_backward/pallas_call | solution.py:634
  504.8 12.0 %collective-permute-done.75 = bf16[640,512]{1,0:T(8,128)(2,1)} collective-permute-done((bf16[640,512]{1,0:T(8,128)(2,1)}, bf16[640,512]{1,0:T(8,128)(2,1)}, u32[]{:S(2)}, u32[]{:S(2)}) %collective-permute-start.75) | collective-permute-done | bytes 655392 | tf_op jit(solution)/shard_map/ppermute | solution.py:17
  518.8 12.3 %collective-permute-done.76 = bf16[640,512]{1,0:T(8,128)(2,1)S(1)} collective-permute-done((bf16[640,512]{1,0:T(8,128)(2,1)}, bf16[640,512]{1,0:T(8,128)(2,1)S(1)}, u32[]{:S(2)}, u32[]{:S(2)}) %collective-permute-start.76) | collective-permute-done | bytes 655392 | tf_op jit(solution)/shard_map/ppermute | solution.py:17
  546.7 11.0 %convolution_convert_fusion.1 = bf16[1536,2048]{1,0:T(8,128)(2,1)} fusion(bf16[1024,1536]{1,0:T(8,128)(2,1)S(1)} %copy-done.51, bf16[1024,2048]{1,0:T(8,128)(2,1)} %copy-done.43), kind=kOutput, calls=%fused_computation.7 | convolution fusion | flops 6445596672 | bytes 13631488 | tf_op jit(solution)/shard_map/dot_general | solution.py:607
  557.8 19.6 %convolution_convert_fusion = bf16[2048,3072]{1,0:T(8,128)(2,1)} fusion(bf16[1024,2048]{1,0:T(8,128)(2,1)} %constant_dynamic-update-slice_fusion.5.normed_ref, bf16[1024,3072]{1,0:T(8,128)(2,1)} %get-tuple-element.38), kind=kOutput, calls=%fused_computation.1 | convolution fusion | flops 12891193344 | bytes 23068672 | tf_op jit(solution)/shard_map/dot_general | solution.py:610
  616.9 11.2 %collective-permute-done.28 = bf16[128,2048]{1,0:T(8,128)(2,1)S(1)} collective-permute-done((bf16[128,2048]{1,0:T(8,128)(2,1)S(1)}, bf16[128,2048]{1,0:T(8,128)(2,1)S(1)}, u32[]{:S(2)}, u32[]{:S(2)}) %collective-permute-start.28) | collective-permute-done | bytes 524320 | tf_op jit(solution)/shard_map/ppermute | solution.py:17
  652.2 8.9 collective-permute-done.68
  694.9 8.9 collective-permute-done.49
  777.6 88.4 %reduce-scatter.12.cloned.1.call-done = bf16[256,3072]{1,0:T(8,128)(2,1)} async-done(((bf16[2048,3072]{1,0:T(8,128)(2,1)}), bf16[256,3072]{1,0:T(8,128)(2,1)}) %reduce-scatter.12.cloned.1.call-update) | async-done | bytes 1572880 | tf_op jit(solution)/shard_map/reduce_scatter | solution.py:58
  874.9 35.5 %collective-permute-done.89 = bf16[96,2048]{1,0:T(8,128)(2,1)S(1)} collective-permute-done((bf16[96,2048]{1,0:T(8,128)(2,1)S(1)}, bf16[96,2048]{1,0:T(8,128)(2,1)S(1)}, u32[]{:S(2)}, u32[]{:S(2)}) %collective-permute-start.89) | collective-permute-done | bytes 393248 | tf_op jit(solution)/shard_map/ppermute | solution.py:17
  917.7 8.9 collective-permute-done.85
  944.6 10.6 %copy.63 = f32[256,2,4,2,4,192]{0,5,4,3,2,1:T(8,128)} copy(f32[256,2,4,2,4,192]{0,5,3,1,2,4:T(8,128)} %convert_bitcast_fusion) | data formatting | bytes 25165824 | tf_op jit(solution)/shard_map/convert_element_type | solution.py:736
  955.2 12.7 %copy.64 = f32[256,12288]{1,0:T(8,128)} copy(f32[256,12288]{0,1:T(8,128)} %bitcast.252) | data formatting | bytes 25165824
  (560 shorter events, 457.6 us)
Async XLA Ops:
  7.2 83.6 %all-gather.10.cloned.1.call-start = ((), (), s32[]{:S(2)}) async-start(), calls=%async_computation.7 | async-start | bytes 2949120 | tf_op jit(solution)/shard_map/all_gather | solution.py:54
  9.1 91.4 %all-gather.6.cloned.1.call-start = ((), (), s32[]{:S(2)}) async-start(), calls=%async_computation.5 | async-start | bytes 3538944 | tf_op jit(solution)/shard_map/all_gather | solution.py:54
  12.0 108.8 %all-gather.8.cloned.1.call-start = ((), (), s32[]{:S(2)}) async-start(), calls=%async_computation.6 | async-start | bytes 2949120 | tf_op jit(solution)/shard_map/all_gather | solution.py:54
  13.8 270.9 %all-gather.14.cloned.1.call-start = ((), (), s32[]{:S(2)}) async-start(), calls=%async_computation.9 | async-start | bytes 7077888 | tf_op jit(solution)/shard_map/all_gather | solution.py:54
  14.8 291.3 %all-gather.12.cloned.1.call-start = ((), (), s32[]{:S(2)}) async-start(), calls=%async_computation.8 | async-start | bytes 14155776 | tf_op jit(solution)/shard_map/all_gather | solution.py:54
  26.9 635.0 %all-reduce.3.cloned.1.call-start = ((), (), s32[]{:S(2)}) async-start(), calls=%async_computation.12 | async-start | bytes 1310720 | tf_op jit(solution)/shard_map/psum | solution.py:764
  31.5 167.1 %collective-permute-start.22 = (bf16[256,2048]{1,0:T(8,128)(2,1)}, bf16[256,2048]{1,0:T(8,128)(2,1)}, u32[]{:S(2)}, u32[]{:S(2)}) collective-permute-start(bf16[256,2048]{1,0:T(8,128)(2,1)} %bitcast.19), channel_id=1, source_target_pairs={{0,8},{8,0},{16,24},{24,16},{1,9},{9,1},{17,25},{25,17},{2,10},{10... | collective-permute-start | bytes 3145736 | tf_op jit(solution)/shard_map/ppermute | solution.py:17
  95.3 55.4 %collective-permute-start.9 = (bf16[640,512]{1,0:T(8,128)(2,1)}, bf16[640,512]{1,0:T(8,128)(2,1)}, u32[]{:S(2)}, u32[]{:S(2)}) collective-permute-start(bf16[640,512]{1,0:T(8,128)(2,1)} %pad_maximum_fusion.5), channel_id=1, source_target_pairs={{0,8},{8,0},{16,24},{24,16},{1,9},{9,1},{17,25},{25,17},{2,10},{10... | collective-permute-start | bytes 1966088 | tf_op jit(solution)/shard_map/ppermute | solution.py:17
  97.9 60.7 %collective-permute-start.10 = (bf16[640,512]{1,0:T(8,128)(2,1)}, bf16[640,512]{1,0:T(8,128)(2,1)}, u32[]{:S(2)}, u32[]{:S(2)}) collective-permute-start(bf16[640,512]{1,0:T(8,128)(2,1)} %pad_maximum_fusion.6), channel_id=1, source_target_pairs={{0,16},{8,24},{16,0},{24,8},{1,17},{9,25},{17,1},{25,9},{2,18},{10... | collective-permute-start | bytes 1966088 | tf_op jit(solution)/shard_map/ppermute | solution.py:17
  100.3 69.6 %collective-permute-start.11 = (bf16[640,512]{1,0:T(8,128)(2,1)}, bf16[640,512]{1,0:T(8,128)(2,1)}, u32[]{:S(2)}, u32[]{:S(2)}) collective-permute-start(bf16[640,512]{1,0:T(8,128)(2,1)} %pad_maximum_fusion.7), channel_id=1, source_target_pairs={{0,24},{8,16},{16,8},{24,0},{1,25},{9,17},{17,9},{25,1},{2,26},{10... | collective-permute-start | bytes 1966088 | tf_op jit(solution)/shard_map/ppermute | solution.py:17
  198.6 43.1 %collective-permute-start.23 = (bf16[256,2048]{1,0:T(8,128)(2,1)}, bf16[256,2048]{1,0:T(8,128)(2,1)S(1)}, u32[]{:S(2)}, u32[]{:S(2)}) collective-permute-start(bf16[256,2048]{1,0:T(8,128)(2,1)} %bitcast.19), channel_id=1, source_target_pairs={{0,16},{8,24},{16,0},{24,8},{1,17},{9,25},{17,1},{25,9},{2,18},{10... | collective-permute-start | bytes 3145736 | tf_op jit(solution)/shard_map/ppermute | solution.py:17
  205.7 47.1 %collective-permute-start.24 = (bf16[128,2048]{1,0:T(8,128)(2,1)S(1)}, bf16[128,2048]{1,0:T(8,128)(2,1)S(1)}, u32[]{:S(2)}, u32[]{:S(2)}) collective-permute-start(bf16[128,2048]{1,0:T(8,128)(2,1)S(1)} %slice.588), channel_id=1, source_target_pairs={{0,16},{8,24},{16,0},{24,8},{1,17},{9,25},{17,1},{25,9},{2,18},{10... | collective-permute-start | bytes 1572872 | tf_op jit(solution)/shard_map/ppermute | solution.py:17
  221.8 31.1 %collective-permute-start.18 = (bf16[256,2048]{1,0:T(8,128)(2,1)S(1)}, bf16[256,2048]{1,0:T(8,128)(2,1)S(1)}, u32[]{:S(2)}, u32[]{:S(2)}) collective-permute-start(bf16[256,2048]{1,0:T(8,128)(2,1)S(1)} %get-tuple-element.89), channel_id=1, source_target_pairs={{0,8},{8,0},{16,24},{24,16},{1,9},{9,1},{17,25},{25,17},{2,10},{10... | collective-permute-start | bytes 3145736 | tf_op jit(solution)/shard_map/ppermute | solution.py:17
  222.5 52.0 %collective-permute-start.19 = (bf16[256,2048]{1,0:T(8,128)(2,1)S(1)}, bf16[256,2048]{1,0:T(8,128)(2,1)S(1)}, u32[]{:S(2)}, u32[]{:S(2)}) collective-permute-start(bf16[256,2048]{1,0:T(8,128)(2,1)S(1)} %get-tuple-element.89), channel_id=1, source_target_pairs={{0,16},{8,24},{16,0},{24,8},{1,17},{9,25},{17,1},{25,9},{2,18},{10... | collective-permute-start | bytes 3145736 | tf_op jit(solution)/shard_map/ppermute | solution.py:17
  484.1 242.0 %reduce-scatter.8.cloned.1.call-start = ((), (), s32[]{:S(2)}) async-start(), calls=%async_computation.11 | async-start | bytes 2949120 | tf_op jit(solution)/shard_map/reduce_scatter | solution.py:58
  491.8 236.2 %reduce-scatter.10.cloned.1.call-start = ((), (), s32[]{:S(2)}) async-start(), calls=%async_computation.13 | async-start | bytes 2949120 | tf_op jit(solution)/shard_map/reduce_scatter | solution.py:58
  532.7 221.8 %reduce-scatter.6.cloned.1.call-start = ((), (), s32[]{:S(2)}) async-start(), calls=%async_computation.10 | async-start | bytes 3538944 | tf_op jit(solution)/shard_map/reduce_scatter | solution.py:58
  544.9 230.4 %reduce-scatter.14.cloned.1.call-start = ((), (), s32[]{:S(2)}) async-start(), calls=%async_computation.15 | async-start | bytes 7077888 | tf_op jit(solution)/shard_map/reduce_scatter | solution.py:58
  557.7 308.2 %reduce-scatter.12.cloned.1.call-start = ((), (), s32[]{:S(2)}) async-start(), calls=%async_computation.14 | async-start | bytes 14155776 | tf_op jit(solution)/shard_map/reduce_scatter | solution.py:58
  638.7 36.1 %collective-permute-start.48 = (bf16[128,2048]{1,0:T(8,128)(2,1)}, bf16[128,2048]{1,0:T(8,128)(2,1)}, u32[]{:S(2)}, u32[]{:S(2)}) collective-permute-start(bf16[128,2048]{1,0:T(8,128)(2,1)} %get-tuple-element.119), channel_id=1, source_target_pairs={{0,8},{8,0},{16,24},{24,16},{1,9},{9,1},{17,25},{25,17},{2,10},{10... | collective-permute-start | bytes 1572872 | tf_op jit(solution)/shard_map/ppermute | solution.py:17
  642.1 52.1 %collective-permute-start.47 = (bf16[128,2048]{1,0:T(8,128)(2,1)}, bf16[128,2048]{1,0:T(8,128)(2,1)}, u32[]{:S(2)}, u32[]{:S(2)}) collective-permute-start(bf16[128,2048]{1,0:T(8,128)(2,1)} %slice.618), channel_id=1, source_target_pairs={{0,8},{8,0},{16,24},{24,16},{1,9},{9,1},{17,25},{25,17},{2,10},{10... | collective-permute-start | bytes 1572872 | tf_op jit(solution)/shard_map/ppermute | solution.py:17
  646.8 48.1 %collective-permute-start.52 = (bf16[128,2048]{1,0:T(8,128)(2,1)}, bf16[128,2048]{1,0:T(8,128)(2,1)}, u32[]{:S(2)}, u32[]{:S(2)}) collective-permute-start(bf16[128,2048]{1,0:T(8,128)(2,1)} %slice.626), channel_id=1, source_target_pairs={{0,16},{8,24},{16,0},{24,8},{1,17},{9,25},{17,1},{25,9},{2,18},{10... | collective-permute-start | bytes 1572872 | tf_op jit(solution)/shard_map/ppermute | solution.py:17
  692.7 33.2 %collective-permute-start.74 = (bf16[256,640]{1,0:T(8,128)(2,1)S(1)}, bf16[256,640]{1,0:T(8,128)(2,1)S(1)}, u32[]{:S(2)}, u32[]{:S(2)}) collective-permute-start(bf16[256,640]{1,0:T(8,128)(2,1)S(1)} %slice.659), channel_id=1, source_target_pairs={{0,8},{8,0},{16,24},{24,16},{1,9},{9,1},{17,25},{25,17},{2,10},{10... | collective-permute-start | bytes 983048 | tf_op jit(solution)/shard_map/ppermute | solution.py:17
  694.2 31.7 %collective-permute-start.73 = (bf16[256,640]{1,0:T(8,128)(2,1)S(1)}, bf16[256,640]{1,0:T(8,128)(2,1)S(1)}, u32[]{:S(2)}, u32[]{:S(2)}) collective-permute-start(bf16[256,640]{1,0:T(8,128)(2,1)S(1)} %slice.658), channel_id=1, source_target_pairs={{0,16},{8,24},{16,0},{24,8},{1,17},{9,25},{17,1},{25,9},{2,18},{10... | collective-permute-start | bytes 983048 | tf_op jit(solution)/shard_map/ppermute | solution.py:17
  765.2 102.2 %collective-permute-start.62 = (bf16[128,768]{1,0:T(8,128)(2,1)}, bf16[128,768]{1,0:T(8,128)(2,1)S(1)}, u32[]{:S(2)}, u32[]{:S(2)}) collective-permute-start(bf16[128,768]{1,0:T(8,128)(2,1)} %slice.639), channel_id=1, source_target_pairs={{0,16},{8,24},{16,0},{24,8},{1,17},{9,25},{17,1},{25,9},{2,18},{10... | collective-permute-start | bytes 589832 | tf_op jit(solution)/shard_map/ppermute | solution.py:17
  765.9 104.5 %collective-permute-start.63 = (bf16[128,768]{1,0:T(8,128)(2,1)}, bf16[128,768]{1,0:T(8,128)(2,1)S(1)}, u32[]{:S(2)}, u32[]{:S(2)}) collective-permute-start(bf16[128,768]{1,0:T(8,128)(2,1)} %slice.640), channel_id=1, source_target_pairs={{0,8},{8,0},{16,24},{24,16},{1,9},{9,1},{17,25},{25,17},{2,10},{10... | collective-permute-start | bytes 589832 | tf_op jit(solution)/shard_map/ppermute | solution.py:17
  775.3 96.7 %collective-permute-start.87 = (bf16[192,2048]{1,0:T(8,128)(2,1)}, bf16[192,2048]{1,0:T(8,128)(2,1)S(1)}, u32[]{:S(2)}, u32[]{:S(2)}) collective-permute-start(bf16[192,2048]{1,0:T(8,128)(2,1)} %reduce-scatter.14.cloned.1.call-done), channel_id=1, source_target_pairs={{0,16},{8,24},{16,0},{24,8},{1,17},{9,25},{17,1},{25,9},{2,18},{10... | collective-permute-start | bytes 2359304 | tf_op jit(solution)/shard_map/ppermute | solution.py:17
  775.5 97.1 %collective-permute-start.86 = (bf16[192,2048]{1,0:T(8,128)(2,1)}, bf16[192,2048]{1,0:T(8,128)(2,1)S(1)}, u32[]{:S(2)}, u32[]{:S(2)}) collective-permute-start(bf16[192,2048]{1,0:T(8,128)(2,1)} %reduce-scatter.14.cloned.1.call-done), channel_id=1, source_target_pairs={{0,8},{8,0},{16,24},{24,16},{1,9},{9,1},{17,25},{25,17},{2,10},{10... | collective-permute-start | bytes 2359304 | tf_op jit(solution)/shard_map/ppermute | solution.py:17
  865.9 44.5 %collective-permute-start.83 = (bf16[256,3072]{1,0:T(8,128)(2,1)}, bf16[256,3072]{1,0:T(8,128)(2,1)S(1)}, u32[]{:S(2)}, u32[]{:S(2)}) collective-permute-start(bf16[256,3072]{1,0:T(8,128)(2,1)} %reduce-scatter.12.cloned.1.call-done), channel_id=1, source_target_pairs={{0,16},{8,24},{16,0},{24,8},{1,17},{9,25},{17,1},{25,9},{2,18},{10... | collective-permute-start | bytes 4718600 | tf_op jit(solution)/shard_map/ppermute | solution.py:17
  867.4 44.7 %collective-permute-start.82 = (bf16[256,3072]{1,0:T(8,128)(2,1)}, bf16[256,3072]{1,0:T(8,128)(2,1)S(1)}, u32[]{:S(2)}, u32[]{:S(2)}) collective-permute-start(bf16[256,3072]{1,0:T(8,128)(2,1)} %reduce-scatter.12.cloned.1.call-done), channel_id=1, source_target_pairs={{0,8},{8,0},{16,24},{24,16},{1,9},{9,1},{17,25},{25,17},{2,10},{10... | collective-permute-start | bytes 4718600 | tf_op jit(solution)/shard_map/ppermute | solution.py:17
  872.1 38.3 %collective-permute-start.89 = (bf16[96,2048]{1,0:T(8,128)(2,1)S(1)}, bf16[96,2048]{1,0:T(8,128)(2,1)S(1)}, u32[]{:S(2)}, u32[]{:S(2)}) collective-permute-start(bf16[96,2048]{1,0:T(8,128)(2,1)S(1)} %slice.677), channel_id=1, source_target_pairs={{0,8},{8,0},{16,24},{24,16},{1,9},{9,1},{17,25},{25,17},{2,10},{10... | collective-permute-start | bytes 1179656 | tf_op jit(solution)/shard_map/ppermute | solution.py:17
  872.7 37.7 %collective-permute-start.88 = (bf16[96,2048]{1,0:T(8,128)(2,1)S(1)}, bf16[96,2048]{1,0:T(8,128)(2,1)S(1)}, u32[]{:S(2)}, u32[]{:S(2)}) collective-permute-start(bf16[96,2048]{1,0:T(8,128)(2,1)S(1)} %slice.676), channel_id=1, source_target_pairs={{0,16},{8,24},{16,0},{24,8},{1,17},{9,25},{17,1},{25,9},{2,18},{10... | collective-permute-start | bytes 1179656 | tf_op jit(solution)/shard_map/ppermute | solution.py:17
  (124 other events, 1612.1 us)
Sparse Core Ops, SparseCore 0:
  10.2 36.5 all-gather.9
  49.1 37.2 all-gather.5
  88.0 32.7 all-gather.7
  122.9 64.2 all-gather.13
  189.2 116.8 all-gather.11
  484.2 55.4 all-reduce.2
  542.6 36.4 reduce-scatter.7
  581.4 36.4 reduce-scatter.9
  620.1 43.4 reduce-scatter.5
  666.3 69.0 reduce-scatter.13
  738.3 127.5 reduce-scatter.11

commit v2 on v1

--- a/solution.py
+++ b/solution.py
@@ -24,19 +24,22 @@
     )
 
 
-def gather_seq(block):
+def gather_seq(block, hop=None):
     half = block.shape[0] // 2
-    first = swap(block, 1)
-    second = swap(block, 2)
+    first, second = (swap(block, 1), swap(block, 2)) if hop is None else hop
     third = jnp.concatenate([swap(first[:half], 2), swap(second[half:], 1)], 0)
     return [block, first, second, third]
 
 
-def scatter_seq(parts):
+def first_hop(third):
+    half = third.shape[0] // 2
+    return swap(third[:half], 1), swap(third[half:], 2)
+
+
+def scatter_seq(parts, hop=None):
     half = parts[0].shape[0] // 2
     own, first, second, third = parts
-    top = swap(third[:half], 1)
-    bottom = swap(third[half:], 2)
+    top, bottom = first_hop(third) if hop is None else hop
     first_top = swap(first[:half], 1)
     second_bottom = swap(second[half:], 2)
     second_top = swap((second[:half].astype(f32) + top.astype(f32)).astype(bf16), 2)
@@ -58,6 +61,31 @@
     return lax.psum_scatter(block, "group", scatter_dimension=0, tiled=True)
 
 
+def after(value, *others):
+    return lax.optimization_barrier((value, *others))[0]
+
+
+def total_group(value):
+    count = lax.axis_size("group")
+    place = lax.axis_index("group")
+    route = lambda step: [(i, i ^ step) for i in range(count)]
+    steps = [1 << i for i in range(count.bit_length() - 1)]
+    for step in steps:
+        half = value.shape[0] // 2
+        bit = (place // step) % 2
+        kept = lax.dynamic_slice_in_dim(value, bit * half, half, 0)
+        given = lax.dynamic_slice_in_dim(value, (1 - bit) * half, half, 0)
+        got = lax.ppermute(given, "group", route(step))
+        value = (kept.astype(f32) + got.astype(f32)).astype(value.dtype)
+    for step in reversed(steps):
+        bit = (place // step) % 2
+        got = lax.ppermute(value, "group", route(step))
+        value = jnp.where(
+            bit == 0, jnp.concatenate([value, got], 0), jnp.concatenate([got, value], 0)
+        )
+    return value
+
+
 def total(value):
     for axis in ("group", "seq"):
         count = lax.axis_size(axis)
@@ -75,13 +103,16 @@
 def entering(decay, state, sign):
     count = lax.axis_size("group")
     pair = jnp.stack([decay, state])
-    pair = shift(pair, sign)
-    step = 1
-    while step < count:
-        before = shift(pair, sign * step)
-        pair = jnp.stack(link((before[0], before[1]), (pair[0], pair[1])))
-        step *= 2
-    return pair[1]
+    near = [shift(pair, sign * distance) for distance in range(1, min(4, count - 1) + 1)]
+    decay, state = near[0][0], near[0][1]
+    for before in near[1:]:
+        decay, state = link((before[0], before[1]), (decay, state))
+    covered = len(near)
+    while covered < count - 1:
+        before = shift(jnp.stack([decay, state]), sign * covered)
+        decay, state = link((before[0], before[1]), (decay, state))
+        covered *= 2
+    return state
 
 
 def rms_low(value, gain):
@@ -246,7 +277,7 @@
 
 def backward_kernel(
     head, odd_ref, back_ref, cum_ref, gh_ref, h_ref, carry_ref, enter_ref, recur_ref, input_ref,
-    decay_ref, conv_ref, u_ref, rim_ref, cw_ref, gw_ref, gs_ref, sp_ref,
+    decay_ref, conv_ref, u_ref, gy_ref, rim_ref, cw_ref, gw_ref, gs_ref, sp_ref,
     gu_ref, tail_ref, lead_ref, small_ref, taps_ref, gwg_ref, gsg_ref,
     padded, ahead, behind, low, gg, direct,
 ):
@@ -349,7 +380,8 @@
         for k in range(1, taps):
             out = out + cw_ref[k : k + 1] * pltpu.roll(window, 24 - k, 0)[:16]
             new.append(fold(sums[k + 1], grad * pltpu.roll(inputs, k, 0)[8:]))
-        gu_ref[0, pl.ds(start, 16), :] = out.astype(bf16)
+        gu_ref[0, pl.ds(start, 16), :wide] = out.astype(bf16)
+        gu_ref[0, pl.ds(start, 16), wide:] = gy_ref[0, pl.ds(start, 16), :]
 
         @pl.when(index == tokens // 16 - 1)
         def _():
@@ -372,7 +404,7 @@
 
 def mlp_kernel(normed_ref, weight_ref, grad_ref, hidden_ref, out_ref):
     part = hidden_ref.shape[1]
-    rows = 256
+    rows = 512
 
     def step(index, none):
         span = pl.ds(pl.multiple_of(index * rows, rows), rows)
@@ -388,6 +420,68 @@
     lax.fori_loop(0, normed_ref.shape[0] // rows, step, 0)
 
 
+def spread_mlp_kernel(layout, mine_ref, a_ref, b_ref, c_ref, d_ref, out_ref):
+    parts, per_part, fine = layout
+    blocks = (a_ref, b_ref, c_ref, d_ref)
+    part = per_part * fine
+    span = part * len(blocks)
+    for mine in range(len(blocks)):
+
+        @pl.when(mine_ref[0] == mine)
+        def _(mine=mine):
+            for p in range(parts):
+                for h in range(2):
+                    base = (2 * p + h) * part
+                    wholes = [blocks[k][:, base : base + part].astype(f32) for k in range(len(blocks))]
+                    pieces = [
+                        wholes[mine ^ a][:, g * fine : (g + 1) * fine]
+                        for g in range(per_part)
+                        for a in range(len(blocks))
+                    ]
+                    at = (h * parts + p) * span
+                    out_ref[:, at : at + span] = jnp.concatenate(pieces, 1)
+
+
+def spread_in_kernel(head, mine_ref, a_ref, b_ref, c_ref, d_ref, out_ref):
+    blocks = (a_ref, b_ref, c_ref, d_ref)
+    half = head // 2
+    wide = 3 * head
+    rec = out_ref.shape[1] // 2
+    for mine in range(len(blocks)):
+
+        @pl.when(mine_ref[0] == mine)
+        def _(mine=mine):
+            for k, block in enumerate(blocks):
+                member = mine ^ k
+                first, shared = 5 * (member // 2) + 3 * (member % 2), 5 * (member // 2) + 2
+                at = first * head
+                out_ref[:, at : at + 2 * head] = block[:, : 2 * head].astype(f32)
+                out_ref[:, rec + at : rec + at + 2 * head] = block[:, wide : wide + 2 * head].astype(f32)
+                at = rec + shared * head + (member % 2) * half
+                out_ref[:, at : at + half] = block[:, wide + 2 * head :].astype(f32)
+                if k % 2 == 0:
+                    at = shared * head
+                    out_ref[:, at : at + head] = block[:, 2 * head : wide].astype(f32) + blocks[k + 1][
+                        :, 2 * head : wide
+                    ].astype(f32)
+
+
+def spread(kernel, mine, blocks, columns, name):
+    rows, wide = blocks[0].shape
+    step = min(32, rows)
+    piece = pl.BlockSpec((step, wide), lambda i: (i, 0))
+    return pl.pallas_call(
+        kernel,
+        grid=(rows // step,),
+        in_specs=[SCALAR] + [piece] * len(blocks),
+        out_specs=pl.BlockSpec((step, columns), lambda i: (i, 0)),
+        out_shape=jax.ShapeDtypeStruct((rows, columns), f32),
+        compiler_params=params("arbitrary"),
+        cost_estimate=cost(8),
+        name=name,
+    )(mine.astype(jnp.int32).reshape(1), *blocks)
+
+
 def params(*semantics):
     return pltpu.CompilerParams(dimension_semantics=semantics, vmem_limit_bytes=VMEM_LIMIT)
 
@@ -403,9 +497,9 @@
 SCALAR = pl.BlockSpec(memory_space=pltpu.SMEM)
 
 
-def cost(elements, operations, moved):
+def cost(microseconds):
     return pl.CostEstimate(
-        flops=elements * operations, bytes_accessed=moved, transcendentals=elements * 6
+        flops=int(microseconds * 1e9), bytes_accessed=int(microseconds * 3e6), transcendentals=0
     )
 
 
@@ -462,27 +556,26 @@
             -1,
         )
 
-    in_u = gather_group(widen(in_weight))
-    in_y = gather_group(owned(in_weight, rec))
-    out_piece = model // members
-    out_cols = gather_group(
-        lax.dynamic_slice_in_dim(out_weight, mine * out_piece, out_piece, 1)
-    )
+    in_cols = gather_group(jnp.concatenate([widen(in_weight), owned(in_weight, rec)], 1))
+    in_u, in_y = in_cols[:, :wide], in_cols[:, wide:]
+    x_own = block_input[0]
+    x_blocks = gather_seq(x_own)
+    x_all = jnp.concatenate(x_blocks, 0)
+    c_own = after(out_cotangent[0], x_blocks[1])
+    c_blocks = gather_seq(c_own)
+    c_all = jnp.concatenate(c_blocks, 0)
     fine = hidden // devices // members
-    down_rows = gather_group(lax.dynamic_slice_in_dim(down_weight, mine * fine, fine, 0))
     part = min(384, hidden // members)
     per_part = part // fine
     parts = hidden // members // part
-    cut = mlp_weight.reshape(-1, 2, parts, per_part, members, fine)
+    cut = after(mlp_weight, x_blocks[1]).reshape(-1, 2, parts, per_part, members, fine)
     cut = lax.dynamic_index_in_dim(cut, mine, 4, keepdims=False)
-    mlp_cols = gather_group(cut.transpose(0, 2, 1, 3, 4).reshape(mlp_weight.shape[0], -1))
-
-    x_own = block_input[0]
-    c_own = out_cotangent[0]
-    x_all = jnp.concatenate(gather_seq(x_own), 0)
-    c_all = jnp.concatenate(gather_seq(c_own), 0)
-    normed = rms_low(x_all.astype(f32), norm_gain)
-
+    cut = cut.transpose(0, 2, 1, 3, 4).reshape(mlp_weight.shape[0], -1)
+    normed = after(rms_low(x_all.astype(f32), norm_gain), cut)
+    out_piece = model // members
+    out_cols = gather_group(
+        after(lax.dynamic_slice_in_dim(out_weight, mine * out_piece, out_piece, 1), in_cols, normed)
+    )
     def rows_for(value, k):
         start, common = first_of(mine ^ k)
         return jnp.concatenate(
@@ -503,6 +596,7 @@
         out_rows = lax.dynamic_update_slice_in_dim(out_rows, piece, (mine ^ k) * out_piece, 1)
 
     u = jnp.dot(normed, in_u, preferred_element_type=f32).reshape(members, tokens, wide)
+    u = after(u, c_blocks[1], c_blocks[2])
     y = jnp.dot(normed, in_y, preferred_element_type=f32).reshape(members, tokens, own)
     lead = taps - 1
     rim = jnp.pad(shift(u[:, tokens - lead :], 1), ((0, 0), (8 - lead, 0), (0, 0)))
@@ -539,10 +633,16 @@
             pltpu.VMEM((2, tokens, own), f32),
         ],
         compiler_params=params("arbitrary"),
-        cost_estimate=cost(rows * own, 1100, rows * own * 28),
+        cost_estimate=cost(14),
         name="recurrence_forward",
     )(odd_flag, u, rim, cw, cb, gw, gs, gb, soft)
+    down_rows = gather_group(
+        after(
+            lax.dynamic_slice_in_dim(down_weight, mine * fine, fine, 0), out_cols, decay_cum
+        )
+    )
     carried = entering(decay_cum[:, -1], state_local[:, -1], 1)
+    carried = after(carried, out_rows)
     carried8 = jnp.broadcast_to(carried[:, None], (members, 8, own))
     h, merged = pl.pallas_call(
         merge_kernel,
@@ -551,19 +651,20 @@
         out_specs=[per_seq(tokens, own)] * 2,
         out_shape=[full, jax.ShapeDtypeStruct((members, tokens, own), bf16)],
         compiler_params=params("arbitrary"),
-        cost_estimate=cost(rows * own, 20, rows * own * 18),
+        cost_estimate=cost(14),
         name="recurrence_merge",
     )(state_local, decay_cum, carried8, y)
-    partial = [None] * members
-    for k in (3, 1, 2, 0):
-        partial[k] = jnp.dot(merged[k], out_rows, preferred_element_type=f32).astype(bf16)
+    partial = jnp.dot(merged.reshape(rows, own), out_rows, preferred_element_type=f32)
+    partial = partial.astype(bf16)
+    mlp_cols = gather_group(after(cut, down_rows, merged))
+    partial = lax.optimization_barrier(partial).reshape(members, tokens, model)
     x32 = x_own.astype(f32)
-    resid = x32 + scatter_seq(partial)
-    normed2 = jnp.concatenate(gather_seq(rms_low(resid, mlp_gain)), 0)
-
     grad_hidden = lax.dot_general(
         c_all, down_rows, (((1,), (1,)), ((), ())), preferred_element_type=f32
     )
+    resid = after(x32 + scatter_seq(partial), grad_hidden)
+    normed2 = jnp.concatenate(gather_seq(rms_low(resid, mlp_gain)), 0)
+
     width = parts * part
     hidden_low, grad_gu = pl.pallas_call(
         mlp_kernel,
@@ -589,36 +690,35 @@
         ),
         name="mlp",
     )(normed2, mlp_cols, grad_hidden)
-    partial = [None] * members
-    for k in (3, 1, 2, 0):
-        partial[k] = lax.dot_general(
-            grad_gu[k * tokens : (k + 1) * tokens],
-            mlp_cols,
-            (((1,), (1,)), ((), ())),
-            preferred_element_type=f32,
-        ).astype(bf16)
-    grad_normed2 = scatter_seq(partial)
+    across = (((1,), (1,)), ((), ()))
+    down = (((0,), (0,)), ((), ()))
+    down_part = lax.dot_general(hidden_low, c_all, down, preferred_element_type=f32).astype(bf16)
+    down_sum = scatter_group(down_part)
+    partial = lax.dot_general(
+        after(grad_gu, down_part), mlp_cols, across, preferred_element_type=f32
+    ).astype(bf16)
+    mlp_part = lax.dot_general(
+        normed2, after(grad_gu, partial), down, preferred_element_type=f32
+    ).astype(bf16)
+    grad_normed2 = scatter_seq(lax.optimization_barrier(partial).reshape(members, tokens, model))
+    final = jnp.dot(
+        after(hidden_low, mlp_part), down_rows, preferred_element_type=f32
+    ).astype(bf16)
+    grad_normed2 = after(grad_normed2, final)
     grad_resid_norm, mlp_gain_grad = rms_back(resid, mlp_gain, grad_normed2)
     grad_resid = c_own.astype(f32) + grad_resid_norm
     grad_resid_all = jnp.concatenate(gather_seq(grad_resid.astype(bf16)), 0)
-
-    down = (((0,), (0,)), ((), ()))
-    down_sum = scatter_group(
-        lax.dot_general(hidden_low, c_all, down, preferred_element_type=f32).astype(bf16)
-    )
-    mlp_sum = scatter_group(
-        lax.dot_general(normed2, grad_gu, down, preferred_element_type=f32).astype(bf16)
-    )
-    partial = [None] * members
-    for k in (3, 1, 2, 0):
-        partial[k] = jnp.dot(
-            hidden_low[k * tokens : (k + 1) * tokens], down_rows, preferred_element_type=f32
-        ).astype(bf16)
-    block_out = (resid + scatter_seq(partial)).astype(bf16)[None]
-
+    mlp_sum = scatter_group(after(mlp_part, down_sum, grad_normed2))
+
+    final = after(final, grad_resid_all).reshape(members, tokens, model)
+    final_hop = first_hop(final[3])
+    block_out = (resid + scatter_seq(final, final_hop)).astype(bf16)[None]
     grad_merged = lax.dot_general(
         grad_resid_all, out_rows, (((1,), (1,)), ((), ())), preferred_element_type=f32
     ).reshape(members, tokens, own)
+    grad_merged = after(grad_merged, *final_hop)
+    down_first = after(down_sum, *final_hop)
+    down_hop = swap(down_first, 1), swap(down_first, 2)
     grad_h, grad_y, back_local, back_cum = pl.pallas_call(
         adjoint_kernel,
         grid=(members,),
@@ -626,12 +726,12 @@
         out_specs=[per_seq(tokens, own)] * 4,
         out_shape=[full, jax.ShapeDtypeStruct((members, tokens, own), bf16), full, full],
         compiler_params=params("arbitrary"),
-        cost_estimate=cost(rows * own, 50, rows * own * 30),
+        cost_estimate=cost(10),
         name="recurrence_adjoint",
     )(grad_merged, h, y, decay)
     incoming = entering(back_cum[:, 0], back_local[:, 0], -1)
     incoming8 = jnp.broadcast_to(incoming[:, None], (members, 8, own))
-    grad_u, tail, owed, small, tap_sums, gw_grad, gs_grad = pl.pallas_call(
+    grad_proj, tail, owed, small, tap_sums, gw_grad, gs_grad = pl.pallas_call(
         functools.partial(backward_kernel, head),
         grid=(members,),
         in_specs=[
@@ -641,6 +741,7 @@
             per_seq(8, own),
             *[per_seq(tokens, own)] * 3,
             *[per_seq(tokens, wide)] * 2,
+            per_seq(tokens, own),
             per_seq(8, wide),
             whole(taps, wide),
             whole(2, 2, head, head),
@@ -648,7 +749,7 @@
             whole(1, own),
         ],
         out_specs=[
-            per_seq(tokens, wide),
+            per_seq(tokens, wide + own),
             per_seq(8, wide),
             per_seq(8, wide),
             whole(8, own),
@@ -657,7 +758,7 @@
             whole(2, head, half),
         ],
         out_shape=[
-            jax.ShapeDtypeStruct((members, tokens, wide), bf16),
+            jax.ShapeDtypeStruct((members, tokens, wide + own), bf16),
             jax.ShapeDtypeStruct((members, 8, wide), f32),
             jax.ShapeDtypeStruct((members, 8, wide), f32),
             jax.ShapeDtypeStruct((8, own), f32),
@@ -674,33 +775,15 @@
             pltpu.VMEM((tokens + 8, wide), f32),
         ],
         compiler_params=params("arbitrary"),
-        cost_estimate=cost(rows * own, 2200, rows * own * 36),
+        cost_estimate=cost(19),
         name="recurrence_backward",
     )(
         odd_flag, back_local, back_cum, grad_h, h, carried8, incoming8, recur, gate,
-        decay, conv, u, rim, cw, gw, gs, soft,
+        decay, conv, u, grad_y, rim, cw, gw, gs, soft,
     )
     tail = (tail + shift(owed, -1)).astype(bf16)
-    grad_u = lax.dynamic_update_slice(grad_u, tail, (0, tokens - 8, 0))
-    flat_u = grad_u.reshape(rows, wide)
-    flat_y = grad_y.reshape(rows, own)
-    partial = [None] * members
-    across = (((1,), (1,)), ((), ()))
-    for k in (3, 1, 2, 0):
-        partial[k] = (
-            lax.dot_general(grad_u[k], in_u, across, preferred_element_type=f32)
-            + lax.dot_general(grad_y[k], in_y, across, preferred_element_type=f32)
-        ).astype(bf16)
-    grad_normed = scatter_seq(partial)
-    grad_input_norm, norm_gain_grad = rms_back(x32, norm_gain, grad_normed)
-    input_grad = (grad_resid + grad_input_norm)[None]
-
-    y_sum = scatter_group(
-        lax.dot_general(normed, flat_y, down, preferred_element_type=f32).astype(bf16)
-    )
-    u_sum = scatter_group(
-        lax.dot_general(normed, flat_u, down, preferred_element_type=f32).astype(bf16)
-    )
+    grad_proj = lax.dynamic_update_slice(grad_proj, tail, (0, tokens - 8, 0))
+    grad_proj = grad_proj.reshape(rows, wide + own)
     out_part = lax.dot_general(
         merged.reshape(rows, own), grad_resid_all, down, preferred_element_type=f32
     ).astype(bf16)
@@ -716,53 +799,58 @@
         out_terms = lax.dynamic_update_slice_in_dim(
             out_terms, piece[2 * head :], common * head + ((mine ^ k) % 2) * half, 0
         )
-    out_sum = scatter_group(out_terms)
-
-    down_parts = jnp.stack(gather_seq(down_sum))
+    gate_terms = jnp.concatenate([gw_grad[:, 0], gw_grad[:, 1], gs_grad], -1).reshape(-1, own)
+    decay_terms = small[2:3] * (-8.0) * owned(jax.nn.sigmoid(decay_param))[None]
+    sizes = ((taps + 1) * wide, 3 * own, model)
+    small_terms = jnp.concatenate(
+        [
+            tap_sums[: taps + 1].reshape(-1),
+            small[:2].reshape(-1),
+            decay_terms.reshape(-1),
+            mlp_gain_grad,
+        ]
+    )
+    small_rows = 64
+    small_terms = jnp.pad(small_terms, (0, small_rows * own - small_terms.shape[0]))
+    terms = jnp.concatenate([gate_terms, small_terms.reshape(small_rows, own)], 0).astype(bf16)
+    group_terms = total_group(terms)
+    partial = lax.dot_general(
+        after(grad_proj, out_terms, *down_hop, group_terms), in_cols, across, preferred_element_type=f32
+    )
+    partial = lax.optimization_barrier(partial.astype(bf16)).reshape(members, tokens, model)
+    hop = first_hop(partial[3])
+    out_sum = scatter_group(after(out_terms, mlp_sum, grad_proj))
+    in_part = lax.dot_general(normed, grad_proj, down, preferred_element_type=f32).astype(bf16)
+    in_sum = scatter_group(after(in_part, out_sum, *hop))
+
+    out_blocks = gather_seq(out_sum)
+    grad_normed = scatter_seq(partial, (after(hop[0], out_sum), after(hop[1], out_sum)))
+    mlp_late = after(mlp_sum, out_sum)
+    mlp_hop = swap(mlp_late, 1), swap(mlp_late, 2)
+    term_parts = gather_seq(after(group_terms, *hop))
+    gate_parts = [after(piece[: 2 * head], in_sum) for piece in term_parts]
+    small_parts = jnp.stack([piece[2 * head :].reshape(-1) for piece in term_parts])
+    grad_input_norm, norm_gain_grad = rms_back(x32, norm_gain, grad_normed)
+    input_grad = (grad_resid + grad_input_norm)[None]
+
+    mlp_blocks = gather_seq(mlp_late, mlp_hop)
+    mlp_grad = spread(
+        functools.partial(spread_mlp_kernel, (parts, per_part, fine)),
+        mine,
+        mlp_blocks,
+        2 * hidden,
+        "spread_mlp",
+    )
+    out_parts = jnp.stack(out_blocks)
+    out_grad = jnp.concatenate(
+        [lax.dynamic_index_in_dim(out_parts, mine ^ a, 0, keepdims=False) for a in range(members)],
+        1,
+    ).astype(f32)
+    down_parts = jnp.stack(gather_seq(down_sum, down_hop))
     down_grad = jnp.concatenate(
         [lax.dynamic_index_in_dim(down_parts, mine ^ a, 0, keepdims=False) for a in range(members)],
         0,
     ).astype(f32)
-    mlp_parts = jnp.stack(gather_seq(mlp_sum))
-    mlp_grad = jnp.stack(
-        [
-            lax.dynamic_index_in_dim(mlp_parts, mine ^ a, 0, keepdims=False).reshape(
-                -1, parts, 2, per_part, fine
-            )
-            for a in range(members)
-        ],
-        4,
-    )
-    mlp_grad = mlp_grad.transpose(0, 2, 1, 3, 4, 5).reshape(-1, 2 * hidden).astype(f32)
-    out_parts = jnp.stack(gather_seq(out_sum))
-    out_grad = jnp.concatenate(
-        [lax.dynamic_index_in_dim(out_parts, mine ^ a, 0, keepdims=False) for a in range(members)],
-        1,
-    ).astype(f32)
-    u_parts = gather_seq(u_sum)
-    y_parts = gather_seq(y_sum)
-    in_grad = jnp.zeros((u_sum.shape[0], 2 * rec), f32)
-    for k in range(members):
-        start, common = first_of(mine ^ k)
-        in_grad = lax.dynamic_update_slice_in_dim(
-            in_grad, u_parts[k][:, : 2 * head].astype(f32), start * head, 1
-        )
-        in_grad = lax.dynamic_update_slice_in_dim(
-            in_grad, y_parts[k][:, : 2 * head].astype(f32), rec + start * head, 1
-        )
-        in_grad = lax.dynamic_update_slice_in_dim(
-            in_grad,
-            y_parts[k][:, 2 * head :].astype(f32),
-            rec + common * head + ((mine ^ k) % 2) * half,
-            1,
-        )
-        if k % 2 == 0:
-            both = u_parts[k][:, 2 * head :].astype(f32) + u_parts[k + 1][:, 2 * head :].astype(f32)
-            in_grad = lax.dynamic_update_slice_in_dim(in_grad, both, common * head, 1)
-
-    gate_terms = jnp.concatenate([gw_grad[:, 0], gw_grad[:, 1], gs_grad], -1).astype(bf16)
-    gate_sum = lax.psum(gate_terms, "group")
-    gate_parts = gather_seq(gate_sum.reshape(2 * head, own))
     gate_grad = jnp.zeros((2, heads, head, head), f32)
     for k in range(members):
         start, common = first_of(mine ^ k)
@@ -778,32 +866,37 @@
             )
             gate_grad = lax.dynamic_update_slice_in_dim(gate_grad, halves[:, None], common, 1)
 
-    def place(value, wide_shared):
+    def place(value, member, wide_shared):
+        start, common = first_of(member)
+        at = common * head if wide_shared else common * head + (member % 2) * half
         out = jnp.zeros((value.shape[0], rec), f32)
-        out = lax.dynamic_update_slice_in_dim(out, value[:, : 2 * head], first * head, 1)
-        at = shared * head if wide_shared else shared * head + odd * half
+        out = lax.dynamic_update_slice_in_dim(out, value[:, : 2 * head], start * head, 1)
         return lax.dynamic_update_slice_in_dim(out, value[:, 2 * head :], at, 1)
 
-    decay_terms = small[2:3] * (-8.0) * owned(jax.nn.sigmoid(decay_param))[None]
-    channel = jnp.concatenate(
-        [place(tap_sums[: taps + 1], True), place(jnp.concatenate([small[:2], decay_terms], 0), False)],
-        0,
-    )
-    packed = jnp.concatenate([channel.reshape(-1, 128), mlp_gain_grad.reshape(-1, 128)], 0)
-    packed = total(packed)
-    channel = packed[: (taps + 4) * rec // 128].reshape(taps + 4, rec)
-    mlp_gain_grad = packed[(taps + 4) * rec // 128 :].reshape(-1)
+    tap_grads, own_grads, mlp_gain_grad = 0.0, 0.0, 0.0
+    for member in range(members):
+        piece = lax.dynamic_index_in_dim(small_parts, mine ^ member, 0, keepdims=False).astype(f32)
+        one, two, three, _ = jnp.split(
+            piece, (sizes[0], sizes[0] + sizes[1], sizes[0] + sizes[1] + sizes[2])
+        )
+        tap_grads = tap_grads + place(one.reshape(-1, wide), member, True)
+        own_grads = own_grads + place(two.reshape(-1, own), member, False)
+        mlp_gain_grad = mlp_gain_grad + three
     norm_gain_grad = total(norm_gain_grad.reshape(-1, 128)).reshape(-1)
+    in_grad = spread(
+        functools.partial(spread_in_kernel, head), mine, gather_seq(after(in_sum, *mlp_hop, *out_blocks, *term_parts)), 2 * rec, "spread_in"
+    )
+
     return (
         block_out,
         input_grad,
         norm_gain_grad,
         in_grad,
-        channel[1 : taps + 1],
-        channel[0],
+        tap_grads[1:],
+        tap_grads[0],
         gate_grad,
-        channel[taps + 1 : taps + 3],
-        channel[taps + 3],
+        own_grads[:2],
+        own_grads[2],
         out_grad,
         mlp_gain_grad,
         mlp_grad,

time: 987 us -> 819 us (0.83)
  waiting for transfers between devices: 434 us -> 293 us
  matrix products: 147 us -> 114 us
  Pallas kernels: 72.6 us -> 87.7 us
  starting transfers between devices: 120 us -> 107 us
    reduce_scatter x5 -> x4, waiting for transfers between devices: 88.4 us -> 0.06 us  [scatter_group(): return lax.psum_scatter(block, 'group', scatter_dimension=0, tiled=True)]
    ppermute x70 -> x66, waiting for transfers between devices: 285 us -> 235 us  [swap(): lax.ppermute(block, 'seq', [(i, i ^ k) for i in range(lax.axis_size('seq'...]
    dot_general x23 -> x6, matrix products: 98.9 us -> 73.4 us  [the longest x1 19.5 us: shards(): lax.dot_general(normed2, after(grad_gu, partial), down, preferred_element...]
    pallas_call x0 -> x2, Pallas kernels: none -> 16.9 us  [spread(): pl.pallas_call(kernel, grid=(rows // step,), in_specs=[SCALAR] + [piece]...]
    dynamic_update_slice x17 -> x1, other arithmetic: 15.2 us -> 0.63 us  [shards(): grad_proj = lax.dynamic_update_slice(grad_proj, tail, (0, tokens - 8, 0))]
    unnamed x130 -> x152, local copies, waits for them, and re-layouts: 36.4 us -> 22.4 us
    ppermute x0 -> x6, waiting for transfers between devices: none -> 10.4 us  [the longest x3 8.24 us: total_group(): got = lax.ppermute(given, 'group', route(step))]
    optimization_barrier x0 -> x2, local copies, waits for them, and re-layouts: none -> 10.4 us  [after(): return lax.optimization_barrier((value, *others))[0]]
  transfers between devices with their start and end apart: 101 -> 97, of which waited for: 54 -> 44; matrix products, arithmetic and copies ran while one was open for 27% -> 35% of each run, Pallas kernels for 2% -> 7%
where the time goes in v2:
time: 819 us; the launch traced here: 807 us
  waiting for transfers between devices  293 us (36%)
  local copies, waits for them, and re-layouts  121 us (15%)
  matrix products  114 us (14%)
  starting transfers between devices  107 us (13%)
  Pallas kernels  87.7 us (11%)
  other arithmetic  67.1 us (8%)
  between operations  16.6 us (2%)
    ppermute x66, waiting for transfers between devices, swap(): lax.ppermute(block, 'seq', [(i, i ^ k) for i in range(lax.axis_size('seq'...  235 us
    ppermute x66, starting transfers between devices, swap(): lax.ppermute(block, 'seq', [(i, i ^ k) for i in range(lax.axis_size('seq'...  72.5 us
    ppermute x12, starting transfers between devices, shift(): lax.ppermute(block, 'group', [(i - distance, i) for i in devices if i - d...  25.3 us
    unnamed x152, local copies, waits for them, and re-layouts  22.4 us
    pallas_call x1, Pallas kernels, shards(): pl.pallas_call(mlp_kernel, grid=(parts,), in_specs=[whole(rows, model), p...  21.2 us
    ppermute x5, waiting for transfers between devices, total(): lax.ppermute(value, axis, [(i, i ^ step) for i in range(count)])  19.5 us
    dot_general x1, matrix products, shards(): lax.dot_general(normed2, after(grad_gu, partial), down, preferred_element...  19.5 us
    pallas_call x1, Pallas kernels, shards(): pl.pallas_call(functools.partial(backward_kernel, head), grid=(members,),...  18.6 us
  transfers between devices with their start and end apart: 97, of which 44 were waited for; matrix products, arithmetic and copies ran while one was open for 35% of the time, Pallas kernels for 7%

profile of v2, /device:TPU:0, one launch (start us, length us, event | category | flops | bytes accessed | tf_op | source)
XLA Modules:
  0.0 807.0 jit_solution(11285603067423113915)
XLA Ops:
  19.8 17.9 %collective-permute-done = bf16[256,2048]{1,0:T(8,128)(2,1)} collective-permute-done((bf16[256,2048]{1,0:T(8,128)(2,1)}, bf16[256,2048]{1,0:T(8,128)(2,1)}, u32[]{:S(2)}, u32[]{:S(2)}) %collective-permute-start) | collective-permute-done | bytes 1048608 | tf_op jit(solution)/shard_map/ppermute | solution.py:17
  47.1 8.7 %copy.38 = bf16[256,12288]{0,1:T(8,128)(2,1)} copy(bf16[256,12288]{1,0:T(8,128)(2,1)} %param.24) | data formatting | bytes 12582912 | tf_op jit(solution)/shard_map/optimization_barrier | solution.py:65
  94.4 14.4 %collective-permute-done.4 = bf16[256,2048]{1,0:T(8,128)(2,1)S(1)} collective-permute-done((bf16[256,2048]{1,0:T(8,128)(2,1)}, bf16[256,2048]{1,0:T(8,128)(2,1)S(1)}, u32[]{:S(2)}, u32[]{:S(2)}) %collective-permute-start.4) | collective-permute-done | bytes 1048608 | tf_op jit(solution)/shard_map/ppermute | solution.py:17
  113.2 14.3 %recurrence_forward.1 = (f32[4,256,768]{2,1,0:T(8,128)}, f32[4,256,640]{2,1,0:T(8,128)}, f32[4,256,640]{2,1,0:T(8,128)}, f32[4,256,640]{2,1,0:T(8,128)}, f32[4,256,640]{2,1,0:T(8,128)}, /*index=5*/f32[4,256,640]{2,1,0:T(8,128)}) custom-call(s32[1]{0:T(128)} %bitcast.1.odd_ref, f32[4,256,768]{2,1,0:T(8,128)} %bitcast.209, f32[4,8,768]{2,1,0:T(8,128)} %pad.17.rim_ref, ...), custom_call_target="tpu_custom_call" | custom-call | flops 14000000000 | bytes 42000000 | tf_op jit(solution)/shard_map/recurrence_forward/pallas_call | solution.py:614
  160.7 20.8 %collective-permute-done.12 = bf16[640,512]{1,0:T(8,128)(2,1)S(1)} collective-permute-done((bf16[640,512]{1,0:T(8,128)(2,1)S(1)}, bf16[640,512]{1,0:T(8,128)(2,1)S(1)}, u32[]{:S(2)}, u32[]{:S(2)}) %collective-permute-start.12) | collective-permute-done | bytes 655392 | tf_op jit(solution)/shard_map/ppermute | solution.py:17
  204.4 11.3 %collective-permute-done.16 = bf16[128,2048]{1,0:T(8,128)(2,1)S(1)} collective-permute-done((bf16[128,2048]{1,0:T(8,128)(2,1)S(1)}, bf16[128,2048]{1,0:T(8,128)(2,1)S(1)}, u32[]{:S(2)}, u32[]{:S(2)}) %collective-permute-start.16) | collective-permute-done | bytes 524320 | tf_op jit(solution)/shard_map/ppermute | solution.py:17
  219.7 7.2 collective-permute-done.15
  232.7 9.2 %collective-permute-done.21 = bf16[128,2048]{1,0:T(8,128)(2,1)S(1)} collective-permute-done((bf16[128,2048]{1,0:T(8,128)(2,1)S(1)}, bf16[128,2048]{1,0:T(8,128)(2,1)S(1)}, u32[]{:S(2)}, u32[]{:S(2)}) %collective-permute-start.21) | collective-permute-done | bytes 524320 | tf_op jit(solution)/shard_map/ppermute | solution.py:17
  242.1 8.8 %collective-permute-done.20 = bf16[128,2048]{1,0:T(8,128)(2,1)S(1)} collective-permute-done((bf16[128,2048]{1,0:T(8,128)(2,1)S(1)}, bf16[128,2048]{1,0:T(8,128)(2,1)S(1)}, u32[]{:S(2)}, u32[]{:S(2)}) %collective-permute-start.20) | collective-permute-done | bytes 524320 | tf_op jit(solution)/shard_map/ppermute | solution.py:17
  251.6 8.6 %fusion.52.grad_ref = f32[1024,1536]{1,0:T(8,128)} fusion(bf16[1024,2048]{1,0:T(8,128)(2,1)S(1)} %constant_dynamic-update-slice_fusion.5, bf16[1536,2048]{1,0:T(8,128)(2,1)S(1)} %bitcast.212), kind=kOutput, calls=%fused_computation.261 | convolution fusion | flops 6442450944 | bytes 16777216 | tf_op jit(solution)/shard_map/dot_general | solution.py:662
  264.7 20.0 %collective-permute-done.23 = bf16[256,2048]{1,0:T(8,128)(2,1)S(1)} collective-permute-done((bf16[256,2048]{1,0:T(8,128)(2,1)S(1)}, bf16[256,2048]{1,0:T(8,128)(2,1)S(1)}, u32[]{:S(2)}, u32[]{:S(2)}) %collective-permute-start.23) | collective-permute-done | bytes 1048608 | tf_op jit(solution)/shard_map/ppermute | solution.py:17
  290.1 7.1 collective-permute-done.25
  298.9 13.4 %all-gather.11.cloned.1.call-done.weight_ref = bf16[2048,3072]{1,0:T(8,128)(2,1)} async-done(((bf16[256,3072]{1,0:T(8,128)(2,1)}), bf16[2048,3072]{1,0:T(8,128)(2,1)}) %all-gather.11.cloned.1.call-update) | async-done | bytes 12582928 | tf_op jit(solution)/shard_map/all_gather | solution.py:57
  312.3 21.2 %mlp.1 = (bf16[1024,1536]{1,0:T(8,128)(2,1)}, bf16[1024,3072]{1,0:T(8,128)(2,1)}) custom-call(bf16[1024,2048]{1,0:T(8,128)(2,1)} %constant_dynamic-update-slice_fusion.10.normed_ref, bf16[2048,3072]{1,0:T(8,128)(2,1)} %all-gather.11.cloned.1.call-done.weight_ref, f32[1024,1536]{1,0:T(8,128)} %fusion.52.grad_ref), custom_call_target="tpu_custom_call" | custom-call | flops 12884901888 | bytes 32505856 | tf_op jit(solution)/shard_map/mlp/pallas_call | solution.py:669
  333.6 11.3 %convolution_convert_fusion.2 = bf16[1536,2048]{1,0:T(8,128)(2,1)} fusion(bf16[1024,1536]{1,0:T(8,128)(2,1)} %get-tuple-element.79, bf16[1024,2048]{1,0:T(8,128)(2,1)} %copy-done.36), kind=kOutput, calls=%fused_computation.7 | convolution fusion | flops 6445596672 | bytes 13631488 | tf_op jit(solution)/shard_map/dot_general | solution.py:695
  344.9 18.0 %convolution_convert_fusion.3 = bf16[1024,2048]{1,0:T(8,128)(2,1)S(1)} fusion(bf16[1024,3072]{1,0:T(8,128)(2,1)} %get-tuple-element.78, bf16[2048,3072]{1,0:T(8,128)(2,1)} %all-gather.11.cloned.1.call-done.weight_ref), kind=kOutput, calls=%fused_computation.13 | convolution fusion | flops 12886999040 | bytes 23068672 | tf_op jit(solution)/shard_map/dot_general | solution.py:697
  367.7 11.3 %collective-permute-done.28 = bf16[128,2048]{1,0:T(8,128)(2,1)S(1)} collective-permute-done((bf16[128,2048]{1,0:T(8,128)(2,1)S(1)}, bf16[128,2048]{1,0:T(8,128)(2,1)S(1)}, u32[]{:S(2)}, u32[]{:S(2)}) %collective-permute-start.28) | collective-permute-done | bytes 524320 | tf_op jit(solution)/shard_map/ppermute | solution.py:17
  380.6 19.5 %convolution_convert_fusion = bf16[2048,3072]{1,0:T(8,128)(2,1)} fusion(bf16[1024,2048]{1,0:T(8,128)(2,1)} %constant_dynamic-update-slice_fusion.10.normed_ref, bf16[1024,3072]{1,0:T(8,128)(2,1)} %get-tuple-element.78), kind=kOutput, calls=%fused_computation | convolution fusion | flops 12891193344 | bytes 23068672 | tf_op jit(solution)/shard_map/dot_general | solution.py:700
  404.6 11.4 %convolution_convert_fusion.4 = bf16[1024,2048]{1,0:T(8,128)(2,1)} fusion(bf16[1024,1536]{1,0:T(8,128)(2,1)S(1)} %copy-done.60, bf16[1536,2048]{1,0:T(8,128)(2,1)} %all-gather.9.cloned.1.call-done), kind=kOutput, calls=%fused_computation.14 | convolution fusion | flops 6444548096 | bytes 13631488 | tf_op jit(solution)/shard_map/dot_general | solution.py:704
  426.7 19.7 %collective-permute-done.33 = bf16[256,2048]{1,0:T(8,128)(2,1)S(1)} collective-permute-done((bf16[256,2048]{1,0:T(8,128)(2,1)}, bf16[256,2048]{1,0:T(8,128)(2,1)S(1)}, u32[]{:S(2)}, u32[]{:S(2)}) %collective-permute-start.33) | collective-permute-done | bytes 1048608 | tf_op jit(solution)/shard_map/ppermute | solution.py:17
  476.9 10.3 %recurrence_adjoint.1 = (f32[4,256,640]{2,1,0:T(8,128)}, bf16[4,256,640]{2,1,0:T(8,128)(2,1)}, f32[4,256,640]{2,1,0:T(8,128)}, f32[4,256,640]{2,1,0:T(8,128)}) custom-call(f32[4,256,640]{2,1,0:T(8,128)} %bitcast.217, f32[4,256,640]{2,1,0:T(8,128)} %get-tuple-element.83.h_ref, f32[4,256,640]{2,1,0:T(8,128)} %bitcast.216, ...), custom_call_target="tpu_custom_call" | custom-call | flops 10000000000 | bytes 30000000 | tf_op jit(solution)/shard_map/recurrence_adjoint/pallas_call | solution.py:722
  511.3 18.6 %recurrence_backward.1 = (bf16[4,256,1408]{2,1,0:T(8,128)(2,1)}, f32[4,8,768]{2,1,0:T(8,128)}, f32[4,8,768]{2,1,0:T(8,128)}, f32[8,640]{1,0:T(8,128)}, f32[8,768...) custom-call(s32[1]{0:T(128)} %bitcast.1.odd_ref, f32[4,256,640]{2,1,0:T(8,128)} %get-tuple-element.85.back_ref, ...), custom_call_target="tpu_custom_call" | custom-call | flops 19000000512 | bytes 57000000 | tf_op jit(solution)/shard_map/recurrence_backward/pallas_call | solution.py:734
  568.6 10.4 %convolution_convert_fusion.1 = bf16[2048,1408]{1,0:T(8,128)(2,1)} fusion(bf16[1024,2048]{1,0:T(8,128)(2,1)S(1)} %copy-done.16, bf16[1024,1408]{1,0:T(8,128)(2,1)} %bitcast.213), kind=kOutput, calls=%fused_computation.6 | convolution fusion | flops 5908463616 | bytes 12845056 | tf_op jit(solution)/shard_map/dot_general | solution.py:823
  584.4 10.3 %collective-permute-done.52 = bf16[192,2048]{1,0:T(8,128)(2,1)S(1)} collective-permute-done((bf16[192,2048]{1,0:T(8,128)(2,1)}, bf16[192,2048]{1,0:T(8,128)(2,1)S(1)}, u32[]{:S(2)}, u32[]{:S(2)}) %collective-permute-start.52) | collective-permute-done | bytes 786464 | tf_op jit(solution)/shard_map/ppermute | solution.py:17
  597.6 8.7 %convolution_convert_fusion.5 = bf16[1024,2048]{1,0:T(8,128)(2,1)S(1)} fusion(bf16[1024,1408]{1,0:T(8,128)(2,1)S(1)} %bitcast.214, bf16[2048,1408]{1,0:T(8,128)(2,1)} %all-gather.5.cloned.1.call-done), kind=kOutput, calls=%fused_computation.15 | convolution fusion | flops 5907677184 | bytes 12845056 | tf_op jit(solution)/shard_map/dot_general | solution.py:817
  613.7 8.9 %collective-permute-done.61 = bf16[128,2048]{1,0:T(8,128)(2,1)S(1)} collective-permute-done((bf16[128,2048]{1,0:T(8,128)(2,1)S(1)}, bf16[128,2048]{1,0:T(8,128)(2,1)S(1)}, u32[]{:S(2)}, u32[]{:S(2)}) %collective-permute-start.61) | collective-permute-done | bytes 524320 | tf_op jit(solution)/shard_map/ppermute | solution.py:17
  630.3 18.1 %collective-permute-done.78 = bf16[576,640]{1,0:T(8,128)(2,1)S(1)} collective-permute-done((bf16[576,640]{1,0:T(8,128)(2,1)S(1)}, bf16[576,640]{1,0:T(8,128)(2,1)S(1)}, u32[]{:S(2)}, u32[]{:S(2)}) %collective-permute-start.78) | collective-permute-done | bytes 737312 | tf_op jit(solution)/shard_map/ppermute | solution.py:17
  679.8 9.6 %collective-permute-done.62 = bf16[128,2048]{1,0:T(8,128)(2,1)S(1)} collective-permute-done((bf16[128,2048]{1,0:T(8,128)(2,1)S(1)}, bf16[128,2048]{1,0:T(8,128)(2,1)S(1)}, u32[]{:S(2)}, u32[]{:S(2)}) %collective-permute-start.62) | collective-permute-done | bytes 524320 | tf_op jit(solution)/shard_map/ppermute | solution.py:17
  700.2 9.5 %collective-permute-done.76 = bf16[160,512]{1,0:T(8,128)(2,1)S(1)} collective-permute-done((bf16[160,512]{1,0:T(8,128)(2,1)S(1)}, bf16[160,512]{1,0:T(8,128)(2,1)S(1)}, u32[]{:S(2)}, u32[]{:S(2)}) %collective-permute-start.76) | collective-permute-done | bytes 163872 | tf_op jit(solution)/shard_map/ppermute | solution.py:17
  722.3 15.5 %collective-permute-done.69 = f32[16,128]{1,0:T(8,128)S(1)} collective-permute-done((f32[16,128]{1,0:T(8,128)S(1)}, f32[16,128]{1,0:T(8,128)S(1)}, u32[]{:S(2)}, u32[]{:S(2)}) %collective-permute-start.69) | collective-permute-done | bytes 8224 | tf_op jit(solution)/shard_map/ppermute | solution.py:94
  754.6 10.0 %spread_mlp.1 = f32[256,12288]{1,0:T(8,128)} custom-call(s32[1]{0:T(128)} %bitcast.26.mine_ref, bf16[256,3072]{1,0:T(8,128)(2,1)} %reduce-scatter.7.cloned.1.call-done.a_ref, bf16[256,3072]{1,0:T(8,128)(2,1)} %copy-done.33, bf16[256,3072]{1,0:T(8,128)(2,1)} %copy-done.34, bf16[256,3072]{1,0:T(8,128)(2,1)} %pad_maximum_fusion.3.d_ref), custom_call_target="tpu_custom_call" | custom-call | flops 8000000000 | bytes 24000000 | tf_op jit(solution)/shard_map/spread_mlp/pallas_call | solution.py:473
  792.7 6.9 spread_in.1
  (567 shorter events, 379.3 us)
Async XLA Ops:
  7.2 67.3 %all-gather.5.cloned.1.call-start = ((), (), s32[]{:S(2)}) async-start(), calls=%async_computation.4 | async-start | bytes 6488064 | tf_op jit(solution)/shard_map/all_gather | solution.py:57
  11.2 116.3 %all-gather.7.cloned.1.call-start = ((), (), s32[]{:S(2)}) async-start(), calls=%async_computation.5 | async-start | bytes 2949120 | tf_op jit(solution)/shard_map/all_gather | solution.py:57
  11.3 26.5 %collective-permute-start = (bf16[256,2048]{1,0:T(8,128)(2,1)}, bf16[256,2048]{1,0:T(8,128)(2,1)}, u32[]{:S(2)}, u32[]{:S(2)}) collective-permute-start(bf16[256,2048]{1,0:T(8,128)(2,1)} %bitcast.171), channel_id=1, source_target_pairs={{0,8},{8,0},{16,24},{24,16},{1,9},{9,1},{17,25},{25,17},{2,10},{10... | collective-permute-start | bytes 3145736 | tf_op jit(solution)/shard_map/ppermute | solution.py:17
  14.3 27.1 %collective-permute-start.1 = (bf16[256,2048]{1,0:T(8,128)(2,1)}, bf16[256,2048]{1,0:T(8,128)(2,1)}, u32[]{:S(2)}, u32[]{:S(2)}) collective-permute-start(bf16[256,2048]{1,0:T(8,128)(2,1)} %bitcast.172), channel_id=1, source_target_pairs={{0,16},{8,24},{16,0},{24,8},{1,17},{9,25},{17,1},{25,9},{2,18},{10... | collective-permute-start | bytes 3145736 | tf_op jit(solution)/shard_map/ppermute | solution.py:17
  74.5 118.7 %all-gather.9.cloned.1.call-start = ((), (), s32[]{:S(2)}) async-start(), calls=%async_computation.6 | async-start | bytes 7077888 | tf_op jit(solution)/shard_map/all_gather | solution.py:57
  83.3 25.5 %collective-permute-start.4 = (bf16[256,2048]{1,0:T(8,128)(2,1)}, bf16[256,2048]{1,0:T(8,128)(2,1)S(1)}, u32[]{:S(2)}, u32[]{:S(2)}) collective-permute-start(bf16[256,2048]{1,0:T(8,128)(2,1)} %bitcast.174), channel_id=1, source_target_pairs={{0,8},{8,0},{16,24},{24,16},{1,9},{9,1},{17,25},{25,17},{2,10},{10... | collective-permute-start | bytes 3145736 | tf_op jit(solution)/shard_map/ppermute | solution.py:17
  84.8 25.2 %collective-permute-start.5 = (bf16[256,2048]{1,0:T(8,128)(2,1)}, bf16[256,2048]{1,0:T(8,128)(2,1)S(1)}, u32[]{:S(2)}, u32[]{:S(2)}) collective-permute-start(bf16[256,2048]{1,0:T(8,128)(2,1)} %bitcast.175), channel_id=1, source_target_pairs={{0,16},{8,24},{16,0},{24,8},{1,17},{9,25},{17,1},{25,9},{2,18},{10... | collective-permute-start | bytes 3145736 | tf_op jit(solution)/shard_map/ppermute | solution.py:17
  127.6 184.8 %all-gather.11.cloned.1.call-start = ((), (), s32[]{:S(2)}) async-start(), calls=%async_computation.7 | async-start | bytes 14155776 | tf_op jit(solution)/shard_map/all_gather | solution.py:57
  149.7 31.9 %collective-permute-start.14 = (bf16[640,512]{1,0:T(8,128)(2,1)S(1)}, bf16[640,512]{1,0:T(8,128)(2,1)S(1)}, u32[]{:S(2)}, u32[]{:S(2)}) collective-permute-start(bf16[640,512]{1,0:T(8,128)(2,1)S(1)} %pad_maximum_fusion.10), channel_id=1, source_target_pairs={{0,24},{8,16},{16,8},{24,0},{1,25},{9,17},{17,9},{25,1},{2,26},{10... | collective-permute-start | bytes 1966088 | tf_op jit(solution)/shard_map/ppermute | solution.py:17
  151.3 30.2 %collective-permute-start.13 = (bf16[640,512]{1,0:T(8,128)(2,1)S(1)}, bf16[640,512]{1,0:T(8,128)(2,1)S(1)}, u32[]{:S(2)}, u32[]{:S(2)}) collective-permute-start(bf16[640,512]{1,0:T(8,128)(2,1)S(1)} %pad_maximum_fusion.9), channel_id=1, source_target_pairs={{0,16},{8,24},{16,0},{24,8},{1,17},{9,25},{17,1},{25,9},{2,18},{10... | collective-permute-start | bytes 1966088 | tf_op jit(solution)/shard_map/ppermute | solution.py:17
  151.9 29.6 %collective-permute-start.12 = (bf16[640,512]{1,0:T(8,128)(2,1)S(1)}, bf16[640,512]{1,0:T(8,128)(2,1)S(1)}, u32[]{:S(2)}, u32[]{:S(2)}) collective-permute-start(bf16[640,512]{1,0:T(8,128)(2,1)S(1)} %pad_maximum_fusion.8), channel_id=1, source_target_pairs={{0,8},{8,0},{16,24},{24,16},{1,9},{9,1},{17,25},{25,17},{2,10},{10... | collective-permute-start | bytes 1966088 | tf_op jit(solution)/shard_map/ppermute | solution.py:17
  195.0 223.8 %reduce-scatter.5.cloned.1.call-start = ((), (), s32[]{:S(2)}) async-start(), calls=%async_computation.8 | async-start | bytes 7077888 | tf_op jit(solution)/shard_map/reduce_scatter | solution.py:61
  202.9 25.4 %collective-permute-start.18 = (bf16[128,2048]{1,0:T(8,128)(2,1)S(1)}, bf16[128,2048]{1,0:T(8,128)(2,1)S(1)}, u32[]{:S(2)}, u32[]{:S(2)}) collective-permute-start(bf16[128,2048]{1,0:T(8,128)(2,1)S(1)} %get-tuple-element.151), channel_id=1, source_target_pairs={{0,16},{8,24},{16,0},{24,8},{1,17},{9,25},{17,1},{25,9},{2,18},{10... | collective-permute-start | bytes 1572872 | tf_op jit(solution)/shard_map/ppermute | solution.py:17
  344.9 235.4 %reduce-scatter.7.cloned.1.call-start = ((), (), s32[]{:S(2)}) async-start(), calls=%async_computation.9 | async-start | bytes 14155776 | tf_op jit(solution)/shard_map/reduce_scatter | solution.py:61
  365.6 35.0 %collective-permute-start.27 = (bf16[128,2048]{1,0:T(8,128)(2,1)}, bf16[128,2048]{1,0:T(8,128)(2,1)}, u32[]{:S(2)}, u32[]{:S(2)}) collective-permute-start(bf16[128,2048]{1,0:T(8,128)(2,1)} %get-tuple-element.143), channel_id=1, source_target_pairs={{0,8},{8,0},{16,24},{24,16},{1,9},{9,1},{17,25},{25,17},{2,10},{10... | collective-permute-start | bytes 1572872 | tf_op jit(solution)/shard_map/ppermute | solution.py:17
  366.2 34.4 %collective-permute-start.30 = (bf16[128,2048]{1,0:T(8,128)(2,1)}, bf16[128,2048]{1,0:T(8,128)(2,1)}, u32[]{:S(2)}, u32[]{:S(2)}) collective-permute-start(bf16[128,2048]{1,0:T(8,128)(2,1)} %get-tuple-element.145), channel_id=1, source_target_pairs={{0,16},{8,24},{16,0},{24,8},{1,17},{9,25},{17,1},{25,9},{2,18},{10... | collective-permute-start | bytes 1572872 | tf_op jit(solution)/shard_map/ppermute | solution.py:17
  418.8 237.5 %reduce-scatter.9.cloned.1.call-start = ((), (), s32[]{:S(2)}) async-start(), calls=%async_computation.10 | async-start | bytes 2949120 | tf_op jit(solution)/shard_map/reduce_scatter | solution.py:61
  423.8 24.6 %collective-permute-start.34 = (bf16[256,2048]{1,0:T(8,128)(2,1)}, bf16[256,2048]{1,0:T(8,128)(2,1)}, u32[]{:S(2)}, u32[]{:S(2)}) collective-permute-start(bf16[256,2048]{1,0:T(8,128)(2,1)} %get-tuple-element.126), channel_id=1, source_target_pairs={{0,16},{8,24},{16,0},{24,8},{1,17},{9,25},{17,1},{25,9},{2,18},{10... | collective-permute-start | bytes 3145736 | tf_op jit(solution)/shard_map/ppermute | solution.py:17
  468.1 66.6 %collective-permute-start.49 = (bf16[640,512]{1,0:T(8,128)(2,1)}, bf16[640,512]{1,0:T(8,128)(2,1)}, u32[]{:S(2)}, u32[]{:S(2)}) collective-permute-start(bf16[640,512]{1,0:T(8,128)(2,1)} %get-tuple-element.159), channel_id=1, source_target_pairs={{0,8},{8,0},{16,24},{24,16},{1,9},{9,1},{17,25},{25,17},{2,10},{10... | collective-permute-start | bytes 1966088 | tf_op jit(solution)/shard_map/ppermute | solution.py:17
  494.9 44.0 %collective-permute-start.50 = (bf16[640,512]{1,0:T(8,128)(2,1)}, bf16[640,512]{1,0:T(8,128)(2,1)}, u32[]{:S(2)}, u32[]{:S(2)}) collective-permute-start(bf16[640,512]{1,0:T(8,128)(2,1)} %get-tuple-element.158), channel_id=1, source_target_pairs={{0,16},{8,24},{16,0},{24,8},{1,17},{9,25},{17,1},{25,9},{2,18},{10... | collective-permute-start | bytes 1966088 | tf_op jit(solution)/shard_map/ppermute | solution.py:17
  496.9 45.5 %collective-permute-start.51 = (bf16[640,512]{1,0:T(8,128)(2,1)}, bf16[640,512]{1,0:T(8,128)(2,1)}, u32[]{:S(2)}, u32[]{:S(2)}) collective-permute-start(bf16[640,512]{1,0:T(8,128)(2,1)} %get-tuple-element.157), channel_id=1, source_target_pairs={{0,24},{8,16},{16,8},{24,0},{1,25},{9,17},{17,9},{25,1},{2,26},{10... | collective-permute-start | bytes 1966088 | tf_op jit(solution)/shard_map/ppermute | solution.py:17
  498.7 62.0 %collective-permute-start.37 = (bf16[128,2048]{1,0:T(8,128)(2,1)}, bf16[128,2048]{1,0:T(8,128)(2,1)}, u32[]{:S(2)}, u32[]{:S(2)}) collective-permute-start(bf16[128,2048]{1,0:T(8,128)(2,1)} %get-tuple-element.137), channel_id=1, source_target_pairs={{0,8},{8,0},{16,24},{24,16},{1,9},{9,1},{17,25},{25,17},{2,10},{10... | collective-permute-start | bytes 1572872 | tf_op jit(solution)/shard_map/ppermute | solution.py:17
  509.3 71.0 %collective-permute-start.42 = (bf16[128,2048]{1,0:T(8,128)(2,1)}, bf16[128,2048]{1,0:T(8,128)(2,1)}, u32[]{:S(2)}, u32[]{:S(2)}) collective-permute-start(bf16[128,2048]{1,0:T(8,128)(2,1)} %get-tuple-element.138), channel_id=1, source_target_pairs={{0,16},{8,24},{16,0},{24,8},{1,17},{9,25},{17,1},{25,9},{2,18},{10... | collective-permute-start | bytes 1572872 | tf_op jit(solution)/shard_map/ppermute | solution.py:17
  534.7 26.1 %collective-permute-start.39 = (bf16[128,2048]{1,0:T(8,128)(2,1)}, bf16[128,2048]{1,0:T(8,128)(2,1)}, u32[]{:S(2)}, u32[]{:S(2)}) collective-permute-start(bf16[128,2048]{1,0:T(8,128)(2,1)} %add_convert_fusion.3), channel_id=1, source_target_pairs={{0,16},{8,24},{16,0},{24,8},{1,17},{9,25},{17,1},{25,9},{2,18},{10... | collective-permute-start | bytes 1572872 | tf_op jit(solution)/shard_map/ppermute | solution.py:17
  567.0 27.6 %collective-permute-start.52 = (bf16[192,2048]{1,0:T(8,128)(2,1)}, bf16[192,2048]{1,0:T(8,128)(2,1)S(1)}, u32[]{:S(2)}, u32[]{:S(2)}) collective-permute-start(bf16[192,2048]{1,0:T(8,128)(2,1)} %reduce-scatter.5.cloned.1.call-done), channel_id=1, source_target_pairs={{0,8},{8,0},{16,24},{24,16},{1,9},{9,1},{17,25},{25,17},{2,10},{10... | collective-permute-start | bytes 2359304 | tf_op jit(solution)/shard_map/ppermute | solution.py:17
  567.8 28.4 %collective-permute-start.53 = (bf16[192,2048]{1,0:T(8,128)(2,1)}, bf16[192,2048]{1,0:T(8,128)(2,1)}, u32[]{:S(2)}, u32[]{:S(2)}) collective-permute-start(bf16[192,2048]{1,0:T(8,128)(2,1)} %reduce-scatter.5.cloned.1.call-done), channel_id=1, source_target_pairs={{0,16},{8,24},{16,0},{24,8},{1,17},{9,25},{17,1},{25,9},{2,18},{10... | collective-permute-start | bytes 2359304 | tf_op jit(solution)/shard_map/ppermute | solution.py:17
  580.3 184.4 %reduce-scatter.11.cloned.1.call-start = ((), (), s32[]{:S(2)}) async-start(), calls=%async_computation.11 | async-start | bytes 6488064 | tf_op jit(solution)/shard_map/reduce_scatter | solution.py:61
  610.0 69.8 %collective-permute-start.60 = (bf16[128,2048]{1,0:T(8,128)(2,1)}, bf16[128,2048]{1,0:T(8,128)(2,1)}, u32[]{:S(2)}, u32[]{:S(2)}) collective-permute-start(bf16[128,2048]{1,0:T(8,128)(2,1)} %get-tuple-element.131), channel_id=1, source_target_pairs={{0,8},{8,0},{16,24},{24,16},{1,9},{9,1},{17,25},{25,17},{2,10},{10... | collective-permute-start | bytes 1572872 | tf_op jit(solution)/shard_map/ppermute | solution.py:17
  610.8 98.9 %collective-permute-start.65 = (bf16[128,2048]{1,0:T(8,128)(2,1)}, bf16[128,2048]{1,0:T(8,128)(2,1)}, u32[]{:S(2)}, u32[]{:S(2)}) collective-permute-start(bf16[128,2048]{1,0:T(8,128)(2,1)} %get-tuple-element.132), channel_id=1, source_target_pairs={{0,16},{8,24},{16,0},{24,8},{1,17},{9,25},{17,1},{25,9},{2,18},{10... | collective-permute-start | bytes 1572872 | tf_op jit(solution)/shard_map/ppermute | solution.py:17
  650.1 24.9 %collective-permute-start.79 = (bf16[288,640]{1,0:T(8,128)(2,1)}, bf16[288,640]{1,0:T(8,128)(2,1)}, u32[]{:S(2)}, u32[]{:S(2)}) collective-permute-start(bf16[288,640]{1,0:T(8,128)(2,1)} %slice.654), channel_id=1, source_target_pairs={{0,16},{8,24},{16,0},{24,8},{1,17},{9,25},{17,1},{25,9},{2,18},{10... | collective-permute-start | bytes 1105928 | tf_op jit(solution)/shard_map/ppermute | solution.py:17
  697.5 40.7 %collective-permute-start.71 = (bf16[256,3072]{1,0:T(8,128)(2,1)S(1)}, bf16[256,3072]{1,0:T(8,128)(2,1)S(1)}, u32[]{:S(2)}, u32[]{:S(2)}) collective-permute-start(bf16[256,3072]{1,0:T(8,128)(2,1)S(1)} %copy-done.56), channel_id=1, source_target_pairs={{0,8},{8,0},{16,24},{24,16},{1,9},{9,1},{17,25},{25,17},{2,10},{10... | collective-permute-start | bytes 4718600 | tf_op jit(solution)/shard_map/ppermute | solution.py:17
  699.4 40.6 %collective-permute-start.72 = (bf16[256,3072]{1,0:T(8,128)(2,1)S(1)}, bf16[256,3072]{1,0:T(8,128)(2,1)S(1)}, u32[]{:S(2)}, u32[]{:S(2)}) collective-permute-start(bf16[256,3072]{1,0:T(8,128)(2,1)S(1)} %copy-done.56), channel_id=1, source_target_pairs={{0,16},{8,24},{16,0},{24,8},{1,17},{9,25},{17,1},{25,9},{2,18},{10... | collective-permute-start | bytes 4718600 | tf_op jit(solution)/shard_map/ppermute | solution.py:17
  (128 other events, 1969.6 us)
Sparse Core Ops, SparseCore 0:
  11.3 63.1 all-gather.4
  76.1 32.5 all-gather.6
  127.7 65.4 all-gather.8
  195.3 117.0 all-gather.10
  345.0 68.0 reduce-scatter.4
  418.9 128.3 reduce-scatter.6
  580.4 36.8 reduce-scatter.8
  656.5 63.2 reduce-scatter.10

commit v3 on v2

--- a/solution.py
+++ b/solution.py
@@ -638,10 +638,11 @@
     )(odd_flag, u, rim, cw, cb, gw, gs, gb, soft)
     down_rows = gather_group(
         after(
-            lax.dynamic_slice_in_dim(down_weight, mine * fine, fine, 0), out_cols, decay_cum
+            lax.dynamic_slice_in_dim(down_weight, mine * fine, fine, 0), out_cols, u
         )
     )
     carried = entering(decay_cum[:, -1], state_local[:, -1], 1)
+    arrived = carried
     carried = after(carried, out_rows)
     carried8 = jnp.broadcast_to(carried[:, None], (members, 8, own))
     h, merged = pl.pallas_call(
@@ -656,7 +657,7 @@
     )(state_local, decay_cum, carried8, y)
     partial = jnp.dot(merged.reshape(rows, own), out_rows, preferred_element_type=f32)
     partial = partial.astype(bf16)
-    mlp_cols = gather_group(after(cut, down_rows, merged))
+    mlp_cols = gather_group(after(cut, down_rows, out_rows, arrived))
     partial = lax.optimization_barrier(partial).reshape(members, tokens, model)
     x32 = x_own.astype(f32)
     grad_hidden = lax.dot_general(
@@ -787,18 +788,17 @@
     out_part = lax.dot_general(
         merged.reshape(rows, own), grad_resid_all, down, preferred_element_type=f32
     ).astype(bf16)
-    out_terms = jnp.zeros((rec, out_piece), bf16)
+    pieces = []
     for k in range(members):
         piece = lax.dynamic_slice_in_dim(out_part, (mine ^ k) * out_piece, out_piece, 1)
-        if k:
-            piece = swap(piece, k)
-        start, common = first_of(mine ^ k)
-        out_terms = lax.dynamic_update_slice_in_dim(
-            out_terms, piece[: 2 * head], start * head, 0
-        )
-        out_terms = lax.dynamic_update_slice_in_dim(
-            out_terms, piece[2 * head :], common * head + ((mine ^ k) % 2) * half, 0
-        )
+        pieces.append(swap(piece, k) if k else piece)
+    pieces = jnp.stack(pieces)
+    out_terms = []
+    for member in range(members):
+        piece = lax.dynamic_index_in_dim(pieces, mine ^ member, 0, keepdims=False)
+        cut_at = 2 * head if member % 2 else 0
+        out_terms += [piece[cut_at:], piece[:cut_at]]
+    out_terms = jnp.concatenate(out_terms, 0)
     gate_terms = jnp.concatenate([gw_grad[:, 0], gw_grad[:, 1], gs_grad], -1).reshape(-1, own)
     decay_terms = small[2:3] * (-8.0) * owned(jax.nn.sigmoid(decay_param))[None]
     sizes = ((taps + 1) * wide, 3 * own, model)

time: 819 us -> 819 us (level)
  waiting for transfers between devices: 293 us -> 265 us
  matrix products: 114 us -> 129 us
  starting transfers between devices: 107 us -> 122 us
    ppermute x66, waiting for transfers between devices: 235 us -> 211 us  [swap(): lax.ppermute(block, 'seq', [(i, i ^ k) for i in range(lax.axis_size('seq'...]
    dynamic_update_slice x8 -> x0, local copies, waits for them, and re-layouts: 12 us -> none  [the longest x4 6.59 us: shards(): lax.dynamic_update_slice_in_dim(out_terms, piece[:2 * head], start * head...]
    ppermute x66, starting transfers between devices: 72.5 us -> 83 us  [swap(): lax.ppermute(block, 'seq', [(i, i ^ k) for i in range(lax.axis_size('seq'...]
    dot_general x1, matrix products: 11.3 us -> 21.1 us  [shards(): lax.dot_general(hidden_low, c_all, down, preferred_element_type=f32)]
    unnamed x152 -> x143, local copies, waits for them, and re-layouts: 22.4 us -> 28.1 us
  transfers between devices with their start and end apart: 97 -> 97, of which waited for: 44 -> 43; matrix products, arithmetic and copies ran while one was open for 35% -> 36% of each run, Pallas kernels for 7% -> 7%
where the time goes in v3:
time: 819 us; the launch traced here: 813 us
  waiting for transfers between devices  265 us (32%)
  matrix products  129 us (16%)
  local copies, waits for them, and re-layouts  122 us (15%)
  starting transfers between devices  122 us (15%)
  Pallas kernels  87.7 us (11%)
  other arithmetic  71.5 us (9%)
  between operations  16.3 us (2%)
    ppermute x66, waiting for transfers between devices, swap(): lax.ppermute(block, 'seq', [(i, i ^ k) for i in range(lax.axis_size('seq'...  211 us
    ppermute x66, starting transfers between devices, swap(): lax.ppermute(block, 'seq', [(i, i ^ k) for i in range(lax.axis_size('seq'...  83 us
    ppermute x12, starting transfers between devices, shift(): lax.ppermute(block, 'group', [(i - distance, i) for i in devices if i - d...  28.6 us
    unnamed x143, local copies, waits for them, and re-layouts  28.1 us
    pallas_call x1, Pallas kernels, shards(): pl.pallas_call(mlp_kernel, grid=(parts,), in_specs=[whole(rows, model), p...  21.2 us
    dot_general x1, matrix products, shards(): lax.dot_general(hidden_low, c_all, down, preferred_element_type=f32)  21.1 us
    dot_general x1, matrix products, shards(): lax.dot_general(normed2, after(grad_gu, partial), down, preferred_element...  19.4 us
    ppermute x5, waiting for transfers between devices, total(): lax.ppermute(value, axis, [(i, i ^ step) for i in range(count)])  18.3 us
  transfers between devices with their start and end apart: 97, of which 43 were waited for; matrix products, arithmetic and copies ran while one was open for 36% of the time, Pallas kernels for 7%

profile of v3, /device:TPU:0, one launch (start us, length us, event | category | flops | bytes accessed | tf_op | source)
XLA Modules:
  0.0 813.0 jit_solution(15780748860990115501)
XLA Ops:
  19.8 17.9 %collective-permute-done = bf16[256,2048]{1,0:T(8,128)(2,1)} collective-permute-done((bf16[256,2048]{1,0:T(8,128)(2,1)}, bf16[256,2048]{1,0:T(8,128)(2,1)}, u32[]{:S(2)}, u32[]{:S(2)}) %collective-permute-start) | collective-permute-done | bytes 1048608 | tf_op jit(solution)/shard_map/ppermute | solution.py:17
  47.1 8.7 %copy.38 = bf16[256,12288]{0,1:T(8,128)(2,1)} copy(bf16[256,12288]{1,0:T(8,128)(2,1)} %param.24) | data formatting | bytes 12582912 | tf_op jit(solution)/shard_map/optimization_barrier | solution.py:65
  78.5 8.2 %fusion.3 = f32[1024,768]{1,0:T(8,128)} fusion(bf16[1024,2048]{1,0:T(8,128)(2,1)} %fusion.2, bf16[2048,1408]{1,0:T(8,128)(2,1)} %all-gather.5.cloned.1.call-done), kind=kOutput, calls=%fused_computation.18 | convolution fusion | flops 3221225472 | bytes 10485760 | tf_op jit(solution)/shard_map/dot_general | solution.py:598
  86.8 13.5 %collective-permute-done.4 = bf16[256,2048]{1,0:T(8,128)(2,1)} collective-permute-done((bf16[256,2048]{1,0:T(8,128)(2,1)}, bf16[256,2048]{1,0:T(8,128)(2,1)}, u32[]{:S(2)}, u32[]{:S(2)}) %collective-permute-start.4) | collective-permute-done | bytes 1048608 | tf_op jit(solution)/shard_map/ppermute | solution.py:17
  101.5 7.9 all-gather.7.cloned.1.call-done
  124.1 14.5 %recurrence_forward.1 = (f32[4,256,768]{2,1,0:T(8,128)}, f32[4,256,640]{2,1,0:T(8,128)}, f32[4,256,640]{2,1,0:T(8,128)}, f32[4,256,640]{2,1,0:T(8,128)}, f32[4,256,640]{2,1,0:T(8,128)}, /*index=5*/f32[4,256,640]{2,1,0:T(8,128)}) custom-call(s32[1]{0:T(128)} %bitcast.1.odd_ref, f32[4,256,768]{2,1,0:T(8,128)} %bitcast.234, f32[4,8,768]{2,1,0:T(8,128)} %pad.17.rim_ref, ...), custom_call_target="tpu_custom_call" | custom-call | flops 14000000000 | bytes 42000000 | tf_op jit(solution)/shard_map/recurrence_forward/pallas_call | solution.py:614
  139.6 8.4 %collective-permute-start.10 = (f32[2,4,640]{2,0,1:T(2,128)S(1)}, f32[2,4,640]{2,0,1:T(2,128)S(1)}, u32[]{:S(2)}, u32[]{:S(2)}) collective-permute-start(f32[2,4,640]{2,0,1:T(2,128)S(1)} %pad_maximum_fusion.13), channel_id=1, source_target_pairs={{0,4},{1,5},{2,6},{3,7},{8,12},{9,13},{10,14},{11,15},{16,20},{17,... | collective-permute-start | bytes 61448 | tf_op jit(solution)/shard_map/ppermute | solution.py:22
  175.4 12.6 %collective-permute-done.13 = bf16[640,512]{1,0:T(8,128)(2,1)} collective-permute-done((bf16[640,512]{1,0:T(8,128)(2,1)}, bf16[640,512]{1,0:T(8,128)(2,1)}, u32[]{:S(2)}, u32[]{:S(2)}) %collective-permute-start.13) | collective-permute-done | bytes 655392 | tf_op jit(solution)/shard_map/ppermute | solution.py:17
  194.1 7.9 fusion.5
  218.6 11.4 %collective-permute-done.16 = bf16[128,2048]{1,0:T(8,128)(2,1)S(1)} collective-permute-done((bf16[128,2048]{1,0:T(8,128)(2,1)S(1)}, bf16[128,2048]{1,0:T(8,128)(2,1)S(1)}, u32[]{:S(2)}, u32[]{:S(2)}) %collective-permute-start.16) | collective-permute-done | bytes 524320 | tf_op jit(solution)/shard_map/ppermute | solution.py:17
  247.6 8.6 %collective-permute-done.21 = bf16[128,2048]{1,0:T(8,128)(2,1)S(1)} collective-permute-done((bf16[128,2048]{1,0:T(8,128)(2,1)S(1)}, bf16[128,2048]{1,0:T(8,128)(2,1)S(1)}, u32[]{:S(2)}, u32[]{:S(2)}) %collective-permute-start.21) | collective-permute-done | bytes 524320 | tf_op jit(solution)/shard_map/ppermute | solution.py:17
  263.2 8.6 %fusion.56.grad_ref = f32[1024,1536]{1,0:T(8,128)} fusion(bf16[1024,2048]{1,0:T(8,128)(2,1)S(1)} %constant_dynamic-update-slice_fusion.5, bf16[1536,2048]{1,0:T(8,128)(2,1)S(1)} %bitcast.237), kind=kOutput, calls=%fused_computation.265 | convolution fusion | flops 6442450944 | bytes 16777216 | tf_op jit(solution)/shard_map/dot_general | solution.py:663
  275.4 18.2 %collective-permute-done.23 = bf16[256,2048]{1,0:T(8,128)(2,1)S(1)} collective-permute-done((bf16[256,2048]{1,0:T(8,128)(2,1)S(1)}, bf16[256,2048]{1,0:T(8,128)(2,1)S(1)}, u32[]{:S(2)}, u32[]{:S(2)}) %collective-permute-start.23) | collective-permute-done | bytes 1048608 | tf_op jit(solution)/shard_map/ppermute | solution.py:17
  310.5 21.2 %mlp.1 = (bf16[1024,1536]{1,0:T(8,128)(2,1)}, bf16[1024,3072]{1,0:T(8,128)(2,1)}) custom-call(bf16[1024,2048]{1,0:T(8,128)(2,1)} %constant_dynamic-update-slice_fusion.10.normed_ref, bf16[2048,3072]{1,0:T(8,128)(2,1)} %all-gather.11.cloned.1.call-done.weight_ref, f32[1024,1536]{1,0:T(8,128)} %fusion.56.grad_ref), custom_call_target="tpu_custom_call" | custom-call | flops 12884901888 | bytes 32505856 | tf_op jit(solution)/shard_map/mlp/pallas_call | solution.py:670
  331.7 21.1 %convolution_convert_fusion.2 = bf16[1536,2048]{1,0:T(8,128)(2,1)} fusion(bf16[1024,1536]{1,0:T(8,128)(2,1)} %get-tuple-element.79, bf16[1024,2048]{1,0:T(8,128)(2,1)} %copy-done.31), kind=kOutput, calls=%fused_computation.7 | convolution fusion | flops 6445596672 | bytes 13631488 | tf_op jit(solution)/shard_map/dot_general | solution.py:696
  352.9 17.6 %convolution_convert_fusion.3 = bf16[1024,2048]{1,0:T(8,128)(2,1)S(1)} fusion(bf16[1024,3072]{1,0:T(8,128)(2,1)} %get-tuple-element.78, bf16[2048,3072]{1,0:T(8,128)(2,1)} %all-gather.11.cloned.1.call-done.weight_ref), kind=kOutput, calls=%fused_computation.13 | convolution fusion | flops 12886999040 | bytes 23068672 | tf_op jit(solution)/shard_map/dot_general | solution.py:698
  375.2 11.3 %collective-permute-done.28 = bf16[128,2048]{1,0:T(8,128)(2,1)S(1)} collective-permute-done((bf16[128,2048]{1,0:T(8,128)(2,1)S(1)}, bf16[128,2048]{1,0:T(8,128)(2,1)S(1)}, u32[]{:S(2)}, u32[]{:S(2)}) %collective-permute-start.28) | collective-permute-done | bytes 524320 | tf_op jit(solution)/shard_map/ppermute | solution.py:17
  388.2 19.4 %convolution_convert_fusion = bf16[2048,3072]{1,0:T(8,128)(2,1)} fusion(bf16[1024,2048]{1,0:T(8,128)(2,1)} %constant_dynamic-update-slice_fusion.10.normed_ref, bf16[1024,3072]{1,0:T(8,128)(2,1)} %get-tuple-element.78), kind=kOutput, calls=%fused_computation | convolution fusion | flops 12891193344 | bytes 23068672 | tf_op jit(solution)/shard_map/dot_general | solution.py:701
  412.2 11.5 %convolution_convert_fusion.4 = bf16[1024,2048]{1,0:T(8,128)(2,1)} fusion(bf16[1024,1536]{1,0:T(8,128)(2,1)S(1)} %copy-done.53, bf16[1536,2048]{1,0:T(8,128)(2,1)} %all-gather.9.cloned.1.call-done), kind=kOutput, calls=%fused_computation.14 | convolution fusion | flops 6444548096 | bytes 13631488 | tf_op jit(solution)/shard_map/dot_general | solution.py:705
  434.3 19.7 %collective-permute-done.33 = bf16[256,2048]{1,0:T(8,128)(2,1)S(1)} collective-permute-done((bf16[256,2048]{1,0:T(8,128)(2,1)}, bf16[256,2048]{1,0:T(8,128)(2,1)S(1)}, u32[]{:S(2)}, u32[]{:S(2)}) %collective-permute-start.33) | collective-permute-done | bytes 1048608 | tf_op jit(solution)/shard_map/ppermute | solution.py:17
  481.4 10.2 %recurrence_adjoint.1 = (f32[4,256,640]{2,1,0:T(8,128)}, bf16[4,256,640]{2,1,0:T(8,128)(2,1)}, f32[4,256,640]{2,1,0:T(8,128)}, f32[4,256,640]{2,1,0:T(8,128)}) custom-call(f32[4,256,640]{2,1,0:T(8,128)} %bitcast.242, f32[4,256,640]{2,1,0:T(8,128)} %get-tuple-element.83.h_ref, f32[4,256,640]{2,1,0:T(8,128)} %bitcast.241, ...), custom_call_target="tpu_custom_call" | custom-call | flops 10000000000 | bytes 30000000 | tf_op jit(solution)/shard_map/recurrence_adjoint/pallas_call | solution.py:723
  522.1 18.3 %recurrence_backward.1 = (bf16[4,256,1408]{2,1,0:T(8,128)(2,1)}, f32[4,8,768]{2,1,0:T(8,128)}, f32[4,8,768]{2,1,0:T(8,128)}, f32[8,640]{1,0:T(8,128)}, f32[8,768...) custom-call(s32[1]{0:T(128)} %bitcast.1.odd_ref, f32[4,256,640]{2,1,0:T(8,128)} %get-tuple-element.85.back_ref, ...), custom_call_target="tpu_custom_call" | custom-call | flops 19000000512 | bytes 57000000 | tf_op jit(solution)/shard_map/recurrence_backward/pallas_call | solution.py:735
  576.6 10.4 %convolution_convert_fusion.1 = bf16[2048,1408]{1,0:T(8,128)(2,1)} fusion(bf16[1024,2048]{1,0:T(8,128)(2,1)S(1)} %copy-done.15, bf16[1024,1408]{1,0:T(8,128)(2,1)} %bitcast.238), kind=kOutput, calls=%fused_computation.6 | convolution fusion | flops 5908463616 | bytes 12845056 | tf_op jit(solution)/shard_map/dot_general | solution.py:823
  592.3 9.5 %collective-permute-done.52 = bf16[192,2048]{1,0:T(8,128)(2,1)S(1)} collective-permute-done((bf16[192,2048]{1,0:T(8,128)(2,1)}, bf16[192,2048]{1,0:T(8,128)(2,1)S(1)}, u32[]{:S(2)}, u32[]{:S(2)}) %collective-permute-start.52) | collective-permute-done | bytes 786464 | tf_op jit(solution)/shard_map/ppermute | solution.py:17
  606.0 8.8 %convolution_convert_fusion.5 = bf16[1024,2048]{1,0:T(8,128)(2,1)S(1)} fusion(bf16[1024,1408]{1,0:T(8,128)(2,1)S(1)} %bitcast.239, bf16[2048,1408]{1,0:T(8,128)(2,1)} %all-gather.5.cloned.1.call-done), kind=kOutput, calls=%fused_computation.15 | convolution fusion | flops 5907677184 | bytes 12845056 | tf_op jit(solution)/shard_map/dot_general | solution.py:817
  622.1 8.9 %collective-permute-done.61 = bf16[128,2048]{1,0:T(8,128)(2,1)S(1)} collective-permute-done((bf16[128,2048]{1,0:T(8,128)(2,1)S(1)}, bf16[128,2048]{1,0:T(8,128)(2,1)S(1)}, u32[]{:S(2)}, u32[]{:S(2)}) %collective-permute-start.61) | collective-permute-done | bytes 524320 | tf_op jit(solution)/shard_map/ppermute | solution.py:17
  638.5 16.4 %collective-permute-done.78 = bf16[576,640]{1,0:T(8,128)(2,1)S(1)} collective-permute-done((bf16[576,640]{1,0:T(8,128)(2,1)S(1)}, bf16[576,640]{1,0:T(8,128)(2,1)S(1)}, u32[]{:S(2)}, u32[]{:S(2)}) %collective-permute-start.78) | collective-permute-done | bytes 737312 | tf_op jit(solution)/shard_map/ppermute | solution.py:17
  686.9 9.0 %collective-permute-done.62 = bf16[128,2048]{1,0:T(8,128)(2,1)S(1)} collective-permute-done((bf16[128,2048]{1,0:T(8,128)(2,1)S(1)}, bf16[128,2048]{1,0:T(8,128)(2,1)S(1)}, u32[]{:S(2)}, u32[]{:S(2)}) %collective-permute-start.62) | collective-permute-done | bytes 524320 | tf_op jit(solution)/shard_map/ppermute | solution.py:17
  706.6 9.5 %collective-permute-done.76 = bf16[160,512]{1,0:T(8,128)(2,1)S(1)} collective-permute-done((bf16[160,512]{1,0:T(8,128)(2,1)S(1)}, bf16[160,512]{1,0:T(8,128)(2,1)S(1)}, u32[]{:S(2)}, u32[]{:S(2)}) %collective-permute-start.76) | collective-permute-done | bytes 163872 | tf_op jit(solution)/shard_map/ppermute | solution.py:17
  729.0 14.3 %collective-permute-done.69 = f32[16,128]{1,0:T(8,128)S(1)} collective-permute-done((f32[16,128]{1,0:T(8,128)S(1)}, f32[16,128]{1,0:T(8,128)S(1)}, u32[]{:S(2)}, u32[]{:S(2)}) %collective-permute-start.69) | collective-permute-done | bytes 8224 | tf_op jit(solution)/shard_map/ppermute | solution.py:94
  760.0 9.9 %spread_mlp.1 = f32[256,12288]{1,0:T(8,128)} custom-call(s32[1]{0:T(128)} %bitcast.36.mine_ref, bf16[256,3072]{1,0:T(8,128)(2,1)} %reduce-scatter.7.cloned.1.call-done.a_ref, bf16[256,3072]{1,0:T(8,128)(2,1)} %copy-done.28, bf16[256,3072]{1,0:T(8,128)(2,1)} %copy-done.29, bf16[256,3072]{1,0:T(8,128)(2,1)} %pad_maximum_fusion.4.d_ref), custom_call_target="tpu_custom_call" | custom-call | flops 8000000000 | bytes 24000000 | tf_op jit(solution)/shard_map/spread_mlp/pallas_call | solution.py:473
  799.0 6.9 spread_in.1
  (551 shorter events, 396.4 us)
Async XLA Ops:
  7.2 67.3 %all-gather.5.cloned.1.call-start = ((), (), s32[]{:S(2)}) async-start(), calls=%async_computation.4 | async-start | bytes 6488064 | tf_op jit(solution)/shard_map/all_gather | solution.py:57
  11.2 98.1 %all-gather.7.cloned.1.call-start = ((), (), s32[]{:S(2)}) async-start(), calls=%async_computation.5 | async-start | bytes 2949120 | tf_op jit(solution)/shard_map/all_gather | solution.py:57
  11.3 26.5 %collective-permute-start = (bf16[256,2048]{1,0:T(8,128)(2,1)}, bf16[256,2048]{1,0:T(8,128)(2,1)}, u32[]{:S(2)}, u32[]{:S(2)}) collective-permute-start(bf16[256,2048]{1,0:T(8,128)(2,1)} %bitcast.196), channel_id=1, source_target_pairs={{0,8},{8,0},{16,24},{24,16},{1,9},{9,1},{17,25},{25,17},{2,10},{10... | collective-permute-start | bytes 3145736 | tf_op jit(solution)/shard_map/ppermute | solution.py:17
  14.3 27.1 %collective-permute-start.1 = (bf16[256,2048]{1,0:T(8,128)(2,1)}, bf16[256,2048]{1,0:T(8,128)(2,1)}, u32[]{:S(2)}, u32[]{:S(2)}) collective-permute-start(bf16[256,2048]{1,0:T(8,128)(2,1)} %bitcast.197), channel_id=1, source_target_pairs={{0,16},{8,24},{16,0},{24,8},{1,17},{9,25},{17,1},{25,9},{2,18},{10... | collective-permute-start | bytes 3145736 | tf_op jit(solution)/shard_map/ppermute | solution.py:17
  74.5 117.5 %all-gather.9.cloned.1.call-start = ((), (), s32[]{:S(2)}) async-start(), calls=%async_computation.6 | async-start | bytes 7077888 | tf_op jit(solution)/shard_map/all_gather | solution.py:57
  74.6 25.7 %collective-permute-start.4 = (bf16[256,2048]{1,0:T(8,128)(2,1)}, bf16[256,2048]{1,0:T(8,128)(2,1)}, u32[]{:S(2)}, u32[]{:S(2)}) collective-permute-start(bf16[256,2048]{1,0:T(8,128)(2,1)} %bitcast.199), channel_id=1, source_target_pairs={{0,8},{8,0},{16,24},{24,16},{1,9},{9,1},{17,25},{25,17},{2,10},{10... | collective-permute-start | bytes 3145736 | tf_op jit(solution)/shard_map/ppermute | solution.py:17
  76.1 25.3 %collective-permute-start.5 = (bf16[256,2048]{1,0:T(8,128)(2,1)}, bf16[256,2048]{1,0:T(8,128)(2,1)}, u32[]{:S(2)}, u32[]{:S(2)}) collective-permute-start(bf16[256,2048]{1,0:T(8,128)(2,1)} %bitcast.200), channel_id=1, source_target_pairs={{0,16},{8,24},{16,0},{24,8},{1,17},{9,25},{17,1},{25,9},{2,18},{10... | collective-permute-start | bytes 3145736 | tf_op jit(solution)/shard_map/ppermute | solution.py:17
  109.3 201.2 %all-gather.11.cloned.1.call-start = ((), (), s32[]{:S(2)}) async-start(), calls=%async_computation.7 | async-start | bytes 14155776 | tf_op jit(solution)/shard_map/all_gather | solution.py:57
  157.9 30.1 %collective-permute-start.13 = (bf16[640,512]{1,0:T(8,128)(2,1)}, bf16[640,512]{1,0:T(8,128)(2,1)}, u32[]{:S(2)}, u32[]{:S(2)}) collective-permute-start(bf16[640,512]{1,0:T(8,128)(2,1)} %pad_maximum_fusion.10), channel_id=1, source_target_pairs={{0,16},{8,24},{16,0},{24,8},{1,17},{9,25},{17,1},{25,9},{2,18},{10... | collective-permute-start | bytes 1966088 | tf_op jit(solution)/shard_map/ppermute | solution.py:17
  160.3 29.7 %collective-permute-start.14 = (bf16[640,512]{1,0:T(8,128)(2,1)}, bf16[640,512]{1,0:T(8,128)(2,1)}, u32[]{:S(2)}, u32[]{:S(2)}) collective-permute-start(bf16[640,512]{1,0:T(8,128)(2,1)} %pad_maximum_fusion.11), channel_id=1, source_target_pairs={{0,24},{8,16},{16,8},{24,0},{1,25},{9,17},{17,9},{25,1},{2,26},{10... | collective-permute-start | bytes 1966088 | tf_op jit(solution)/shard_map/ppermute | solution.py:17
  193.8 232.7 %reduce-scatter.5.cloned.1.call-start = ((), (), s32[]{:S(2)}) async-start(), calls=%async_computation.8 | async-start | bytes 7077888 | tf_op jit(solution)/shard_map/reduce_scatter | solution.py:61
  217.1 25.5 %collective-permute-start.18 = (bf16[128,2048]{1,0:T(8,128)(2,1)S(1)}, bf16[128,2048]{1,0:T(8,128)(2,1)S(1)}, u32[]{:S(2)}, u32[]{:S(2)}) collective-permute-start(bf16[128,2048]{1,0:T(8,128)(2,1)S(1)} %get-tuple-element.151), channel_id=1, source_target_pairs={{0,16},{8,24},{16,0},{24,8},{1,17},{9,25},{17,1},{25,9},{2,18},{10... | collective-permute-start | bytes 1572872 | tf_op jit(solution)/shard_map/ppermute | solution.py:17
  273.7 24.5 %collective-permute-start.24 = (bf16[256,2048]{1,0:T(8,128)(2,1)S(1)}, bf16[256,2048]{1,0:T(8,128)(2,1)S(1)}, u32[]{:S(2)}, u32[]{:S(2)}) collective-permute-start(bf16[256,2048]{1,0:T(8,128)(2,1)S(1)} %get-tuple-element.128), channel_id=1, source_target_pairs={{0,16},{8,24},{16,0},{24,8},{1,17},{9,25},{17,1},{25,9},{2,18},{10... | collective-permute-start | bytes 3145736 | tf_op jit(solution)/shard_map/ppermute | solution.py:17
  352.8 235.4 %reduce-scatter.7.cloned.1.call-start = ((), (), s32[]{:S(2)}) async-start(), calls=%async_computation.9 | async-start | bytes 14155776 | tf_op jit(solution)/shard_map/reduce_scatter | solution.py:61
  373.2 35.0 %collective-permute-start.27 = (bf16[128,2048]{1,0:T(8,128)(2,1)}, bf16[128,2048]{1,0:T(8,128)(2,1)}, u32[]{:S(2)}, u32[]{:S(2)}) collective-permute-start(bf16[128,2048]{1,0:T(8,128)(2,1)} %get-tuple-element.143), channel_id=1, source_target_pairs={{0,8},{8,0},{16,24},{24,16},{1,9},{9,1},{17,25},{25,17},{2,10},{10... | collective-permute-start | bytes 1572872 | tf_op jit(solution)/shard_map/ppermute | solution.py:17
  373.8 34.4 %collective-permute-start.30 = (bf16[128,2048]{1,0:T(8,128)(2,1)}, bf16[128,2048]{1,0:T(8,128)(2,1)}, u32[]{:S(2)}, u32[]{:S(2)}) collective-permute-start(bf16[128,2048]{1,0:T(8,128)(2,1)} %get-tuple-element.145), channel_id=1, source_target_pairs={{0,16},{8,24},{16,0},{24,8},{1,17},{9,25},{17,1},{25,9},{2,18},{10... | collective-permute-start | bytes 1572872 | tf_op jit(solution)/shard_map/ppermute | solution.py:17
  426.5 236.3 %reduce-scatter.9.cloned.1.call-start = ((), (), s32[]{:S(2)}) async-start(), calls=%async_computation.10 | async-start | bytes 2949120 | tf_op jit(solution)/shard_map/reduce_scatter | solution.py:61
  431.4 24.6 %collective-permute-start.34 = (bf16[256,2048]{1,0:T(8,128)(2,1)}, bf16[256,2048]{1,0:T(8,128)(2,1)}, u32[]{:S(2)}, u32[]{:S(2)}) collective-permute-start(bf16[256,2048]{1,0:T(8,128)(2,1)} %get-tuple-element.126), channel_id=1, source_target_pairs={{0,16},{8,24},{16,0},{24,8},{1,17},{9,25},{17,1},{25,9},{2,18},{10... | collective-permute-start | bytes 3145736 | tf_op jit(solution)/shard_map/ppermute | solution.py:17
  500.2 45.1 %collective-permute-start.49 = (bf16[640,512]{1,0:T(8,128)(2,1)}, bf16[640,512]{1,0:T(8,128)(2,1)}, u32[]{:S(2)}, u32[]{:S(2)}) collective-permute-start(bf16[640,512]{1,0:T(8,128)(2,1)} %get-tuple-element.160), channel_id=1, source_target_pairs={{0,8},{8,0},{16,24},{24,16},{1,9},{9,1},{17,25},{25,17},{2,10},{10... | collective-permute-start | bytes 1966088 | tf_op jit(solution)/shard_map/ppermute | solution.py:17
  501.3 44.8 %collective-permute-start.50 = (bf16[640,512]{1,0:T(8,128)(2,1)}, bf16[640,512]{1,0:T(8,128)(2,1)}, u32[]{:S(2)}, u32[]{:S(2)}) collective-permute-start(bf16[640,512]{1,0:T(8,128)(2,1)} %get-tuple-element.159), channel_id=1, source_target_pairs={{0,16},{8,24},{16,0},{24,8},{1,17},{9,25},{17,1},{25,9},{2,18},{10... | collective-permute-start | bytes 1966088 | tf_op jit(solution)/shard_map/ppermute | solution.py:17
  507.7 40.0 %collective-permute-start.51 = (bf16[640,512]{1,0:T(8,128)(2,1)}, bf16[640,512]{1,0:T(8,128)(2,1)}, u32[]{:S(2)}, u32[]{:S(2)}) collective-permute-start(bf16[640,512]{1,0:T(8,128)(2,1)} %get-tuple-element.158), channel_id=1, source_target_pairs={{0,24},{8,16},{16,8},{24,0},{1,25},{9,17},{17,9},{25,1},{2,26},{10... | collective-permute-start | bytes 1966088 | tf_op jit(solution)/shard_map/ppermute | solution.py:17
  509.8 58.9 %collective-permute-start.37 = (bf16[128,2048]{1,0:T(8,128)(2,1)}, bf16[128,2048]{1,0:T(8,128)(2,1)}, u32[]{:S(2)}, u32[]{:S(2)}) collective-permute-start(bf16[128,2048]{1,0:T(8,128)(2,1)} %get-tuple-element.137), channel_id=1, source_target_pairs={{0,8},{8,0},{16,24},{24,16},{1,9},{9,1},{17,25},{25,17},{2,10},{10... | collective-permute-start | bytes 1572872 | tf_op jit(solution)/shard_map/ppermute | solution.py:17
  520.1 68.3 %collective-permute-start.42 = (bf16[128,2048]{1,0:T(8,128)(2,1)}, bf16[128,2048]{1,0:T(8,128)(2,1)}, u32[]{:S(2)}, u32[]{:S(2)}) collective-permute-start(bf16[128,2048]{1,0:T(8,128)(2,1)} %get-tuple-element.138), channel_id=1, source_target_pairs={{0,16},{8,24},{16,0},{24,8},{1,17},{9,25},{17,1},{25,9},{2,18},{10... | collective-permute-start | bytes 1572872 | tf_op jit(solution)/shard_map/ppermute | solution.py:17
  574.0 27.8 %collective-permute-start.52 = (bf16[192,2048]{1,0:T(8,128)(2,1)}, bf16[192,2048]{1,0:T(8,128)(2,1)S(1)}, u32[]{:S(2)}, u32[]{:S(2)}) collective-permute-start(bf16[192,2048]{1,0:T(8,128)(2,1)} %reduce-scatter.5.cloned.1.call-done), channel_id=1, source_target_pairs={{0,8},{8,0},{16,24},{24,16},{1,9},{9,1},{17,25},{25,17},{2,10},{10... | collective-permute-start | bytes 2359304 | tf_op jit(solution)/shard_map/ppermute | solution.py:17
  575.2 28.2 %collective-permute-start.53 = (bf16[192,2048]{1,0:T(8,128)(2,1)}, bf16[192,2048]{1,0:T(8,128)(2,1)}, u32[]{:S(2)}, u32[]{:S(2)}) collective-permute-start(bf16[192,2048]{1,0:T(8,128)(2,1)} %reduce-scatter.5.cloned.1.call-done), channel_id=1, source_target_pairs={{0,16},{8,24},{16,0},{24,8},{1,17},{9,25},{17,1},{25,9},{2,18},{10... | collective-permute-start | bytes 2359304 | tf_op jit(solution)/shard_map/ppermute | solution.py:17
  588.3 181.7 %reduce-scatter.11.cloned.1.call-start = ((), (), s32[]{:S(2)}) async-start(), calls=%async_computation.11 | async-start | bytes 6488064 | tf_op jit(solution)/shard_map/reduce_scatter | solution.py:61
  617.3 69.6 %collective-permute-start.60 = (bf16[128,2048]{1,0:T(8,128)(2,1)}, bf16[128,2048]{1,0:T(8,128)(2,1)}, u32[]{:S(2)}, u32[]{:S(2)}) collective-permute-start(bf16[128,2048]{1,0:T(8,128)(2,1)} %get-tuple-element.131), channel_id=1, source_target_pairs={{0,8},{8,0},{16,24},{24,16},{1,9},{9,1},{17,25},{25,17},{2,10},{10... | collective-permute-start | bytes 1572872 | tf_op jit(solution)/shard_map/ppermute | solution.py:17
  618.7 97.3 %collective-permute-start.65 = (bf16[128,2048]{1,0:T(8,128)(2,1)}, bf16[128,2048]{1,0:T(8,128)(2,1)}, u32[]{:S(2)}, u32[]{:S(2)}) collective-permute-start(bf16[128,2048]{1,0:T(8,128)(2,1)} %get-tuple-element.132), channel_id=1, source_target_pairs={{0,16},{8,24},{16,0},{24,8},{1,17},{9,25},{17,1},{25,9},{2,18},{10... | collective-permute-start | bytes 1572872 | tf_op jit(solution)/shard_map/ppermute | solution.py:17
  632.4 24.1 %collective-permute-start.77 = (bf16[576,640]{1,0:T(8,128)(2,1)S(1)}, bf16[576,640]{1,0:T(8,128)(2,1)S(1)}, u32[]{:S(2)}, u32[]{:S(2)}) collective-permute-start(bf16[576,640]{1,0:T(8,128)(2,1)S(1)} %maximum_select_fusion), channel_id=1, source_target_pairs={{0,8},{8,0},{16,24},{24,16},{1,9},{9,1},{17,25},{25,17},{2,10},{10... | collective-permute-start | bytes 2211848 | tf_op jit(solution)/shard_map/ppermute | solution.py:17
  657.6 23.9 %collective-permute-start.79 = (bf16[288,640]{1,0:T(8,128)(2,1)}, bf16[288,640]{1,0:T(8,128)(2,1)}, u32[]{:S(2)}, u32[]{:S(2)}) collective-permute-start(bf16[288,640]{1,0:T(8,128)(2,1)} %slice.648), channel_id=1, source_target_pairs={{0,16},{8,24},{16,0},{24,8},{1,17},{9,25},{17,1},{25,9},{2,18},{10... | collective-permute-start | bytes 1105928 | tf_op jit(solution)/shard_map/ppermute | solution.py:17
  704.0 40.7 %collective-permute-start.71 = (bf16[256,3072]{1,0:T(8,128)(2,1)S(1)}, bf16[256,3072]{1,0:T(8,128)(2,1)S(1)}, u32[]{:S(2)}, u32[]{:S(2)}) collective-permute-start(bf16[256,3072]{1,0:T(8,128)(2,1)S(1)} %copy-done.50), channel_id=1, source_target_pairs={{0,8},{8,0},{16,24},{24,16},{1,9},{9,1},{17,25},{25,17},{2,10},{10... | collective-permute-start | bytes 4718600 | tf_op jit(solution)/shard_map/ppermute | solution.py:17
  706.0 39.4 %collective-permute-start.72 = (bf16[256,3072]{1,0:T(8,128)(2,1)S(1)}, bf16[256,3072]{1,0:T(8,128)(2,1)S(1)}, u32[]{:S(2)}, u32[]{:S(2)}) collective-permute-start(bf16[256,3072]{1,0:T(8,128)(2,1)S(1)} %copy-done.50), channel_id=1, source_target_pairs={{0,16},{8,24},{16,0},{24,8},{1,17},{9,25},{17,1},{25,9},{2,18},{10... | collective-permute-start | bytes 4718600 | tf_op jit(solution)/shard_map/ppermute | solution.py:17
  (121 other events, 1900.6 us)
Sparse Core Ops, SparseCore 0:
  11.3 63.1 all-gather.4
  76.7 32.5 all-gather.6
  111.5 63.7 all-gather.8
  193.9 116.6 all-gather.10
  352.9 71.6 reduce-scatter.4
  427.3 133.5 reduce-scatter.6
  588.4 36.7 reduce-scatter.8
  662.9 63.6 reduce-scatter.10

commit v4 on v3

--- a/solution.py
+++ b/solution.py
@@ -731,6 +731,7 @@
         name="recurrence_adjoint",
     )(grad_merged, h, y, decay)
     incoming = entering(back_cum[:, 0], back_local[:, 0], -1)
+    incoming = after(incoming, block_out)
     incoming8 = jnp.broadcast_to(incoming[:, None], (members, 8, own))
     grad_proj, tail, owed, small, tap_sums, gw_grad, gs_grad = pl.pallas_call(
         functools.partial(backward_kernel, head),
@@ -820,20 +821,21 @@
     partial = lax.optimization_barrier(partial.astype(bf16)).reshape(members, tokens, model)
     hop = first_hop(partial[3])
     out_sum = scatter_group(after(out_terms, mlp_sum, grad_proj))
+    mlp_hop = swap(mlp_sum, 1), swap(mlp_sum, 2)
     in_part = lax.dot_general(normed, grad_proj, down, preferred_element_type=f32).astype(bf16)
-    in_sum = scatter_group(after(in_part, out_sum, *hop))
+    in_sum = scatter_group(after(in_part, out_sum, *hop, *mlp_hop))
 
     out_blocks = gather_seq(out_sum)
     grad_normed = scatter_seq(partial, (after(hop[0], out_sum), after(hop[1], out_sum)))
-    mlp_late = after(mlp_sum, out_sum)
-    mlp_hop = swap(mlp_late, 1), swap(mlp_late, 2)
-    term_parts = gather_seq(after(group_terms, *hop))
+    term_parts = gather_seq(after(group_terms, grad_normed))
     gate_parts = [after(piece[: 2 * head], in_sum) for piece in term_parts]
-    small_parts = jnp.stack([piece[2 * head :].reshape(-1) for piece in term_parts])
+    small_parts = jnp.stack(
+        [after(piece[2 * head :], in_sum).reshape(-1) for piece in term_parts]
+    )
+    mlp_blocks = gather_seq(mlp_sum, mlp_hop)
     grad_input_norm, norm_gain_grad = rms_back(x32, norm_gain, grad_normed)
     input_grad = (grad_resid + grad_input_norm)[None]
 
-    mlp_blocks = gather_seq(mlp_late, mlp_hop)
     mlp_grad = spread(
         functools.partial(spread_mlp_kernel, (parts, per_part, fine)),
         mine,

time: 819 us -> 839 us (1.024)
  waiting for transfers between devices: 265 us -> 291 us
  starting transfers between devices: 122 us -> 110 us
    ppermute x66, waiting for transfers between devices: 211 us -> 244 us  [swap(): lax.ppermute(block, 'seq', [(i, i ^ k) for i in range(lax.axis_size('seq'...]
    ppermute x66, starting transfers between devices: 83 us -> 73.8 us  [swap(): lax.ppermute(block, 'seq', [(i, i ^ k) for i in range(lax.axis_size('seq'...]
    unnamed x143 -> x141, local copies, waits for them, and re-layouts: 28.1 us -> 30.6 us
  transfers between devices with their start and end apart: 97 -> 97, of which waited for: 43 -> 53; matrix products, arithmetic and copies ran while one was open for 36% -> 36% of each run, Pallas kernels for 7% -> 7%
where the time goes in v4:
time: 839 us; the launch traced here: 833 us
  waiting for transfers between devices  291 us (35%)
  local copies, waits for them, and re-layouts  130 us (15%)
  matrix products  129 us (15%)
  starting transfers between devices  110 us (13%)
  Pallas kernels  87.9 us (10%)
  other arithmetic  68.9 us (8%)
  between operations  16.2 us (2%)
    ppermute x66, waiting for transfers between devices, swap(): lax.ppermute(block, 'seq', [(i, i ^ k) for i in range(lax.axis_size('seq'...  244 us
    ppermute x66, starting transfers between devices, swap(): lax.ppermute(block, 'seq', [(i, i ^ k) for i in range(lax.axis_size('seq'...  73.8 us
    unnamed x141, local copies, waits for them, and re-layouts  30.6 us
    ppermute x12, starting transfers between devices, shift(): lax.ppermute(block, 'group', [(i - distance, i) for i in devices if i - d...  27.8 us
    pallas_call x1, Pallas kernels, shards(): pl.pallas_call(mlp_kernel, grid=(parts,), in_specs=[whole(rows, model), p...  21.2 us
    dot_general x1, matrix products, shards(): lax.dot_general(hidden_low, c_all, down, preferred_element_type=f32)  21.1 us
    dot_general x1, matrix products, shards(): lax.dot_general(normed2, after(grad_gu, partial), down, preferred_element...  19.4 us
    pallas_call x1, Pallas kernels, shards(): pl.pallas_call(functools.partial(backward_kernel, head), grid=(members,),...  18.6 us
  transfers between devices with their start and end apart: 97, of which 53 were waited for; matrix products, arithmetic and copies ran while one was open for 36% of the time, Pallas kernels for 7%

profile of v4, /device:TPU:0, one launch (start us, length us, event | category | flops | bytes accessed | tf_op | source)
XLA Modules:
  0.0 833.2 jit_solution(6483979585992680058)
XLA Ops:
  19.8 17.9 %collective-permute-done = bf16[256,2048]{1,0:T(8,128)(2,1)} collective-permute-done((bf16[256,2048]{1,0:T(8,128)(2,1)}, bf16[256,2048]{1,0:T(8,128)(2,1)}, u32[]{:S(2)}, u32[]{:S(2)}) %collective-permute-start) | collective-permute-done | bytes 1048608 | tf_op jit(solution)/shard_map/ppermute | solution.py:17
  47.1 8.7 %copy.38 = bf16[256,12288]{0,1:T(8,128)(2,1)} copy(bf16[256,12288]{1,0:T(8,128)(2,1)} %param.24) | data formatting | bytes 12582912 | tf_op jit(solution)/shard_map/optimization_barrier | solution.py:65
  78.6 8.2 fusion.3
  86.8 13.5 %collective-permute-done.4 = bf16[256,2048]{1,0:T(8,128)(2,1)} collective-permute-done((bf16[256,2048]{1,0:T(8,128)(2,1)}, bf16[256,2048]{1,0:T(8,128)(2,1)}, u32[]{:S(2)}, u32[]{:S(2)}) %collective-permute-start.4) | collective-permute-done | bytes 1048608 | tf_op jit(solution)/shard_map/ppermute | solution.py:17
  101.5 7.9 all-gather.7.cloned.1.call-done
  124.1 14.5 %recurrence_forward.1 = (f32[4,256,768]{2,1,0:T(8,128)}, f32[4,256,640]{2,1,0:T(8,128)}, f32[4,256,640]{2,1,0:T(8,128)}, f32[4,256,640]{2,1,0:T(8,128)}, f32[4,256,640]{2,1,0:T(8,128)}, /*index=5*/f32[4,256,640]{2,1,0:T(8,128)}) custom-call(s32[1]{0:T(128)} %bitcast.1.odd_ref, f32[4,256,768]{2,1,0:T(8,128)} %bitcast.234, f32[4,8,768]{2,1,0:T(8,128)} %pad.17.rim_ref, ...), custom_call_target="tpu_custom_call" | custom-call | flops 14000000000 | bytes 42000000 | tf_op jit(solution)/shard_map/recurrence_forward/pallas_call | solution.py:614
  139.6 8.4 %collective-permute-start.10 = (f32[2,4,640]{2,0,1:T(2,128)S(1)}, f32[2,4,640]{2,0,1:T(2,128)S(1)}, u32[]{:S(2)}, u32[]{:S(2)}) collective-permute-start(f32[2,4,640]{2,0,1:T(2,128)S(1)} %pad_maximum_fusion.13), channel_id=1, source_target_pairs={{0,4},{1,5},{2,6},{3,7},{8,12},{9,13},{10,14},{11,15},{16,20},{17,... | collective-permute-start | bytes 61448 | tf_op jit(solution)/shard_map/ppermute | solution.py:22
  175.2 13.0 %collective-permute-done.13 = bf16[640,512]{1,0:T(8,128)(2,1)} collective-permute-done((bf16[640,512]{1,0:T(8,128)(2,1)}, bf16[640,512]{1,0:T(8,128)(2,1)}, u32[]{:S(2)}, u32[]{:S(2)}) %collective-permute-start.13) | collective-permute-done | bytes 655392 | tf_op jit(solution)/shard_map/ppermute | solution.py:17
  194.2 7.9 fusion.5
  202.8 6.7 recurrence_merge.1
  218.5 11.8 %collective-permute-done.16 = bf16[128,2048]{1,0:T(8,128)(2,1)S(1)} collective-permute-done((bf16[128,2048]{1,0:T(8,128)(2,1)S(1)}, bf16[128,2048]{1,0:T(8,128)(2,1)S(1)}, u32[]{:S(2)}, u32[]{:S(2)}) %collective-permute-start.16) | collective-permute-done | bytes 524320 | tf_op jit(solution)/shard_map/ppermute | solution.py:17
  247.9 6.8 collective-permute-done.21
  261.5 8.6 %fusion.56.grad_ref = f32[1024,1536]{1,0:T(8,128)} fusion(bf16[1024,2048]{1,0:T(8,128)(2,1)S(1)} %constant_dynamic-update-slice_fusion.5, bf16[1536,2048]{1,0:T(8,128)(2,1)S(1)} %bitcast.237), kind=kOutput, calls=%fused_computation.261 | convolution fusion | flops 6442450944 | bytes 16777216 | tf_op jit(solution)/shard_map/dot_general | solution.py:663
  273.7 18.8 %collective-permute-done.23 = bf16[256,2048]{1,0:T(8,128)(2,1)S(1)} collective-permute-done((bf16[256,2048]{1,0:T(8,128)(2,1)S(1)}, bf16[256,2048]{1,0:T(8,128)(2,1)S(1)}, u32[]{:S(2)}, u32[]{:S(2)}) %collective-permute-start.23) | collective-permute-done | bytes 1048608 | tf_op jit(solution)/shard_map/ppermute | solution.py:17
  310.3 21.2 %mlp.1 = (bf16[1024,1536]{1,0:T(8,128)(2,1)}, bf16[1024,3072]{1,0:T(8,128)(2,1)}) custom-call(bf16[1024,2048]{1,0:T(8,128)(2,1)} %constant_dynamic-update-slice_fusion.10.normed_ref, bf16[2048,3072]{1,0:T(8,128)(2,1)} %all-gather.11.cloned.1.call-done.weight_ref, f32[1024,1536]{1,0:T(8,128)} %fusion.56.grad_ref), custom_call_target="tpu_custom_call" | custom-call | flops 12884901888 | bytes 32505856 | tf_op jit(solution)/shard_map/mlp/pallas_call | solution.py:670
  331.5 21.1 %convolution_convert_fusion.2 = bf16[1536,2048]{1,0:T(8,128)(2,1)} fusion(bf16[1024,1536]{1,0:T(8,128)(2,1)} %get-tuple-element.83, bf16[1024,2048]{1,0:T(8,128)(2,1)} %copy-done.35), kind=kOutput, calls=%fused_computation.7 | convolution fusion | flops 6445596672 | bytes 13631488 | tf_op jit(solution)/shard_map/dot_general | solution.py:696
  352.7 17.6 %convolution_convert_fusion.3 = bf16[1024,2048]{1,0:T(8,128)(2,1)S(1)} fusion(bf16[1024,3072]{1,0:T(8,128)(2,1)} %get-tuple-element.82, bf16[2048,3072]{1,0:T(8,128)(2,1)} %all-gather.11.cloned.1.call-done.weight_ref), kind=kOutput, calls=%fused_computation.13 | convolution fusion | flops 12886999040 | bytes 23068672 | tf_op jit(solution)/shard_map/dot_general | solution.py:698
  375.0 11.2 %collective-permute-done.28 = bf16[128,2048]{1,0:T(8,128)(2,1)S(1)} collective-permute-done((bf16[128,2048]{1,0:T(8,128)(2,1)S(1)}, bf16[128,2048]{1,0:T(8,128)(2,1)S(1)}, u32[]{:S(2)}, u32[]{:S(2)}) %collective-permute-start.28) | collective-permute-done | bytes 524320 | tf_op jit(solution)/shard_map/ppermute | solution.py:17
  387.9 19.4 %convolution_convert_fusion = bf16[2048,3072]{1,0:T(8,128)(2,1)} fusion(bf16[1024,2048]{1,0:T(8,128)(2,1)} %constant_dynamic-update-slice_fusion.10.normed_ref, bf16[1024,3072]{1,0:T(8,128)(2,1)} %get-tuple-element.82), kind=kOutput, calls=%fused_computation | convolution fusion | flops 12891193344 | bytes 23068672 | tf_op jit(solution)/shard_map/dot_general | solution.py:701
  411.9 11.5 %convolution_convert_fusion.4 = bf16[1024,2048]{1,0:T(8,128)(2,1)} fusion(bf16[1024,1536]{1,0:T(8,128)(2,1)S(1)} %copy-done.54, bf16[1536,2048]{1,0:T(8,128)(2,1)} %all-gather.9.cloned.1.call-done), kind=kOutput, calls=%fused_computation.14 | convolution fusion | flops 6444548096 | bytes 13631488 | tf_op jit(solution)/shard_map/dot_general | solution.py:705
  434.0 19.9 %collective-permute-done.33 = bf16[256,2048]{1,0:T(8,128)(2,1)S(1)} collective-permute-done((bf16[256,2048]{1,0:T(8,128)(2,1)}, bf16[256,2048]{1,0:T(8,128)(2,1)S(1)}, u32[]{:S(2)}, u32[]{:S(2)}) %collective-permute-start.33) | collective-permute-done | bytes 1048608 | tf_op jit(solution)/shard_map/ppermute | solution.py:17
  485.6 10.2 %recurrence_adjoint.1 = (f32[4,256,640]{2,1,0:T(8,128)}, bf16[4,256,640]{2,1,0:T(8,128)(2,1)}, f32[4,256,640]{2,1,0:T(8,128)}, f32[4,256,640]{2,1,0:T(8,128)}) custom-call(f32[4,256,640]{2,1,0:T(8,128)} %bitcast.242, f32[4,256,640]{2,1,0:T(8,128)} %get-tuple-element.87.h_ref, f32[4,256,640]{2,1,0:T(8,128)} %bitcast.241, ...), custom_call_target="tpu_custom_call" | custom-call | flops 10000000000 | bytes 30000000 | tf_op jit(solution)/shard_map/recurrence_adjoint/pallas_call | solution.py:723
  525.3 18.6 %recurrence_backward.1 = (bf16[4,256,1408]{2,1,0:T(8,128)(2,1)}, f32[4,8,768]{2,1,0:T(8,128)}, f32[4,8,768]{2,1,0:T(8,128)}, f32[8,640]{1,0:T(8,128)}, f32[8,768...) custom-call(s32[1]{0:T(128)} %bitcast.1.odd_ref, f32[4,256,640]{2,1,0:T(8,128)} %get-tuple-element.89.back_ref, ...), custom_call_target="tpu_custom_call" | custom-call | flops 19000000512 | bytes 57000000 | tf_op jit(solution)/shard_map/recurrence_backward/pallas_call | solution.py:736
  583.5 10.3 %collective-permute-done.52 = bf16[192,2048]{1,0:T(8,128)(2,1)} collective-permute-done((bf16[192,2048]{1,0:T(8,128)(2,1)}, bf16[192,2048]{1,0:T(8,128)(2,1)}, u32[]{:S(2)}, u32[]{:S(2)}) %collective-permute-start.52) | collective-permute-done | bytes 786464 | tf_op jit(solution)/shard_map/ppermute | solution.py:17
  594.4 10.4 %convolution_convert_fusion.5 = bf16[1024,2048]{1,0:T(8,128)(2,1)S(1)} fusion(bf16[1024,1408]{1,0:T(8,128)(2,1)} %bitcast.238, bf16[2048,1408]{1,0:T(8,128)(2,1)} %all-gather.5.cloned.1.call-done), kind=kOutput, calls=%fused_computation.15 | convolution fusion | flops 5907677184 | bytes 12845056 | tf_op jit(solution)/shard_map/dot_general | solution.py:818
  612.2 8.6 %convolution_convert_fusion.1 = bf16[2048,1408]{1,0:T(8,128)(2,1)} fusion(bf16[1024,2048]{1,0:T(8,128)(2,1)S(1)} %copy-done.17, bf16[1024,1408]{1,0:T(8,128)(2,1)S(1)} %bitcast.239), kind=kOutput, calls=%fused_computation.6 | convolution fusion | flops 5908463616 | bytes 12845056 | tf_op jit(solution)/shard_map/dot_general | solution.py:825
  624.5 30.2 %collective-permute-done.71.b_ref = bf16[256,3072]{1,0:T(8,128)(2,1)} collective-permute-done((bf16[256,3072]{1,0:T(8,128)(2,1)}, bf16[256,3072]{1,0:T(8,128)(2,1)}, u32[]{:S(2)}, u32[]{:S(2)}) %collective-permute-start.71) | collective-permute-done | bytes 1572896 | tf_op jit(solution)/shard_map/ppermute | solution.py:17
  657.1 14.7 %collective-permute-done.77 = bf16[576,640]{1,0:T(8,128)(2,1)S(1)} collective-permute-done((bf16[576,640]{1,0:T(8,128)(2,1)S(1)}, bf16[576,640]{1,0:T(8,128)(2,1)S(1)}, u32[]{:S(2)}, u32[]{:S(2)}) %collective-permute-start.77) | collective-permute-done | bytes 737312 | tf_op jit(solution)/shard_map/ppermute | solution.py:17
  706.4 12.9 %collective-permute-done.86 = bf16[128,3072]{1,0:T(8,128)(2,1)S(1)} collective-permute-done((bf16[128,3072]{1,0:T(8,128)(2,1)S(1)}, bf16[128,3072]{1,0:T(8,128)(2,1)S(1)}, u32[]{:S(2)}, u32[]{:S(2)}) %collective-permute-start.86) | collective-permute-done | bytes 786464 | tf_op jit(solution)/shard_map/ppermute | solution.py:17
  728.7 8.1 collective-permute-done.74
  742.1 9.9 %spread_mlp.1 = f32[256,12288]{1,0:T(8,128)} custom-call(s32[1]{0:T(128)} %bitcast.36.mine_ref, bf16[256,3072]{1,0:T(8,128)(2,1)} %reduce-scatter.7.cloned.1.call-done.a_ref, bf16[256,3072]{1,0:T(8,128)(2,1)} %collective-permute-done.71.b_ref, bf16[256,3072]{1,0:T(8,128)(2,1)} %collective-permute-done.72.c_ref, bf16[256,3072]{1,0:T(8,128)(2,1)} %pad_maximum_fusion.4.d_ref), custom_call_target="tpu_custom_call" | custom-call | flops 8000000000 | bytes 24000000 | tf_op jit(solution)/shard_map/spread_mlp/pallas_call | solution.py:473
  819.2 6.9 spread_in.1
  (557 shorter events, 401.6 us)
Async XLA Ops:
  7.2 67.3 %all-gather.5.cloned.1.call-start = ((), (), s32[]{:S(2)}) async-start(), calls=%async_computation.4 | async-start | bytes 6488064 | tf_op jit(solution)/shard_map/all_gather | solution.py:57
  11.2 98.1 %all-gather.7.cloned.1.call-start = ((), (), s32[]{:S(2)}) async-start(), calls=%async_computation.5 | async-start | bytes 2949120 | tf_op jit(solution)/shard_map/all_gather | solution.py:57
  11.3 26.5 %collective-permute-start = (bf16[256,2048]{1,0:T(8,128)(2,1)}, bf16[256,2048]{1,0:T(8,128)(2,1)}, u32[]{:S(2)}, u32[]{:S(2)}) collective-permute-start(bf16[256,2048]{1,0:T(8,128)(2,1)} %bitcast.192), channel_id=1, source_target_pairs={{0,8},{8,0},{16,24},{24,16},{1,9},{9,1},{17,25},{25,17},{2,10},{10... | collective-permute-start | bytes 3145736 | tf_op jit(solution)/shard_map/ppermute | solution.py:17
  14.3 27.1 %collective-permute-start.1 = (bf16[256,2048]{1,0:T(8,128)(2,1)}, bf16[256,2048]{1,0:T(8,128)(2,1)}, u32[]{:S(2)}, u32[]{:S(2)}) collective-permute-start(bf16[256,2048]{1,0:T(8,128)(2,1)} %bitcast.193), channel_id=1, source_target_pairs={{0,16},{8,24},{16,0},{24,8},{1,17},{9,25},{17,1},{25,9},{2,18},{10... | collective-permute-start | bytes 3145736 | tf_op jit(solution)/shard_map/ppermute | solution.py:17
  74.5 117.6 %all-gather.9.cloned.1.call-start = ((), (), s32[]{:S(2)}) async-start(), calls=%async_computation.6 | async-start | bytes 7077888 | tf_op jit(solution)/shard_map/all_gather | solution.py:57
  74.6 25.7 %collective-permute-start.4 = (bf16[256,2048]{1,0:T(8,128)(2,1)}, bf16[256,2048]{1,0:T(8,128)(2,1)}, u32[]{:S(2)}, u32[]{:S(2)}) collective-permute-start(bf16[256,2048]{1,0:T(8,128)(2,1)} %bitcast.195), channel_id=1, source_target_pairs={{0,8},{8,0},{16,24},{24,16},{1,9},{9,1},{17,25},{25,17},{2,10},{10... | collective-permute-start | bytes 3145736 | tf_op jit(solution)/shard_map/ppermute | solution.py:17
  76.1 25.3 %collective-permute-start.5 = (bf16[256,2048]{1,0:T(8,128)(2,1)}, bf16[256,2048]{1,0:T(8,128)(2,1)}, u32[]{:S(2)}, u32[]{:S(2)}) collective-permute-start(bf16[256,2048]{1,0:T(8,128)(2,1)} %bitcast.196), channel_id=1, source_target_pairs={{0,16},{8,24},{16,0},{24,8},{1,17},{9,25},{17,1},{25,9},{2,18},{10... | collective-permute-start | bytes 3145736 | tf_op jit(solution)/shard_map/ppermute | solution.py:17
  109.3 201.0 %all-gather.11.cloned.1.call-start = ((), (), s32[]{:S(2)}) async-start(), calls=%async_computation.7 | async-start | bytes 14155776 | tf_op jit(solution)/shard_map/all_gather | solution.py:57
  157.9 30.3 %collective-permute-start.13 = (bf16[640,512]{1,0:T(8,128)(2,1)}, bf16[640,512]{1,0:T(8,128)(2,1)}, u32[]{:S(2)}, u32[]{:S(2)}) collective-permute-start(bf16[640,512]{1,0:T(8,128)(2,1)} %pad_maximum_fusion.10), channel_id=1, source_target_pairs={{0,16},{8,24},{16,0},{24,8},{1,17},{9,25},{17,1},{25,9},{2,18},{10... | collective-permute-start | bytes 1966088 | tf_op jit(solution)/shard_map/ppermute | solution.py:17
  160.2 29.9 %collective-permute-start.14 = (bf16[640,512]{1,0:T(8,128)(2,1)}, bf16[640,512]{1,0:T(8,128)(2,1)}, u32[]{:S(2)}, u32[]{:S(2)}) collective-permute-start(bf16[640,512]{1,0:T(8,128)(2,1)} %pad_maximum_fusion.11), channel_id=1, source_target_pairs={{0,24},{8,16},{16,8},{24,0},{1,25},{9,17},{17,9},{25,1},{2,26},{10... | collective-permute-start | bytes 1966088 | tf_op jit(solution)/shard_map/ppermute | solution.py:17
  193.9 232.3 %reduce-scatter.5.cloned.1.call-start = ((), (), s32[]{:S(2)}) async-start(), calls=%async_computation.8 | async-start | bytes 7077888 | tf_op jit(solution)/shard_map/reduce_scatter | solution.py:61
  215.8 25.7 %collective-permute-start.15 = (bf16[128,2048]{1,0:T(8,128)(2,1)S(1)}, bf16[128,2048]{1,0:T(8,128)(2,1)S(1)}, u32[]{:S(2)}, u32[]{:S(2)}) collective-permute-start(bf16[128,2048]{1,0:T(8,128)(2,1)S(1)} %get-tuple-element.157), channel_id=1, source_target_pairs={{0,8},{8,0},{16,24},{24,16},{1,9},{9,1},{17,25},{25,17},{2,10},{10... | collective-permute-start | bytes 1572872 | tf_op jit(solution)/shard_map/ppermute | solution.py:17
  217.4 25.2 %collective-permute-start.18 = (bf16[128,2048]{1,0:T(8,128)(2,1)S(1)}, bf16[128,2048]{1,0:T(8,128)(2,1)S(1)}, u32[]{:S(2)}, u32[]{:S(2)}) collective-permute-start(bf16[128,2048]{1,0:T(8,128)(2,1)S(1)} %get-tuple-element.159), channel_id=1, source_target_pairs={{0,16},{8,24},{16,0},{24,8},{1,17},{9,25},{17,1},{25,9},{2,18},{10... | collective-permute-start | bytes 1572872 | tf_op jit(solution)/shard_map/ppermute | solution.py:17
  272.3 24.3 %collective-permute-start.24 = (bf16[256,2048]{1,0:T(8,128)(2,1)S(1)}, bf16[256,2048]{1,0:T(8,128)(2,1)S(1)}, u32[]{:S(2)}, u32[]{:S(2)}) collective-permute-start(bf16[256,2048]{1,0:T(8,128)(2,1)S(1)} %get-tuple-element.136), channel_id=1, source_target_pairs={{0,16},{8,24},{16,0},{24,8},{1,17},{9,25},{17,1},{25,9},{2,18},{10... | collective-permute-start | bytes 3145736 | tf_op jit(solution)/shard_map/ppermute | solution.py:17
  352.6 224.0 %reduce-scatter.7.cloned.1.call-start = ((), (), s32[]{:S(2)}) async-start(), calls=%async_computation.9 | async-start | bytes 14155776 | tf_op jit(solution)/shard_map/reduce_scatter | solution.py:61
  372.9 35.0 %collective-permute-start.27 = (bf16[128,2048]{1,0:T(8,128)(2,1)}, bf16[128,2048]{1,0:T(8,128)(2,1)}, u32[]{:S(2)}, u32[]{:S(2)}) collective-permute-start(bf16[128,2048]{1,0:T(8,128)(2,1)} %get-tuple-element.151), channel_id=1, source_target_pairs={{0,8},{8,0},{16,24},{24,16},{1,9},{9,1},{17,25},{25,17},{2,10},{10... | collective-permute-start | bytes 1572872 | tf_op jit(solution)/shard_map/ppermute | solution.py:17
  373.5 34.4 %collective-permute-start.30 = (bf16[128,2048]{1,0:T(8,128)(2,1)}, bf16[128,2048]{1,0:T(8,128)(2,1)}, u32[]{:S(2)}, u32[]{:S(2)}) collective-permute-start(bf16[128,2048]{1,0:T(8,128)(2,1)} %get-tuple-element.153), channel_id=1, source_target_pairs={{0,16},{8,24},{16,0},{24,8},{1,17},{9,25},{17,1},{25,9},{2,18},{10... | collective-permute-start | bytes 1572872 | tf_op jit(solution)/shard_map/ppermute | solution.py:17
  426.3 229.4 %reduce-scatter.9.cloned.1.call-start = ((), (), s32[]{:S(2)}) async-start(), calls=%async_computation.10 | async-start | bytes 2949120 | tf_op jit(solution)/shard_map/reduce_scatter | solution.py:61
  431.3 24.8 %collective-permute-start.34 = (bf16[256,2048]{1,0:T(8,128)(2,1)}, bf16[256,2048]{1,0:T(8,128)(2,1)}, u32[]{:S(2)}, u32[]{:S(2)}) collective-permute-start(bf16[256,2048]{1,0:T(8,128)(2,1)} %get-tuple-element.134), channel_id=1, source_target_pairs={{0,16},{8,24},{16,0},{24,8},{1,17},{9,25},{17,1},{25,9},{2,18},{10... | collective-permute-start | bytes 3145736 | tf_op jit(solution)/shard_map/ppermute | solution.py:17
  482.1 36.9 %collective-permute-start.42 = (bf16[128,2048]{1,0:T(8,128)(2,1)}, bf16[128,2048]{1,0:T(8,128)(2,1)S(1)}, u32[]{:S(2)}, u32[]{:S(2)}) collective-permute-start(bf16[128,2048]{1,0:T(8,128)(2,1)} %get-tuple-element.146), channel_id=1, source_target_pairs={{0,16},{8,24},{16,0},{24,8},{1,17},{9,25},{17,1},{25,9},{2,18},{10... | collective-permute-start | bytes 1572872 | tf_op jit(solution)/shard_map/ppermute | solution.py:17
  513.0 35.8 %collective-permute-start.51 = (bf16[640,512]{1,0:T(8,128)(2,1)}, bf16[640,512]{1,0:T(8,128)(2,1)}, u32[]{:S(2)}, u32[]{:S(2)}) collective-permute-start(bf16[640,512]{1,0:T(8,128)(2,1)} %get-tuple-element.166), channel_id=1, source_target_pairs={{0,24},{8,16},{16,8},{24,0},{1,25},{9,17},{17,9},{25,1},{2,26},{10... | collective-permute-start | bytes 1966088 | tf_op jit(solution)/shard_map/ppermute | solution.py:17
  514.7 34.1 %collective-permute-start.50 = (bf16[640,512]{1,0:T(8,128)(2,1)}, bf16[640,512]{1,0:T(8,128)(2,1)}, u32[]{:S(2)}, u32[]{:S(2)}) collective-permute-start(bf16[640,512]{1,0:T(8,128)(2,1)} %get-tuple-element.167), channel_id=1, source_target_pairs={{0,16},{8,24},{16,0},{24,8},{1,17},{9,25},{17,1},{25,9},{2,18},{10... | collective-permute-start | bytes 1966088 | tf_op jit(solution)/shard_map/ppermute | solution.py:17
  517.9 30.9 %collective-permute-start.49 = (bf16[640,512]{1,0:T(8,128)(2,1)}, bf16[640,512]{1,0:T(8,128)(2,1)}, u32[]{:S(2)}, u32[]{:S(2)}) collective-permute-start(bf16[640,512]{1,0:T(8,128)(2,1)} %get-tuple-element.168), channel_id=1, source_target_pairs={{0,8},{8,0},{16,24},{24,16},{1,9},{9,1},{17,25},{25,17},{2,10},{10... | collective-permute-start | bytes 1966088 | tf_op jit(solution)/shard_map/ppermute | solution.py:17
  576.6 196.9 %reduce-scatter.11.cloned.1.call-start = ((), (), s32[]{:S(2)}) async-start(), calls=%async_computation.11 | async-start | bytes 6488064 | tf_op jit(solution)/shard_map/reduce_scatter | solution.py:61
  610.1 44.7 %collective-permute-start.71 = (bf16[256,3072]{1,0:T(8,128)(2,1)}, bf16[256,3072]{1,0:T(8,128)(2,1)}, u32[]{:S(2)}, u32[]{:S(2)}) collective-permute-start(bf16[256,3072]{1,0:T(8,128)(2,1)} %reduce-scatter.7.cloned.1.call-done.a_ref), channel_id=1, source_target_pairs={{0,8},{8,0},{16,24},{24,16},{1,9},{9,1},{17,25},{25,17},{2,10},{10... | collective-permute-start | bytes 4718600 | tf_op jit(solution)/shard_map/ppermute | solution.py:17
  610.9 44.8 %collective-permute-start.72 = (bf16[256,3072]{1,0:T(8,128)(2,1)}, bf16[256,3072]{1,0:T(8,128)(2,1)}, u32[]{:S(2)}, u32[]{:S(2)}) collective-permute-start(bf16[256,3072]{1,0:T(8,128)(2,1)} %reduce-scatter.7.cloned.1.call-done.a_ref), channel_id=1, source_target_pairs={{0,16},{8,24},{16,0},{24,8},{1,17},{9,25},{17,1},{25,9},{2,18},{10... | collective-permute-start | bytes 4718600 | tf_op jit(solution)/shard_map/ppermute | solution.py:17
  686.7 67.4 %collective-permute-start.65 = (bf16[128,2048]{1,0:T(8,128)(2,1)}, bf16[128,2048]{1,0:T(8,128)(2,1)S(1)}, u32[]{:S(2)}, u32[]{:S(2)}) collective-permute-start(bf16[128,2048]{1,0:T(8,128)(2,1)} %get-tuple-element.140), channel_id=1, source_target_pairs={{0,16},{8,24},{16,0},{24,8},{1,17},{9,25},{17,1},{25,9},{2,18},{10... | collective-permute-start | bytes 1572872 | tf_op jit(solution)/shard_map/ppermute | solution.py:17
  688.3 50.3 %collective-permute-start.60 = (bf16[128,2048]{1,0:T(8,128)(2,1)S(1)}, bf16[128,2048]{1,0:T(8,128)(2,1)S(1)}, u32[]{:S(2)}, u32[]{:S(2)}) collective-permute-start(bf16[128,2048]{1,0:T(8,128)(2,1)S(1)} %copy-done.30), channel_id=1, source_target_pairs={{0,8},{8,0},{16,24},{24,16},{1,9},{9,1},{17,25},{25,17},{2,10},{10... | collective-permute-start | bytes 1572872 | tf_op jit(solution)/shard_map/ppermute | solution.py:17
  702.7 35.9 %collective-permute-start.62 = (bf16[128,2048]{1,0:T(8,128)(2,1)S(1)}, bf16[128,2048]{1,0:T(8,128)(2,1)S(1)}, u32[]{:S(2)}, u32[]{:S(2)}) collective-permute-start(bf16[128,2048]{1,0:T(8,128)(2,1)S(1)} %add_convert_fusion.1), channel_id=1, source_target_pairs={{0,16},{8,24},{16,0},{24,8},{1,17},{9,25},{17,1},{25,9},{2,18},{10... | collective-permute-start | bytes 1572872 | tf_op jit(solution)/shard_map/ppermute | solution.py:17
  727.1 25.0 %collective-permute-start.75 = (bf16[160,512]{1,0:T(8,128)(2,1)}, bf16[160,512]{1,0:T(8,128)(2,1)}, u32[]{:S(2)}, u32[]{:S(2)}) collective-permute-start(bf16[160,512]{1,0:T(8,128)(2,1)} %slice.646), channel_id=1, source_target_pairs={{0,16},{8,24},{16,0},{24,8},{1,17},{9,25},{17,1},{25,9},{2,18},{10... | collective-permute-start | bytes 491528 | tf_op jit(solution)/shard_map/ppermute | solution.py:17
  773.5 36.3 %collective-permute-start.81 = (bf16[256,1408]{1,0:T(8,128)(2,1)}, bf16[256,1408]{1,0:T(8,128)(2,1)}, u32[]{:S(2)}, u32[]{:S(2)}) collective-permute-start(bf16[256,1408]{1,0:T(8,128)(2,1)} %reduce-scatter.11.cloned.1.call-done.a_ref), channel_id=1, source_target_pairs={{0,8},{8,0},{16,24},{24,16},{1,9},{9,1},{17,25},{25,17},{2,10},{10... | collective-permute-start | bytes 2162696 | tf_op jit(solution)/shard_map/ppermute | solution.py:17
  774.6 33.2 %collective-permute-start.82 = (bf16[256,1408]{1,0:T(8,128)(2,1)}, bf16[256,1408]{1,0:T(8,128)(2,1)}, u32[]{:S(2)}, u32[]{:S(2)}) collective-permute-start(bf16[256,1408]{1,0:T(8,128)(2,1)} %reduce-scatter.11.cloned.1.call-done.a_ref), channel_id=1, source_target_pairs={{0,16},{8,24},{16,0},{24,8},{1,17},{9,25},{17,1},{25,9},{2,18},{10... | collective-permute-start | bytes 2162696 | tf_op jit(solution)/shard_map/ppermute | solution.py:17
  (125 other events, 1543.2 us)
Sparse Core Ops, SparseCore 0:
  11.3 63.1 all-gather.4
  76.7 32.5 all-gather.6
  111.5 63.7 all-gather.8
  194.0 116.2 all-gather.10
  352.7 69.4 reduce-scatter.4
  426.4 129.7 reduce-scatter.6
  576.8 36.7 reduce-scatter.8
  655.8 62.7 reduce-scatter.10

commit v5 on v3

--- a/solution.py
+++ b/solution.py
@@ -882,7 +882,7 @@
         tap_grads = tap_grads + place(one.reshape(-1, wide), member, True)
         own_grads = own_grads + place(two.reshape(-1, own), member, False)
         mlp_gain_grad = mlp_gain_grad + three
-    norm_gain_grad = total(norm_gain_grad.reshape(-1, 128)).reshape(-1)
+    norm_gain_grad = total(after(norm_gain_grad, *mlp_blocks).reshape(-1, 128)).reshape(-1)
     in_grad = spread(
         functools.partial(spread_in_kernel, head), mine, gather_seq(after(in_sum, *mlp_hop, *out_blocks, *term_parts)), 2 * rec, "spread_in"
     )

time: 819 us -> 850 us (1.038)
  waiting for transfers between devices: 265 us -> 302 us
    ppermute x66, waiting for transfers between devices: 211 us -> 261 us  [swap(): lax.ppermute(block, 'seq', [(i, i ^ k) for i in range(lax.axis_size('seq'...]
    ppermute x5, waiting for transfers between devices: 18.3 us -> 5.52 us  [total(): lax.ppermute(value, axis, [(i, i ^ step) for i in range(count)])]
    unnamed x143 -> x158, local copies, waits for them, and re-layouts: 28.1 us -> 29.2 us
  transfers between devices with their start and end apart: 97 -> 97, of which waited for: 43 -> 43; matrix products, arithmetic and copies ran while one was open for 36% -> 34% of each run, Pallas kernels for 7% -> 7%
where the time goes in v5:
time: 850 us; the launch traced here: 844 us
  waiting for transfers between devices  302 us (36%)
  matrix products  129 us (15%)
  local copies, waits for them, and re-layouts  123 us (14%)
  starting transfers between devices  117 us (14%)
  Pallas kernels  87.7 us (10%)
  other arithmetic  69.2 us (8%)
  between operations  16.4 us (2%)
    ppermute x66, waiting for transfers between devices, swap(): lax.ppermute(block, 'seq', [(i, i ^ k) for i in range(lax.axis_size('seq'...  261 us
    ppermute x66, starting transfers between devices, swap(): lax.ppermute(block, 'seq', [(i, i ^ k) for i in range(lax.axis_size('seq'...  78.3 us
    unnamed x158, local copies, waits for them, and re-layouts  29.2 us
    ppermute x12, starting transfers between devices, shift(): lax.ppermute(block, 'group', [(i - distance, i) for i in devices if i - d...  28.6 us
    pallas_call x1, Pallas kernels, shards(): pl.pallas_call(mlp_kernel, grid=(parts,), in_specs=[whole(rows, model), p...  21.2 us
    dot_general x1, matrix products, shards(): lax.dot_general(hidden_low, c_all, down, preferred_element_type=f32)  21.1 us
    dot_general x1, matrix products, shards(): lax.dot_general(normed2, after(grad_gu, partial), down, preferred_element...  19.4 us
    pallas_call x1, Pallas kernels, shards(): pl.pallas_call(functools.partial(backward_kernel, head), grid=(members,),...  18.3 us
  transfers between devices with their start and end apart: 97, of which 43 were waited for; matrix products, arithmetic and copies ran while one was open for 34% of the time, Pallas kernels for 7%

profile of v5, /device:TPU:0, one launch (start us, length us, event | category | flops | bytes accessed | tf_op | source)
XLA Modules:
  0.0 843.8 jit_solution(7299749146910235910)
XLA Ops:
  19.8 17.9 %collective-permute-done = bf16[256,2048]{1,0:T(8,128)(2,1)} collective-permute-done((bf16[256,2048]{1,0:T(8,128)(2,1)}, bf16[256,2048]{1,0:T(8,128)(2,1)}, u32[]{:S(2)}, u32[]{:S(2)}) %collective-permute-start) | collective-permute-done | bytes 1048608 | tf_op jit(solution)/shard_map/ppermute | solution.py:17
  47.1 8.7 %copy.38 = bf16[256,12288]{0,1:T(8,128)(2,1)} copy(bf16[256,12288]{1,0:T(8,128)(2,1)} %param.24) | data formatting | bytes 12582912 | tf_op jit(solution)/shard_map/optimization_barrier | solution.py:65
  78.5 8.2 fusion.3
  86.8 13.5 %collective-permute-done.4 = bf16[256,2048]{1,0:T(8,128)(2,1)} collective-permute-done((bf16[256,2048]{1,0:T(8,128)(2,1)}, bf16[256,2048]{1,0:T(8,128)(2,1)}, u32[]{:S(2)}, u32[]{:S(2)}) %collective-permute-start.4) | collective-permute-done | bytes 1048608 | tf_op jit(solution)/shard_map/ppermute | solution.py:17
  101.5 7.9 all-gather.7.cloned.1.call-done
  124.1 14.5 %recurrence_forward.1 = (f32[4,256,768]{2,1,0:T(8,128)}, f32[4,256,640]{2,1,0:T(8,128)}, f32[4,256,640]{2,1,0:T(8,128)}, f32[4,256,640]{2,1,0:T(8,128)}, f32[4,256,640]{2,1,0:T(8,128)}, /*index=5*/f32[4,256,640]{2,1,0:T(8,128)}) custom-call(s32[1]{0:T(128)} %bitcast.1.odd_ref, f32[4,256,768]{2,1,0:T(8,128)} %bitcast.235, f32[4,8,768]{2,1,0:T(8,128)} %pad.17.rim_ref, ...), custom_call_target="tpu_custom_call" | custom-call | flops 14000000000 | bytes 42000000 | tf_op jit(solution)/shard_map/recurrence_forward/pallas_call | solution.py:614
  139.6 8.5 %collective-permute-start.10 = (f32[2,4,640]{2,0,1:T(2,128)S(1)}, f32[2,4,640]{2,0,1:T(2,128)S(1)}, u32[]{:S(2)}, u32[]{:S(2)}) collective-permute-start(f32[2,4,640]{2,0,1:T(2,128)S(1)} %pad_maximum_fusion.12), channel_id=1, source_target_pairs={{0,4},{1,5},{2,6},{3,7},{8,12},{9,13},{10,14},{11,15},{16,20},{17,... | collective-permute-start | bytes 61448 | tf_op jit(solution)/shard_map/ppermute | solution.py:22
  175.3 12.7 %collective-permute-done.13 = bf16[640,512]{1,0:T(8,128)(2,1)} collective-permute-done((bf16[640,512]{1,0:T(8,128)(2,1)}, bf16[640,512]{1,0:T(8,128)(2,1)}, u32[]{:S(2)}, u32[]{:S(2)}) %collective-permute-start.13) | collective-permute-done | bytes 655392 | tf_op jit(solution)/shard_map/ppermute | solution.py:17
  194.1 7.9 fusion.5
  218.5 11.6 %collective-permute-done.16 = bf16[128,2048]{1,0:T(8,128)(2,1)S(1)} collective-permute-done((bf16[128,2048]{1,0:T(8,128)(2,1)S(1)}, bf16[128,2048]{1,0:T(8,128)(2,1)S(1)}, u32[]{:S(2)}, u32[]{:S(2)}) %collective-permute-start.16) | collective-permute-done | bytes 524320 | tf_op jit(solution)/shard_map/ppermute | solution.py:17
  247.8 8.6 %collective-permute-done.21 = bf16[128,2048]{1,0:T(8,128)(2,1)S(1)} collective-permute-done((bf16[128,2048]{1,0:T(8,128)(2,1)S(1)}, bf16[128,2048]{1,0:T(8,128)(2,1)S(1)}, u32[]{:S(2)}, u32[]{:S(2)}) %collective-permute-start.21) | collective-permute-done | bytes 524320 | tf_op jit(solution)/shard_map/ppermute | solution.py:17
  263.2 8.6 %fusion.56.grad_ref = f32[1024,1536]{1,0:T(8,128)} fusion(bf16[1024,2048]{1,0:T(8,128)(2,1)S(1)} %constant_dynamic-update-slice_fusion.5, bf16[1536,2048]{1,0:T(8,128)(2,1)S(1)} %bitcast.238), kind=kOutput, calls=%fused_computation.266 | convolution fusion | flops 6442450944 | bytes 16777216 | tf_op jit(solution)/shard_map/dot_general | solution.py:663
  275.4 18.0 %collective-permute-done.23 = bf16[256,2048]{1,0:T(8,128)(2,1)S(1)} collective-permute-done((bf16[256,2048]{1,0:T(8,128)(2,1)S(1)}, bf16[256,2048]{1,0:T(8,128)(2,1)S(1)}, u32[]{:S(2)}, u32[]{:S(2)}) %collective-permute-start.23) | collective-permute-done | bytes 1048608 | tf_op jit(solution)/shard_map/ppermute | solution.py:17
  310.5 21.2 %mlp.1 = (bf16[1024,1536]{1,0:T(8,128)(2,1)}, bf16[1024,3072]{1,0:T(8,128)(2,1)}) custom-call(bf16[1024,2048]{1,0:T(8,128)(2,1)} %constant_dynamic-update-slice_fusion.10.normed_ref, bf16[2048,3072]{1,0:T(8,128)(2,1)} %all-gather.11.cloned.1.call-done.weight_ref, f32[1024,1536]{1,0:T(8,128)} %fusion.56.grad_ref), custom_call_target="tpu_custom_call" | custom-call | flops 12884901888 | bytes 32505856 | tf_op jit(solution)/shard_map/mlp/pallas_call | solution.py:670
  331.7 21.1 %convolution_convert_fusion.2 = bf16[1536,2048]{1,0:T(8,128)(2,1)} fusion(bf16[1024,1536]{1,0:T(8,128)(2,1)} %get-tuple-element.80, bf16[1024,2048]{1,0:T(8,128)(2,1)} %copy-done.32), kind=kOutput, calls=%fused_computation.7 | convolution fusion | flops 6445596672 | bytes 13631488 | tf_op jit(solution)/shard_map/dot_general | solution.py:696
  352.8 17.6 %convolution_convert_fusion.3 = bf16[1024,2048]{1,0:T(8,128)(2,1)S(1)} fusion(bf16[1024,3072]{1,0:T(8,128)(2,1)} %get-tuple-element.79, bf16[2048,3072]{1,0:T(8,128)(2,1)} %all-gather.11.cloned.1.call-done.weight_ref), kind=kOutput, calls=%fused_computation.13 | convolution fusion | flops 12886999040 | bytes 23068672 | tf_op jit(solution)/shard_map/dot_general | solution.py:698
  375.2 11.3 %collective-permute-done.28 = bf16[128,2048]{1,0:T(8,128)(2,1)S(1)} collective-permute-done((bf16[128,2048]{1,0:T(8,128)(2,1)S(1)}, bf16[128,2048]{1,0:T(8,128)(2,1)S(1)}, u32[]{:S(2)}, u32[]{:S(2)}) %collective-permute-start.28) | collective-permute-done | bytes 524320 | tf_op jit(solution)/shard_map/ppermute | solution.py:17
  388.1 19.4 %convolution_convert_fusion = bf16[2048,3072]{1,0:T(8,128)(2,1)} fusion(bf16[1024,2048]{1,0:T(8,128)(2,1)} %constant_dynamic-update-slice_fusion.10.normed_ref, bf16[1024,3072]{1,0:T(8,128)(2,1)} %get-tuple-element.79), kind=kOutput, calls=%fused_computation | convolution fusion | flops 12891193344 | bytes 23068672 | tf_op jit(solution)/shard_map/dot_general | solution.py:701
  412.1 11.4 %convolution_convert_fusion.4 = bf16[1024,2048]{1,0:T(8,128)(2,1)} fusion(bf16[1024,1536]{1,0:T(8,128)(2,1)S(1)} %copy-done.60, bf16[1536,2048]{1,0:T(8,128)(2,1)} %all-gather.9.cloned.1.call-done), kind=kOutput, calls=%fused_computation.14 | convolution fusion | flops 6444548096 | bytes 13631488 | tf_op jit(solution)/shard_map/dot_general | solution.py:705
  434.2 19.8 %collective-permute-done.33 = bf16[256,2048]{1,0:T(8,128)(2,1)S(1)} collective-permute-done((bf16[256,2048]{1,0:T(8,128)(2,1)}, bf16[256,2048]{1,0:T(8,128)(2,1)S(1)}, u32[]{:S(2)}, u32[]{:S(2)}) %collective-permute-start.33) | collective-permute-done | bytes 1048608 | tf_op jit(solution)/shard_map/ppermute | solution.py:17
  481.3 10.2 %recurrence_adjoint.1 = (f32[4,256,640]{2,1,0:T(8,128)}, bf16[4,256,640]{2,1,0:T(8,128)(2,1)}, f32[4,256,640]{2,1,0:T(8,128)}, f32[4,256,640]{2,1,0:T(8,128)}) custom-call(f32[4,256,640]{2,1,0:T(8,128)} %bitcast.243, f32[4,256,640]{2,1,0:T(8,128)} %get-tuple-element.84.h_ref, f32[4,256,640]{2,1,0:T(8,128)} %bitcast.242, ...), custom_call_target="tpu_custom_call" | custom-call | flops 10000000000 | bytes 30000000 | tf_op jit(solution)/shard_map/recurrence_adjoint/pallas_call | solution.py:723
  521.7 18.3 %recurrence_backward.1 = (bf16[4,256,1408]{2,1,0:T(8,128)(2,1)}, f32[4,8,768]{2,1,0:T(8,128)}, f32[4,8,768]{2,1,0:T(8,128)}, f32[8,640]{1,0:T(8,128)}, f32[8,768...) custom-call(s32[1]{0:T(128)} %bitcast.1.odd_ref, f32[4,256,640]{2,1,0:T(8,128)} %get-tuple-element.86.back_ref, ...), custom_call_target="tpu_custom_call" | custom-call | flops 19000000512 | bytes 57000000 | tf_op jit(solution)/shard_map/recurrence_backward/pallas_call | solution.py:735
  576.1 10.4 %convolution_convert_fusion.1 = bf16[2048,1408]{1,0:T(8,128)(2,1)} fusion(bf16[1024,2048]{1,0:T(8,128)(2,1)S(1)} %copy-done.15, bf16[1024,1408]{1,0:T(8,128)(2,1)} %bitcast.239), kind=kOutput, calls=%fused_computation.6 | convolution fusion | flops 5908463616 | bytes 12845056 | tf_op jit(solution)/shard_map/dot_general | solution.py:823
  591.9 10.0 %collective-permute-done.52 = bf16[192,2048]{1,0:T(8,128)(2,1)S(1)} collective-permute-done((bf16[192,2048]{1,0:T(8,128)(2,1)}, bf16[192,2048]{1,0:T(8,128)(2,1)S(1)}, u32[]{:S(2)}, u32[]{:S(2)}) %collective-permute-start.52) | collective-permute-done | bytes 786464 | tf_op jit(solution)/shard_map/ppermute | solution.py:17
  606.0 8.8 %convolution_convert_fusion.5 = bf16[1024,2048]{1,0:T(8,128)(2,1)S(1)} fusion(bf16[1024,1408]{1,0:T(8,128)(2,1)S(1)} %bitcast.240, bf16[2048,1408]{1,0:T(8,128)(2,1)} %all-gather.5.cloned.1.call-done), kind=kOutput, calls=%fused_computation.15 | convolution fusion | flops 5907677184 | bytes 12845056 | tf_op jit(solution)/shard_map/dot_general | solution.py:817
  620.6 10.4 %collective-permute-done.61 = bf16[128,2048]{1,0:T(8,128)(2,1)S(1)} collective-permute-done((bf16[128,2048]{1,0:T(8,128)(2,1)S(1)}, bf16[128,2048]{1,0:T(8,128)(2,1)S(1)}, u32[]{:S(2)}, u32[]{:S(2)}) %collective-permute-start.61) | collective-permute-done | bytes 524320 | tf_op jit(solution)/shard_map/ppermute | solution.py:17
  645.3 12.8 %collective-permute-done.79 = bf16[576,640]{1,0:T(8,128)(2,1)S(1)} collective-permute-done((bf16[576,640]{1,0:T(8,128)(2,1)S(1)}, bf16[576,640]{1,0:T(8,128)(2,1)S(1)}, u32[]{:S(2)}, u32[]{:S(2)}) %collective-permute-start.79) | collective-permute-done | bytes 737312 | tf_op jit(solution)/shard_map/ppermute | solution.py:17
  688.7 33.3 %collective-permute-done.75 = bf16[320,512]{1,0:T(8,128)(2,1)S(1)} collective-permute-done((bf16[320,512]{1,0:T(8,128)(2,1)}, bf16[320,512]{1,0:T(8,128)(2,1)S(1)}, u32[]{:S(2)}, u32[]{:S(2)}) %collective-permute-start.75) | collective-permute-done | bytes 327712 | tf_op jit(solution)/shard_map/ppermute | solution.py:17
  726.7 21.0 %collective-permute-done.76 = bf16[320,512]{1,0:T(8,128)(2,1)S(1)} collective-permute-done((bf16[320,512]{1,0:T(8,128)(2,1)}, bf16[320,512]{1,0:T(8,128)(2,1)S(1)}, u32[]{:S(2)}, u32[]{:S(2)}) %collective-permute-start.76) | collective-permute-done | bytes 327712 | tf_op jit(solution)/shard_map/ppermute | solution.py:17
  753.7 8.4 collective-permute-done.78
  766.7 7.6 collective-permute-done.68
  790.5 9.9 %spread_mlp.1 = f32[256,12288]{1,0:T(8,128)} custom-call(s32[1]{0:T(128)} %bitcast.36.mine_ref, bf16[256,3072]{1,0:T(8,128)(2,1)} %reduce-scatter.7.cloned.1.call-done.a_ref, bf16[256,3072]{1,0:T(8,128)(2,1)} %copy-done.27, bf16[256,3072]{1,0:T(8,128)(2,1)} %copy-done.28, bf16[256,3072]{1,0:T(8,128)(2,1)} %copy-done.29), custom_call_target="tpu_custom_call" | custom-call | flops 8000000000 | bytes 24000000 | tf_op jit(solution)/shard_map/spread_mlp/pallas_call | solution.py:473
  (566 shorter events, 398.0 us)
Async XLA Ops:
  7.2 67.3 %all-gather.5.cloned.1.call-start = ((), (), s32[]{:S(2)}) async-start(), calls=%async_computation.4 | async-start | bytes 6488064 | tf_op jit(solution)/shard_map/all_gather | solution.py:57
  11.2 98.1 %all-gather.7.cloned.1.call-start = ((), (), s32[]{:S(2)}) async-start(), calls=%async_computation.5 | async-start | bytes 2949120 | tf_op jit(solution)/shard_map/all_gather | solution.py:57
  11.3 26.5 %collective-permute-start = (bf16[256,2048]{1,0:T(8,128)(2,1)}, bf16[256,2048]{1,0:T(8,128)(2,1)}, u32[]{:S(2)}, u32[]{:S(2)}) collective-permute-start(bf16[256,2048]{1,0:T(8,128)(2,1)} %bitcast.196), channel_id=1, source_target_pairs={{0,8},{8,0},{16,24},{24,16},{1,9},{9,1},{17,25},{25,17},{2,10},{10... | collective-permute-start | bytes 3145736 | tf_op jit(solution)/shard_map/ppermute | solution.py:17
  14.3 27.1 %collective-permute-start.1 = (bf16[256,2048]{1,0:T(8,128)(2,1)}, bf16[256,2048]{1,0:T(8,128)(2,1)}, u32[]{:S(2)}, u32[]{:S(2)}) collective-permute-start(bf16[256,2048]{1,0:T(8,128)(2,1)} %bitcast.197), channel_id=1, source_target_pairs={{0,16},{8,24},{16,0},{24,8},{1,17},{9,25},{17,1},{25,9},{2,18},{10... | collective-permute-start | bytes 3145736 | tf_op jit(solution)/shard_map/ppermute | solution.py:17
  74.5 117.5 %all-gather.9.cloned.1.call-start = ((), (), s32[]{:S(2)}) async-start(), calls=%async_computation.6 | async-start | bytes 7077888 | tf_op jit(solution)/shard_map/all_gather | solution.py:57
  74.6 25.7 %collective-permute-start.4 = (bf16[256,2048]{1,0:T(8,128)(2,1)}, bf16[256,2048]{1,0:T(8,128)(2,1)}, u32[]{:S(2)}, u32[]{:S(2)}) collective-permute-start(bf16[256,2048]{1,0:T(8,128)(2,1)} %bitcast.199), channel_id=1, source_target_pairs={{0,8},{8,0},{16,24},{24,16},{1,9},{9,1},{17,25},{25,17},{2,10},{10... | collective-permute-start | bytes 3145736 | tf_op jit(solution)/shard_map/ppermute | solution.py:17
  76.1 25.3 %collective-permute-start.5 = (bf16[256,2048]{1,0:T(8,128)(2,1)}, bf16[256,2048]{1,0:T(8,128)(2,1)}, u32[]{:S(2)}, u32[]{:S(2)}) collective-permute-start(bf16[256,2048]{1,0:T(8,128)(2,1)} %bitcast.200), channel_id=1, source_target_pairs={{0,16},{8,24},{16,0},{24,8},{1,17},{9,25},{17,1},{25,9},{2,18},{10... | collective-permute-start | bytes 3145736 | tf_op jit(solution)/shard_map/ppermute | solution.py:17
  109.3 201.1 %all-gather.11.cloned.1.call-start = ((), (), s32[]{:S(2)}) async-start(), calls=%async_computation.7 | async-start | bytes 14155776 | tf_op jit(solution)/shard_map/all_gather | solution.py:57
  157.9 30.1 %collective-permute-start.13 = (bf16[640,512]{1,0:T(8,128)(2,1)}, bf16[640,512]{1,0:T(8,128)(2,1)}, u32[]{:S(2)}, u32[]{:S(2)}) collective-permute-start(bf16[640,512]{1,0:T(8,128)(2,1)} %pad_maximum_fusion.9), channel_id=1, source_target_pairs={{0,16},{8,24},{16,0},{24,8},{1,17},{9,25},{17,1},{25,9},{2,18},{10... | collective-permute-start | bytes 1966088 | tf_op jit(solution)/shard_map/ppermute | solution.py:17
  160.3 29.7 %collective-permute-start.14 = (bf16[640,512]{1,0:T(8,128)(2,1)}, bf16[640,512]{1,0:T(8,128)(2,1)}, u32[]{:S(2)}, u32[]{:S(2)}) collective-permute-start(bf16[640,512]{1,0:T(8,128)(2,1)} %pad_maximum_fusion.10), channel_id=1, source_target_pairs={{0,24},{8,16},{16,8},{24,0},{1,25},{9,17},{17,9},{25,1},{2,26},{10... | collective-permute-start | bytes 1966088 | tf_op jit(solution)/shard_map/ppermute | solution.py:17
  193.8 232.6 %reduce-scatter.5.cloned.1.call-start = ((), (), s32[]{:S(2)}) async-start(), calls=%async_computation.8 | async-start | bytes 7077888 | tf_op jit(solution)/shard_map/reduce_scatter | solution.py:61
  215.8 25.6 %collective-permute-start.15 = (bf16[128,2048]{1,0:T(8,128)(2,1)S(1)}, bf16[128,2048]{1,0:T(8,128)(2,1)S(1)}, u32[]{:S(2)}, u32[]{:S(2)}) collective-permute-start(bf16[128,2048]{1,0:T(8,128)(2,1)S(1)} %get-tuple-element.151), channel_id=1, source_target_pairs={{0,8},{8,0},{16,24},{24,16},{1,9},{9,1},{17,25},{25,17},{2,10},{10... | collective-permute-start | bytes 1572872 | tf_op jit(solution)/shard_map/ppermute | solution.py:17
  352.8 234.9 %reduce-scatter.7.cloned.1.call-start = ((), (), s32[]{:S(2)}) async-start(), calls=%async_computation.9 | async-start | bytes 14155776 | tf_op jit(solution)/shard_map/reduce_scatter | solution.py:61
  373.1 35.0 %collective-permute-start.27 = (bf16[128,2048]{1,0:T(8,128)(2,1)}, bf16[128,2048]{1,0:T(8,128)(2,1)}, u32[]{:S(2)}, u32[]{:S(2)}) collective-permute-start(bf16[128,2048]{1,0:T(8,128)(2,1)} %get-tuple-element.145), channel_id=1, source_target_pairs={{0,8},{8,0},{16,24},{24,16},{1,9},{9,1},{17,25},{25,17},{2,10},{10... | collective-permute-start | bytes 1572872 | tf_op jit(solution)/shard_map/ppermute | solution.py:17
  373.7 34.4 %collective-permute-start.30 = (bf16[128,2048]{1,0:T(8,128)(2,1)}, bf16[128,2048]{1,0:T(8,128)(2,1)}, u32[]{:S(2)}, u32[]{:S(2)}) collective-permute-start(bf16[128,2048]{1,0:T(8,128)(2,1)} %get-tuple-element.147), channel_id=1, source_target_pairs={{0,16},{8,24},{16,0},{24,8},{1,17},{9,25},{17,1},{25,9},{2,18},{10... | collective-permute-start | bytes 1572872 | tf_op jit(solution)/shard_map/ppermute | solution.py:17
  426.4 236.3 %reduce-scatter.9.cloned.1.call-start = ((), (), s32[]{:S(2)}) async-start(), calls=%async_computation.10 | async-start | bytes 2949120 | tf_op jit(solution)/shard_map/reduce_scatter | solution.py:61
  500.1 44.8 %collective-permute-start.49 = (bf16[640,512]{1,0:T(8,128)(2,1)}, bf16[640,512]{1,0:T(8,128)(2,1)}, u32[]{:S(2)}, u32[]{:S(2)}) collective-permute-start(bf16[640,512]{1,0:T(8,128)(2,1)} %get-tuple-element.162), channel_id=1, source_target_pairs={{0,8},{8,0},{16,24},{24,16},{1,9},{9,1},{17,25},{25,17},{2,10},{10... | collective-permute-start | bytes 1966088 | tf_op jit(solution)/shard_map/ppermute | solution.py:17
  501.2 44.5 %collective-permute-start.50 = (bf16[640,512]{1,0:T(8,128)(2,1)}, bf16[640,512]{1,0:T(8,128)(2,1)}, u32[]{:S(2)}, u32[]{:S(2)}) collective-permute-start(bf16[640,512]{1,0:T(8,128)(2,1)} %get-tuple-element.161), channel_id=1, source_target_pairs={{0,16},{8,24},{16,0},{24,8},{1,17},{9,25},{17,1},{25,9},{2,18},{10... | collective-permute-start | bytes 1966088 | tf_op jit(solution)/shard_map/ppermute | solution.py:17
  507.3 40.1 %collective-permute-start.51 = (bf16[640,512]{1,0:T(8,128)(2,1)}, bf16[640,512]{1,0:T(8,128)(2,1)}, u32[]{:S(2)}, u32[]{:S(2)}) collective-permute-start(bf16[640,512]{1,0:T(8,128)(2,1)} %get-tuple-element.160), channel_id=1, source_target_pairs={{0,24},{8,16},{16,8},{24,0},{1,25},{9,17},{17,9},{25,1},{2,26},{10... | collective-permute-start | bytes 1966088 | tf_op jit(solution)/shard_map/ppermute | solution.py:17
  509.3 59.4 %collective-permute-start.37 = (bf16[128,2048]{1,0:T(8,128)(2,1)}, bf16[128,2048]{1,0:T(8,128)(2,1)}, u32[]{:S(2)}, u32[]{:S(2)}) collective-permute-start(bf16[128,2048]{1,0:T(8,128)(2,1)} %get-tuple-element.139), channel_id=1, source_target_pairs={{0,8},{8,0},{16,24},{24,16},{1,9},{9,1},{17,25},{25,17},{2,10},{10... | collective-permute-start | bytes 1572872 | tf_op jit(solution)/shard_map/ppermute | solution.py:17
  519.8 68.0 %collective-permute-start.42 = (bf16[128,2048]{1,0:T(8,128)(2,1)}, bf16[128,2048]{1,0:T(8,128)(2,1)}, u32[]{:S(2)}, u32[]{:S(2)}) collective-permute-start(bf16[128,2048]{1,0:T(8,128)(2,1)} %get-tuple-element.140), channel_id=1, source_target_pairs={{0,16},{8,24},{16,0},{24,8},{1,17},{9,25},{17,1},{25,9},{2,18},{10... | collective-permute-start | bytes 1572872 | tf_op jit(solution)/shard_map/ppermute | solution.py:17
  573.8 28.1 %collective-permute-start.52 = (bf16[192,2048]{1,0:T(8,128)(2,1)}, bf16[192,2048]{1,0:T(8,128)(2,1)S(1)}, u32[]{:S(2)}, u32[]{:S(2)}) collective-permute-start(bf16[192,2048]{1,0:T(8,128)(2,1)} %reduce-scatter.5.cloned.1.call-done), channel_id=1, source_target_pairs={{0,8},{8,0},{16,24},{24,16},{1,9},{9,1},{17,25},{25,17},{2,10},{10... | collective-permute-start | bytes 2359304 | tf_op jit(solution)/shard_map/ppermute | solution.py:17
  574.9 28.5 %collective-permute-start.53 = (bf16[192,2048]{1,0:T(8,128)(2,1)}, bf16[192,2048]{1,0:T(8,128)(2,1)}, u32[]{:S(2)}, u32[]{:S(2)}) collective-permute-start(bf16[192,2048]{1,0:T(8,128)(2,1)} %reduce-scatter.5.cloned.1.call-done), channel_id=1, source_target_pairs={{0,16},{8,24},{16,0},{24,8},{1,17},{9,25},{17,1},{25,9},{2,18},{10... | collective-permute-start | bytes 2359304 | tf_op jit(solution)/shard_map/ppermute | solution.py:17
  587.8 213.3 %reduce-scatter.11.cloned.1.call-start = ((), (), s32[]{:S(2)}) async-start(), calls=%async_computation.11 | async-start | bytes 6488064 | tf_op jit(solution)/shard_map/reduce_scatter | solution.py:61
  617.3 105.3 %collective-permute-start.60 = (bf16[128,2048]{1,0:T(8,128)(2,1)}, bf16[128,2048]{1,0:T(8,128)(2,1)}, u32[]{:S(2)}, u32[]{:S(2)}) collective-permute-start(bf16[128,2048]{1,0:T(8,128)(2,1)} %get-tuple-element.133), channel_id=1, source_target_pairs={{0,8},{8,0},{16,24},{24,16},{1,9},{9,1},{17,25},{25,17},{2,10},{10... | collective-permute-start | bytes 1572872 | tf_op jit(solution)/shard_map/ppermute | solution.py:17
  632.1 26.0 %collective-permute-start.79 = (bf16[576,640]{1,0:T(8,128)(2,1)S(1)}, bf16[576,640]{1,0:T(8,128)(2,1)S(1)}, u32[]{:S(2)}, u32[]{:S(2)}) collective-permute-start(bf16[576,640]{1,0:T(8,128)(2,1)S(1)} %maximum_select_fusion), channel_id=1, source_target_pairs={{0,8},{8,0},{16,24},{24,16},{1,9},{9,1},{17,25},{25,17},{2,10},{10... | collective-permute-start | bytes 2211848 | tf_op jit(solution)/shard_map/ppermute | solution.py:17
  681.6 80.5 %collective-permute-start.66 = (bf16[256,3072]{1,0:T(8,128)(2,1)}, bf16[256,3072]{1,0:T(8,128)(2,1)S(1)}, u32[]{:S(2)}, u32[]{:S(2)}) collective-permute-start(bf16[256,3072]{1,0:T(8,128)(2,1)} %reduce-scatter.7.cloned.1.call-done.a_ref), channel_id=1, source_target_pairs={{0,8},{8,0},{16,24},{24,16},{1,9},{9,1},{17,25},{25,17},{2,10},{10... | collective-permute-start | bytes 4718600 | tf_op jit(solution)/shard_map/ppermute | solution.py:17
  683.6 40.4 %collective-permute-start.62 = (bf16[128,2048]{1,0:T(8,128)(2,1)S(1)}, bf16[128,2048]{1,0:T(8,128)(2,1)S(1)}, u32[]{:S(2)}, u32[]{:S(2)}) collective-permute-start(bf16[128,2048]{1,0:T(8,128)(2,1)S(1)} %add_convert_fusion.1), channel_id=1, source_target_pairs={{0,16},{8,24},{16,0},{24,8},{1,17},{9,25},{17,1},{25,9},{2,18},{10... | collective-permute-start | bytes 1572872 | tf_op jit(solution)/shard_map/ppermute | solution.py:17
  684.3 78.3 %collective-permute-start.67 = (bf16[256,3072]{1,0:T(8,128)(2,1)S(1)}, bf16[256,3072]{1,0:T(8,128)(2,1)S(1)}, u32[]{:S(2)}, u32[]{:S(2)}) collective-permute-start(bf16[256,3072]{1,0:T(8,128)(2,1)S(1)} %copy-done.57), channel_id=1, source_target_pairs={{0,16},{8,24},{16,0},{24,8},{1,17},{9,25},{17,1},{25,9},{2,18},{10... | collective-permute-start | bytes 4718600 | tf_op jit(solution)/shard_map/ppermute | solution.py:17
  685.9 36.1 %collective-permute-start.75 = (bf16[320,512]{1,0:T(8,128)(2,1)}, bf16[320,512]{1,0:T(8,128)(2,1)S(1)}, u32[]{:S(2)}, u32[]{:S(2)}) collective-permute-start(bf16[320,512]{1,0:T(8,128)(2,1)} %reduce-scatter.9.cloned.1.call-done), channel_id=1, source_target_pairs={{0,8},{8,0},{16,24},{24,16},{1,9},{9,1},{17,25},{25,17},{2,10},{10... | collective-permute-start | bytes 983048 | tf_op jit(solution)/shard_map/ppermute | solution.py:17
  722.0 42.8 %collective-permute-start.65 = (bf16[128,2048]{1,0:T(8,128)(2,1)}, bf16[128,2048]{1,0:T(8,128)(2,1)S(1)}, u32[]{:S(2)}, u32[]{:S(2)}) collective-permute-start(bf16[128,2048]{1,0:T(8,128)(2,1)} %get-tuple-element.134), channel_id=1, source_target_pairs={{0,16},{8,24},{16,0},{24,8},{1,17},{9,25},{17,1},{25,9},{2,18},{10... | collective-permute-start | bytes 1572872 | tf_op jit(solution)/shard_map/ppermute | solution.py:17
  724.1 25.7 %collective-permute-start.77 = (bf16[160,512]{1,0:T(8,128)(2,1)S(1)}, bf16[160,512]{1,0:T(8,128)(2,1)S(1)}, u32[]{:S(2)}, u32[]{:S(2)}) collective-permute-start(bf16[160,512]{1,0:T(8,128)(2,1)S(1)} %slice.648), channel_id=1, source_target_pairs={{0,16},{8,24},{16,0},{24,8},{1,17},{9,25},{17,1},{25,9},{2,18},{10... | collective-permute-start | bytes 491528 | tf_op jit(solution)/shard_map/ppermute | solution.py:17
  (128 other events, 1798.0 us)
Sparse Core Ops, SparseCore 0:
  11.3 63.1 all-gather.4
  76.7 32.5 all-gather.6
  111.5 63.7 all-gather.8
  193.9 116.5 all-gather.10
  352.9 71.5 reduce-scatter.4
  427.3 133.9 reduce-scatter.6
  587.9 37.0 reduce-scatter.8
  662.9 62.6 reduce-scatter.10
